TPU v7x, 512 devices: a whole 4x8x8 slice. The times are simulated.
512 devices in a mesh: ctx: 128 (over z, x, y_lo), head: 4 (over y_hi, core).
Axes of the slice: x: 4, y: 8 (y_hi: 2, y_lo: 4; y = y_hi * 4 + y_lo), z: 8, core: 2. Of those that a mesh axis runs over, the one named last changes fastest.
Arguments:
- q_nope: bfloat16 [32768, 8192], P('ctx', 'head'), may hold values from -6 to 6
- q_rope: bfloat16 [32768, 4096], P('ctx', 'head'), may hold values from -200 to 200
- latent: bfloat16 [32768, 512], P(('ctx', 'head')), may hold values from -6 to 6
- k_rope: bfloat16 [32768, 64], P(('ctx', 'head')), may hold values from -4 to 4
- blocks: int32 [128, 2], replicated, may hold values from 0 to 255, as said below
- w_uk: bfloat16 [512, 8192], P('ctx', 'head'), may hold values from -0.25 to 0.25
- w_uv: bfloat16 [512, 8192], P('ctx', 'head'), may hold values from -0.25 to 0.25
Outputs:
- attended: bfloat16 [32768, 8192], P('ctx', 'head')
Inputs may be any that keep to these rules, and one draw needn't show every extreme that they name: `blocks`: row c holds two block numbers b and 255 - b; the first column is a permutation of 0 to 127.
All inputs are finite; a program needn't handle non-finite values.
Results may differ from a plain program's by a relative error of at most 0.017.
Values may be sent and summed in bfloat16 or wider, within the bound.
No kernel may reach another device: no remote copies, remote signals or barrier semaphores. Data moves between devices by JAX's collectives and lax.ppermute only.
A program may use at most 64 MiB of HBM per device.

v0:
```python
import jax
import jax.numpy as jnp
from jax import lax
from jax.sharding import PartitionSpec as P

ROPE = 64
NOPE = 128
VDIM = 128
STEPS = 3


def for_sending(x):

    def short(part):
        return part.astype(jnp.bfloat16) if part.dtype == jnp.float32 else part

    return jax.tree.map(short, x)


def passed_along(value, axis, steps):
    count = lax.axis_size(axis)
    pairs = [(source, (source + steps) % count) for source in range(count)]
    return lax.ppermute(value, axis, pairs)


def angles_of(pos, width):
    half = width // 2
    freq = 10000.0 ** (-(2.0 * jnp.arange(half, dtype=jnp.float32)) / width)
    return pos.astype(jnp.float32)[..., None] * freq


def rotate(values, angles):
    half = values.shape[-1] // 2
    first = values[..., :half]
    second = values[..., half:]
    cosine = jnp.cos(angles)
    sine = jnp.sin(angles)
    return jnp.concatenate(
        [first * cosine - second * sine, first * sine + second * cosine], axis=-1
    )


def shard_positions(blocks, shard, start, count, tok_len):
    rows = start + jnp.arange(count, dtype=jnp.int32)
    half = tok_len // 2
    pair = blocks[shard]
    block_id = jnp.where(rows < half, pair[0], pair[1])
    return block_id * half + rows % half


def local(q_nope, q_rope, latent, k_rope, blocks, w_uk, w_uv):
    tok_len = q_nope.shape[0]
    heads = q_nope.shape[1] // NOPE
    quarter = latent.shape[0]
    n_ctx = lax.axis_size("ctx")
    ctx_index = lax.axis_index("ctx")
    head_index = lax.axis_index("head")
    scale = 1.0 / (NOPE + ROPE) ** 0.5
    up_keys, up_values = (
        lax.all_gather(w_uk, "ctx", axis=0, tiled=True),
        lax.all_gather(w_uv, "ctx", axis=0, tiled=True),
    )
    own_pos = shard_positions(blocks, ctx_index, head_index * quarter, quarter, tok_len)
    own_rot = rotate(k_rope.astype(jnp.float32), angles_of(own_pos, ROPE)).astype(jnp.bfloat16)
    mine = (latent, own_rot)
    mine = (
        lax.all_gather(mine[0], "head", axis=0, tiled=True),
        lax.all_gather(mine[1], "head", axis=0, tiled=True),
    )
    visited = [mine]
    for step in range(1, STEPS):
        arrived = passed_along(for_sending(visited[-1]), "ctx", 1)
        visited.append(arrived)
    lat_all = jnp.concatenate([piece[0] for piece in visited], 0)
    rot_all = jnp.concatenate([piece[1] for piece in visited], 0)
    key_pos = jnp.concatenate(
        [
            shard_positions(blocks, (ctx_index - step) % n_ctx, 0, tok_len, tok_len)
            for step in range(STEPS)
        ],
        0,
    )
    count = lat_all.shape[0]
    latent_dim = lat_all.shape[1]
    query_pos = shard_positions(blocks, ctx_index, 0, tok_len, tok_len)
    query_r = q_rope.reshape(tok_len, heads, ROPE).astype(jnp.float32)
    query_rot = rotate(query_r, angles_of(query_pos, ROPE)[:, None, :])
    allowed = (key_pos[None, :] <= query_pos[:, None])[None, :, :]
    width = 4
    groups = heads // width
    grouped_n = q_nope.reshape(tok_len, groups, width, NOPE).transpose(1, 0, 2, 3)
    grouped_r = query_rot.reshape(tok_len, groups, width, ROPE).transpose(1, 0, 2, 3)
    grouped_uk = up_keys.reshape(latent_dim, groups, width * NOPE).transpose(1, 0, 2)
    grouped_uv = up_values.reshape(latent_dim, groups, width * VDIM).transpose(1, 0, 2)

    def one_group(pieces):
        query_n, rot_q, keys_up, values_up = pieces
        key_n = jnp.dot(lat_all, keys_up, preferred_element_type=jnp.float32).reshape(
            count, width, NOPE
        )
        score_n = jnp.einsum("thn,khn->htk", query_n, key_n, preferred_element_type=jnp.float32)
        score_r = jnp.einsum("thr,kr->htk", rot_q, rot_all, preferred_element_type=jnp.float32)
        scores = (score_n + score_r) * scale
        masked = jnp.where(allowed, scores, -jnp.inf)
        peak = jnp.max(masked, axis=-1, keepdims=True)
        probs = jnp.exp(masked - peak)
        total = jnp.sum(probs, axis=-1)
        weights = probs.astype(jnp.bfloat16)
        key_v = jnp.dot(lat_all, values_up, preferred_element_type=jnp.float32).reshape(
            count, width, VDIM
        )
        summed = jnp.einsum("htk,khv->thv", weights, key_v, preferred_element_type=jnp.float32)
        return summed / jnp.transpose(total)[:, :, None]

    results = lax.map(one_group, (grouped_n, grouped_r, grouped_uk, grouped_uv))
    return results.transpose(1, 0, 2, 3).reshape(tok_len, heads * VDIM).astype(jnp.bfloat16)


def solution(mesh):
    in_specs = (
        P("ctx", "head"),
        P("ctx", "head"),
        P(("ctx", "head"), None),
        P(("ctx", "head"), None),
        P(),
        P("ctx", "head"),
        P("ctx", "head"),
    )
    out_specs = P("ctx", "head")
    return jax.shard_map(local, mesh=mesh, in_specs=in_specs, out_specs=out_specs, check_vma=False)
```

profile of v0, /device:TPU:6, one launch (start us, length us, event | category | flops | bytes accessed | tf_op | source)
XLA Modules:
  0.0 1417.3 jit_solution(15719257634131533875)
XLA Ops:
  6.5 0.7 all-gather.5.cloned.1.call-update
  7.3 0.7 all-gather.7.cloned.1.call-update
  8.1 0.8 copy.32
  8.9 0.9 constant_dynamic-slice_fusion.3
  9.8 0.6 fusion.51
  10.4 1.3 fusion.48
  11.9 9.2 all_gather.15
  21.1 3.5 collective-permute-start.2
  24.6 10.0 all_gather.13
  34.6 5.6 collective-permute-start
  40.2 1.2 copy.31
  41.6 1.3 fusion.49
  42.9 0.6 fusion.52
  43.4 0.6 fusion.53
  44.0 0.2 multiply_cosine_fusion
  44.4 1.3 multiply_add_fusion.4
  45.7 2.6 multiply_add_fusion.2
  48.3 0.9 pad_maximum_fusion
  49.2 2.5 collective-permute-start.1
  51.8 4.4 collective-permute-start.3
  56.3 1.3 multiply_add_fusion.1
  57.5 0.5 copy.30
  58.1 6.2 collective-permute-done.3
  64.5 0.9 pad_maximum_fusion.1
  65.4 615.8 %all-gather.5.cloned.1.call-done = bf16[128,4,2048]{2,1,0:T(4,128)(2,1)} async-done(((bf16[1,4,2048]{2,1,0:T(4,128)(2,1)}), bf16[128,4,2048]{2,1,0:T(4,128)(2,1)}) %all-gather.5.cloned.1.call-update) | async-done | bytes 2097168 | tf_op jit(solution)/shard_map/all_gather | solution.py:61
  681.2 3.1 reshape.178
  684.4 1.7 copy.34
  686.1 680.0 %all-gather.7.cloned.1.call-done = bf16[128,4,2048]{2,1,0:T(4,128)(2,1)} async-done(((bf16[1,4,2048]{2,1,0:T(4,128)(2,1)}), bf16[128,4,2048]{2,1,0:T(4,128)(2,1)}) %all-gather.7.cloned.1.call-update) | async-done | bytes 2097168 | tf_op jit(solution)/shard_map/all_gather | solution.py:60
  1366.1 3.1 reshape.180
  1369.3 1.7 copy.36
  1371.0 37.1 %while.11 = (s32[]{:T(128)}, bf16[4,256,4,128]{1,3,2,0:T(8,128)(2,1)}, bf16[4,512,512]{2,1,0:T(8,128)(2,1)}, bf16[768,512]{1,0:T(8,128)(2,1)}, bf16[4,256,4,128]...) while((s32[]{:T(128)}, ...), condition=%wide.region_3.4_spmd.clone, body=%wide.region_0.3_spmd.clone.sunk | while | flops 1315239936 | bytes 34465480 | solution.py:115
  1371.0 1.9 fusion.82
  1372.9 0.6 fusion.83
  1373.6 0.2 compare_bitcast_fusion.2
  1373.7 1.8 fusion.84
  1375.6 1.0 fusion.85
  1376.7 1.7 fusion.81
  1378.4 0.9 fusion.86
  1379.3 1.0 copy-done.2
  1380.3 1.9 fusion.82
  1382.2 0.6 fusion.83
  1382.8 0.2 compare_bitcast_fusion.2
  1383.0 1.8 fusion.84
  1384.9 1.0 fusion.85
  1386.0 1.7 fusion.81
  1387.7 0.9 fusion.86
  1388.6 1.0 copy-done.2
  1389.6 1.9 fusion.82
  1391.5 0.6 fusion.83
  1392.1 0.2 compare_bitcast_fusion.2
  1392.3 1.8 fusion.84
  1394.2 1.0 fusion.85
  1395.3 1.7 fusion.81
  1397.0 0.9 fusion.86
  1397.9 1.0 copy-done.2
  1398.9 1.9 fusion.82
  1400.8 0.6 fusion.83
  1401.4 0.2 compare_bitcast_fusion.2
  1401.6 1.8 fusion.84
  1403.5 1.0 fusion.85
  1404.6 1.7 fusion.81
  1406.3 0.9 fusion.86
  1407.2 1.0 copy-done.2
  1408.2 2.3 copy.40
  (38 shorter events, 1.3 us)
Async XLA Ops:
  6.5 51.0 %copy-start = (bf16[256,2048]{1,0:T(8,128)(2,1)S(1)}, bf16[256,2048]{1,0:T(8,128)(2,1)}, u32[]{:S(2)}) copy-start(bf16[256,2048]{1,0:T(8,128)(2,1)} %param.9) | copy-start | bytes 3145732
  6.5 674.7 %all-gather.5.cloned.1.call-start = ((), (), s32[]{:S(2)}) async-start(), calls=%async_computation | async-start | bytes 2113536 | tf_op jit(solution)/shard_map/all_gather | solution.py:61
  7.3 1358.9 %all-gather.7.cloned.1.call-start = ((), (), s32[]{:S(2)}) async-start(), calls=%async_computation.1 | async-start | bytes 2113536 | tf_op jit(solution)/shard_map/all_gather | solution.py:60
  21.1 30.7 %collective-permute-start.2 = (bf16[256,64]{1,0:T(8,128)(2,1)S(1)}, bf16[256,64]{1,0:T(8,128)(2,1)S(1)}, u32[]{:S(2)}, u32[]{:S(2)}) collective-permute-start(bf16[256,64]{1,0:T(8,128)(2,1)S(1)} %all_gather.15), channel_id=1, source_target_pairs={{0,4},{4,8},{8,12},{12,16},{16,20},{20,24},{24,28},{28,32},{32,36}... | collective-permute-start | bytes 98312 | tf_op jit(solution)/shard_map/ppermute | solution.py:23
  34.6 14.7 %collective-permute-start = (bf16[256,512]{1,0:T(8,128)(2,1)S(1)}, bf16[256,512]{1,0:T(8,128)(2,1)S(1)}, u32[]{:S(2)}, u32[]{:S(2)}) collective-permute-start(bf16[256,512]{1,0:T(8,128)(2,1)S(1)} %all_gather.13), channel_id=1, source_target_pairs={{0,4},{4,8},{8,12},{12,16},{16,20},{20,24},{24,28},{28,32},{32,36}... | collective-permute-start | bytes 786440 | tf_op jit(solution)/shard_map/ppermute | solution.py:23
  49.2 15.2 %collective-permute-start.1 = (bf16[256,512]{1,0:T(8,128)(2,1)S(1)}, bf16[256,512]{1,0:T(8,128)(2,1)S(1)}, u32[]{:S(2)}, u32[]{:S(2)}) collective-permute-start(bf16[256,512]{1,0:T(8,128)(2,1)S(1)} %collective-permute-done), channel_id=1, source_target_pairs={{0,4},{4,8},{8,12},{12,16},{16,20},{20,24},{24,28},{28,32},{32,36}... | collective-permute-start | bytes 786440 | tf_op jit(solution)/shard_map/ppermute | solution.py:23
  51.8 12.5 collective-permute-start.3
  1375.6 1.1 copy-start.3
  1375.6 2.8 copy-start.1
  1379.3 1.0 copy-start.2
  1384.9 1.1 copy-start.3
  1384.9 2.8 copy-start.1
  1388.6 1.0 copy-start.2
  1394.2 1.1 copy-start.3
  1394.2 2.8 copy-start.1
  1397.9 1.0 copy-start.2
  1403.4 1.1 copy-start.3
  1403.5 2.8 copy-start.1
  1407.2 1.0 copy-start.2
Sparse Core Ops, SparseCore 0:
  9.4 671.7 all-gather.4
  683.3 682.8 all-gather.6
where the time goes:
time: 1440 us; the launch traced here: 1420 us
  waiting for transfers between devices  1300 us (90%)
  matrix products  27.8 us (2%)
  local copies, waits for them, and re-layouts  21.8 us (2%)
  blocking collectives  19.2 us (1%)
  starting transfers between devices  16.1 us (1%)
  other arithmetic  14.9 us (1%)
    all_gather x1, waiting for transfers between devices, local(): lax.all_gather(w_uk, 'ctx', axis=0, tiled=True)  680 us
    all_gather x1, waiting for transfers between devices, local(): lax.all_gather(w_uv, 'ctx', axis=0, tiled=True)  616 us
  transfers between devices with their start and end apart: 6, of which 4 were waited for; matrix products, arithmetic and copies ran while one was open for 1% of the time, Pallas kernels for 0%

commit v1 on v0

v1 whole, which is shorter than its diff:
```python
import functools

import jax
import jax.numpy as jnp
from jax import lax
from jax.experimental import pallas as pl
from jax.experimental.pallas import tpu as pltpu
from jax.sharding import PartitionSpec as P

ROPE = 64
NOPE = 128
VDIM = 128
STEPS = 3
NZ, NX, NY = 8, 4, 4
HALF = 128
LOG2E = 1.4426950408889634
NEG = -1e30


def place(z, x, y):
    return ((z % NZ) * NX + x % NX) * NY + y


def shifted(value, dz, dx):
    pairs = [
        (place(z, x, y), place(z + dz, x + dx, y))
        for z in range(NZ)
        for x in range(NX)
        for y in range(NY)
    ]
    return lax.ppermute(value, "ctx", pairs)


def members(plan, colour):
    if plan == 0:
        return [(z, (colour - 2 * z) % NX) for z in range(NZ)]
    return [((colour - 2 * x) % 4 + 4 * far, x) for x in range(NX) for far in range(2)]


def colour_groups(plan):
    return [[place(z, x, y) for z, x in members(plan, c) for y in range(NY)] for c in range(4)]


def colour_of(plan, z, x):
    return (x + 2 * z) % 4 if plan == 0 else (z + 2 * x) % 4


def gather_pieces(plan, shard):
    groups = colour_groups(plan)
    size = len(groups[0])
    own = lax.all_to_all(
        jnp.broadcast_to(shard[None], (size,) + shard.shape), "ctx", 0, 0, axis_index_groups=groups
    ).reshape(size * shard.shape[0], shard.shape[1])
    mid = own.shape[0] // 2
    if plan == 0:
        up, down = (0, -1), (0, 1)
        side, other = (-1, 0), (1, 0)
    else:
        up, down = (-1, 0), (1, 0)
        side, other = (0, -1), (0, 1)
    return (
        own,
        shifted(own, *up),
        shifted(own, *down),
        shifted(own[:mid], *side),
        shifted(own[mid:], *other),
    )


def row_order(plan, z, x, rows):
    at = jnp.arange(NZ * NX * NY * rows, dtype=jnp.int32)
    quarter = at.shape[0] // 4
    piece, rest = at // quarter, at % quarter
    step = jnp.where(piece < 2, piece, 5 - piece)
    colour = (colour_of(plan, z, x) + step) % 4
    member, inner = rest // (NY * rows), rest % (NY * rows)
    if plan == 0:
        mz = member
        mx = (colour - 2 * mz) % 4
    else:
        mx = member // 2
        mz = (colour - 2 * mx) % 4 + 4 * (member % 2)
    return (mz * NX + mx) * (NY * rows) + inner


def angles_of(pos, width):
    half = width // 2
    freq = 10000.0 ** (-(2.0 * jnp.arange(half, dtype=jnp.float32)) / width)
    return pos.astype(jnp.float32)[..., None] * freq


def rotate(values, angles):
    half = values.shape[-1] // 2
    first = values[..., :half]
    second = values[..., half:]
    cosine = jnp.cos(angles)
    sine = jnp.sin(angles)
    return jnp.concatenate(
        [first * cosine - second * sine, first * sine + second * cosine], axis=-1
    )


def shard_positions(pair, start, count, tok_len):
    rows = start + jnp.arange(count, dtype=jnp.int32)
    half = tok_len // 2
    block_id = jnp.where(rows < half, pair[0], pair[1])
    return block_id * half + rows % half


def rotate_queries_kernel(x_ref, cos_ref, sin_ref, o_ref):
    lane = lax.broadcasted_iota(jnp.int32, cos_ref.shape, 1)
    low = lane % 64 < 32
    left = lane < 64
    cosine = cos_ref[...]
    sine = sin_ref[...]
    for pair in range(x_ref.shape[1] // 128):
        x = x_ref[:, pair * 128 : (pair + 1) * 128].astype(jnp.float32)
        swapped = jnp.where(low, pltpu.roll(x, 96, 1), pltpu.roll(x, 32, 1))
        turned = x * cosine + swapped * sine
        high = turned.astype(jnp.bfloat16).astype(jnp.float32)
        rest = turned - high
        first = jnp.where(left, high, pltpu.roll(rest, 64, 1))
        second = jnp.where(left, pltpu.roll(high, 64, 1), rest)
        o_ref[:, pair * 256 : pair * 256 + 128] = first.astype(jnp.bfloat16)
        o_ref[:, pair * 256 + 128 : pair * 256 + 256] = second.astype(jnp.bfloat16)


def rotate_queries(q_rope, angles):
    tok_len, width = q_rope.shape
    cosine = jnp.cos(angles)
    sine = jnp.sin(angles)
    cos4 = jnp.concatenate([cosine] * 4, 1)
    sin4 = jnp.concatenate([-sine, sine, -sine, sine], 1)
    return pl.pallas_call(
        rotate_queries_kernel,
        out_shape=jax.ShapeDtypeStruct((tok_len, 2 * width), jnp.bfloat16),
        cost_estimate=pl.CostEstimate(
            flops=4 * tok_len * width, bytes_accessed=6 * tok_len * width, transcendentals=0
        ),
        name="rotate_queries",
    )(q_rope, cos4, sin4)


def attend_kernel(width, pieces, sel_ref, lat_ref, rot_ref, qn_ref, qr_ref, *refs):
    k_refs, v_refs = refs[:pieces], refs[pieces : 2 * pieces]
    o_ref, key_s, val_s = refs[-3:]
    lat = lat_ref[...]
    up_k = jnp.concatenate([r[...] for r in k_refs], 0)
    up_v = jnp.concatenate([r[...] for r in v_refs], 0)
    key_s[...] = jnp.dot(lat, up_k, preferred_element_type=jnp.float32).astype(jnp.bfloat16)
    val_s[...] = jnp.dot(lat, up_v, preferred_element_type=jnp.float32).astype(jnp.bfloat16)
    coef = LOG2E / (NOPE + ROPE) ** 0.5
    row = lax.broadcasted_iota(jnp.int32, (HALF, HALF), 0)
    col = lax.broadcasted_iota(jnp.int32, (HALF, HALF), 1)
    causal = col <= row
    contract = (((1,), (1,)), ((), ()))
    early = [sel_ref[j] != 0 for j in range(STEPS - 1)]
    q_at = [pl.multiple_of(jnp.where(e, 0, HALF), HALF) for e in early]
    k_at = [
        pl.multiple_of(jnp.where(e, j + 1, STEPS + j + 1) * HALF, HALF)
        for j, e in enumerate(early)
    ]

    for h in range(width):
        cols = slice(h * NOPE, (h + 1) * NOPE)

        def queries(start):
            rows = pl.ds(start, HALF)
            return jnp.concatenate([qn_ref[rows, cols], qr_ref[rows, cols]], 1)

        def scores(q, start, count):
            rows = pl.ds(start, count)
            k = jnp.concatenate([key_s[rows, cols], rot_ref[rows, :]], 1)
            return lax.dot_general(q, k, contract, preferred_element_type=jnp.float32)

        q_late = queries(HALF)
        full = scores(q_late, 0, (STEPS + 1) * HALF)
        late = [full[:, i * HALF : (i + 1) * HALF] for i in range(STEPS)]
        late.append(jnp.where(causal, full[:, STEPS * HALF :], NEG))
        first = jnp.where(causal, scores(queries(0), 0, HALF), NEG)
        chosen = [scores(queries(q_at[j]), k_at[j], HALF) for j in range(STEPS - 1)]

        top_late = functools.reduce(jnp.maximum, late)
        top_first = first
        for e, s in zip(early, chosen):
            top_late = jnp.maximum(top_late, jnp.where(e, NEG, s))
            top_first = jnp.maximum(top_first, jnp.where(e, s, NEG))
        top_late = jnp.max(top_late, axis=1, keepdims=True)
        top_first = jnp.max(top_first, axis=1, keepdims=True)
        p_late = [jnp.exp2((s - top_late) * coef) for s in late]
        p_first = jnp.exp2((first - top_first) * coef)
        p_chosen = [
            jnp.exp2((s - jnp.where(e, top_first, top_late)) * coef)
            for e, s in zip(early, chosen)
        ]
        sum_late = functools.reduce(jnp.add, p_late)
        sum_first = p_first
        for e, p in zip(early, p_chosen):
            sum_late = sum_late + jnp.where(e, 0.0, p)
            sum_first = sum_first + jnp.where(e, p, 0.0)
        sum_late = jnp.sum(sum_late, axis=1, keepdims=True)
        sum_first = jnp.sum(sum_first, axis=1, keepdims=True)

        def weighted(p, start, count):
            return jnp.dot(
                p.astype(jnp.bfloat16),
                val_s[pl.ds(start, count), cols],
                preferred_element_type=jnp.float32,
            )

        out_late = weighted(jnp.concatenate(p_late, 1), 0, (STEPS + 1) * HALF)
        out_first = weighted(p_first, 0, HALF)
        for j, e in enumerate(early):
            part = weighted(p_chosen[j], k_at[j], HALF)
            out_late = out_late + jnp.where(e, 0.0, part)
            out_first = out_first + jnp.where(e, part, 0.0)
        o_ref[:HALF, cols] = (out_first / sum_first).astype(jnp.bfloat16)
        o_ref[HALF:, cols] = (out_late / sum_late).astype(jnp.bfloat16)


def attend(lane, lanes, sel, lat, rot, q_nope, q_rot, pieces, earlier):
    tok_len, all_cols = q_nope.shape
    lane_cols = all_cols // lanes
    width = 2
    cols = width * NOPE
    steps = lane_cols // cols
    count, depth = lat.shape

    def whole(shape):
        return pl.BlockSpec(shape, lambda i: (0, 0))

    def mine(shape):
        return pl.BlockSpec(shape, lambda i: (0, lane * steps + i))

    in_specs = [
        pl.BlockSpec(memory_space=pltpu.SMEM),
        whole(lat.shape),
        whole(rot.shape),
        mine((tok_len, cols)),
        mine((tok_len, cols)),
    ]
    in_specs += [pl.BlockSpec((p.shape[0], cols), lambda i: (0, i)) for p in pieces]
    in_specs += [pl.BlockSpec((p.shape[0], cols), lambda i: (0, steps + i)) for p in pieces]
    operands = [sel, lat, rot, q_nope, q_rot, *pieces, *pieces]
    aliases = {}
    if earlier is not None:
        in_specs.append(pl.BlockSpec(memory_space=pl.ANY))
        aliases = {len(operands): 0}
        operands.append(earlier)
    heads = lane_cols // NOPE
    flops = 4 * count * depth * lane_cols + heads * 7 * HALF * HALF * (2 * 256 + 2 * VDIM)
    return pl.pallas_call(
        functools.partial(attend_kernel, width, len(pieces)),
        grid=(steps,),
        in_specs=in_specs,
        out_specs=mine((tok_len, cols)),
        out_shape=jax.ShapeDtypeStruct((tok_len, all_cols), jnp.bfloat16),
        scratch_shapes=[
            pltpu.VMEM((count, cols), jnp.bfloat16),
            pltpu.VMEM((count, cols), jnp.bfloat16),
        ],
        input_output_aliases=aliases,
        compiler_params=pltpu.CompilerParams(vmem_limit_bytes=40 * 1024 * 1024),
        cost_estimate=pl.CostEstimate(
            flops=flops,
            bytes_accessed=2 * (4 * depth * lane_cols + 3 * tok_len * lane_cols + count * 640),
            transcendentals=heads * 7 * HALF * HALF,
        ),
        name=f"attend_{lane}",
    )(*operands)


def local(q_nope, q_rope, latent, k_rope, blocks, w_uk, w_uv):
    tok_len, all_cols = q_nope.shape
    quarter = latent.shape[0]
    w_rows = w_uk.shape[0]
    n_ctx = lax.axis_size("ctx")
    ctx_index = lax.axis_index("ctx")
    head_index = lax.axis_index("head")
    z, x = ctx_index // (NX * NY), (ctx_index // NY) % NX
    lanes = 2
    lane_cols = all_cols // lanes

    pieces = []
    for lane in range(lanes):
        cols = slice(lane * lane_cols, (lane + 1) * lane_cols)
        shard = jnp.concatenate([w_uk[:, cols], w_uv[:, cols]], 1)
        pieces.append(gather_pieces(lane, shard))

    own_pair = blocks[ctx_index]
    own_pos = shard_positions(own_pair, head_index * quarter, quarter, tok_len)
    own_rot = rotate(k_rope.astype(jnp.float32), angles_of(own_pos, ROPE)).astype(jnp.bfloat16)
    own = jnp.concatenate([latent, own_rot, own_rot], 1)
    across = lax.ppermute(own, "head", [(0, 2), (2, 0), (1, 3), (3, 1)])
    upper = head_index // 2 == 0
    two = jnp.stack([jnp.where(upper, own, across), jnp.where(upper, across, own)])
    visited = [two]
    for step in range(1, STEPS):
        pairs = [(source, (source + step) % n_ctx) for source in range(n_ctx)]
        visited.append(lax.ppermute(two, "ctx", pairs))
    held = jnp.stack(visited)
    both = lax.all_gather(held, "head", axis=0, axis_index_groups=[[0, 1], [2, 3]])
    both = both.transpose(2, 1, 0, 3, 4).reshape(STEPS * tok_len, own.shape[1])
    depth = latent.shape[1]
    lat_all, rot_all = both[:, :depth], both[:, depth:]

    lats = []
    for lane in range(lanes):
        order = row_order(lane, z, x, w_rows)
        place_of = lax.broadcasted_iota(jnp.int32, (depth, depth), 0) == order[None, :]
        lats.append(jnp.dot(lat_all, place_of.astype(jnp.bfloat16)))

    query_pos = shard_positions(own_pair, 0, tok_len, tok_len)
    q_rot = rotate_queries(q_rope, angles_of(query_pos, ROPE))
    sel = jnp.stack(
        [
            (blocks[(ctx_index - step) % n_ctx, 0] < own_pair[0]).astype(jnp.int32)
            for step in range(1, STEPS)
        ]
    )
    result = None
    for lane in range(lanes):
        result = attend(
            lane, lanes, sel, lats[lane], rot_all, q_nope, q_rot, pieces[lane], result
        )
    return result


def solution(mesh):
    in_specs = (
        P("ctx", "head"),
        P("ctx", "head"),
        P(("ctx", "head"), None),
        P(("ctx", "head"), None),
        P(),
        P("ctx", "head"),
        P("ctx", "head"),
    )
    out_specs = P("ctx", "head")
    return jax.shard_map(local, mesh=mesh, in_specs=in_specs, out_specs=out_specs, check_vma=False)
```

time: 1440 us -> 125 us (0.09); the launches traced: 1420 us -> 124 us
  waiting for transfers between devices: 1300 us -> 9.01 us
  starting transfers between devices: 16.1 us -> 65.1 us
  matrix products: 27.8 us -> 3.26 us
  Pallas kernels: 0 us -> 19.4 us
  blocking collectives: 19.2 us -> 2.51 us
    all_gather x2 -> x0, waiting for transfers between devices: 1300 us -> none  [the longest x1 680 us: local(): lax.all_gather(w_uk, 'ctx', axis=0, tiled=True)]
    ppermute x4 -> x11, starting transfers between devices: 16.1 us -> 43.9 us  [the longest x8 28.2 us: shifted(): return lax.ppermute(value, 'ctx', pairs)]
    dot_general x20 -> x2, matrix products: 27.8 us -> 3.26 us  [local(): lats.append(jnp.dot(lat_all, place_of.astype(jnp.bfloat16)))]
    all_to_all x0 -> x2, starting transfers between devices: none -> 21.2 us  [gather_pieces(): lax.all_to_all(jnp.broadcast_to(shard[None], (size,) + shard.shape), 'ctx...]
    pallas_call x0 -> x3, Pallas kernels: none -> 19.4 us  [the longest x2 16.1 us: attend(): pl.pallas_call(functools.partial(attend_kernel, width, len(pieces)), grid...]
    all_gather x2 -> x1, blocking collectives: 19.2 us -> 2.51 us  [local(): lax.all_gather(held, 'head', axis=0, axis_index_groups=[[0, 1], [2, 3]])]
  transfers between devices with their start and end apart: 6 -> 13, of which waited for: 4 -> 2; matrix products, arithmetic and copies ran while one was open for 1% -> 15% of each run, Pallas kernels for 0% -> 9%
where the time goes in v1:
time: 125 us; the launch traced here: 124 us
  starting transfers between devices  65.1 us (52%)
  Pallas kernels  19.4 us (16%)
  local copies, waits for them, and re-layouts  17.2 us (14%)
  waiting for transfers between devices  9.01 us (7%)
  other arithmetic  4.56 us (4%)
  matrix products  3.26 us (3%)
  between operations  3.02 us (2%)
  blocking collectives  2.51 us (2%)
    ppermute x8, starting transfers between devices, shifted(): return lax.ppermute(value, 'ctx', pairs)  28.2 us
    all_to_all x2, starting transfers between devices, gather_pieces(): lax.all_to_all(jnp.broadcast_to(shard[None], (size,) + shard.shape), 'ctx...  21.2 us
    pallas_call x2, Pallas kernels, attend(): pl.pallas_call(functools.partial(attend_kernel, width, len(pieces)), grid...  16.1 us
    ppermute x2, starting transfers between devices, local(): visited.append(lax.ppermute(two, 'ctx', pairs))  7.97 us
    ppermute x1, starting transfers between devices, local(): across = lax.ppermute(own, 'head', [(0, 2), (2, 0), (1, 3), (3, 1)])  7.73 us
    all_to_all x2, waiting for transfers between devices, gather_pieces(): lax.all_to_all(jnp.broadcast_to(shard[None], (size,) + shard.shape), 'ctx...  6.94 us
    slice x4, local copies, waits for them, and re-layouts, gather_pieces(): own[mid:]  5.45 us
    slice x2, local copies, waits for them, and re-layouts, gather_pieces(): own[:mid]  3.44 us
  transfers between devices with their start and end apart: 13, of which 2 were waited for; matrix products, arithmetic and copies ran while one was open for 15% of the time, Pallas kernels for 9%

profile of v1, /device:TPU:6, one launch (start us, length us, event | category | flops | bytes accessed | tf_op | source)
XLA Modules:
  0.0 124.1 jit_solution(2100554231538807255)
XLA Ops:
  0.0 0.8 constant_dynamic-slice_fusion.1
  0.8 0.6 fusion.51
  1.4 0.1 copy.11
  1.5 0.0 copy-start.5
  1.5 1.3 %fusion.45 = f32[64]{0:T(128)S(1)} fusion(s32[]{:T(128)} %bitcast.5, s32[]{:T(128)} %bitcast.1, s32[]{:T(128)S(6)} %mul.120), kind=kLoop, calls=%fused_computation.99 | loop fusion | flops 1088 | bytes 268 | tf_op jit(solution)/shard_map/convert_element_type | solution.py:89
  2.8 0.1 fusion.14
  2.9 0.1 copy.12
  3.0 0.1 copy.13
  3.2 0.0 copy-start.7
  3.2 0.0 copy-start.8
  3.2 0.1 concatenate.18
  3.3 7.7 %collective-permute-start = (bf16[64,640]{1,0:T(8,128)(2,1)S(1)}, bf16[64,640]{1,0:T(8,128)(2,1)S(1)}, u32[]{:S(2)}, u32[]{:S(2)}) collective-permute-start(bf16[64,640]{1,0:T(8,128)(2,1)S(1)} %concatenate.18), channel_id=1, source_target_pairs={{0,2},{2,0},{1,3},{3,1},{4,6},{6,4},{5,7},{7,5},{8,10},{10,8},{9,1... | collective-permute-start | bytes 245768 | tf_op jit(solution)/shard_map/ppermute | solution.py:294
  11.1 1.0 broadcast_in_dim.39
  12.1 11.9 %all-to-all-start.1 = ((bf16[32,4,2048]{2,1,0:T(4,128)(2,1)}), bf16[32,4,2048]{2,1,0:T(4,128)(2,1)S(1)}, u32[]{:S(2)}, u32[]{:S(2)}) async-start(bf16[32,4,2048]{2,1,0:T(4,128)(2,1)} %broadcast_in_dim.39), calls=%async_computation.1 | async-start | bytes 1048576 | tf_op jit(solution)/shard_map/all_to_all | solution.py:51
  24.1 1.3 %fusion.41 = f32[256]{0:T(256)S(1)} fusion(s32[]{:T(128)} %bitcast.5, s32[]{:T(128)} %bitcast.1), kind=kLoop, calls=%fused_computation.91 | loop fusion | flops 2816 | bytes 1032 | tf_op jit(solution)/shard_map/convert_element_type | solution.py:89
  25.4 0.5 fusion.6
  26.0 0.0 copy-start.9
  26.0 0.7 copy-done.9
  26.7 0.6 constant_dynamic-slice_fusion.2
  29.7 1.0 pad_maximum_fusion.2
  30.8 0.0 collective-permute-done
  30.8 4.6 %collective-permute-start.2 = (bf16[2,64,640]{2,1,0:T(8,128)(2,1)S(1)}, bf16[2,64,640]{2,1,0:T(8,128)(2,1)S(1)}, u32[]{:S(2)}, u32[]{:S(2)}) collective-permute-start(bf16[2,64,640]{2,1,0:T(8,128)(2,1)S(1)} %get-tuple-element.10), channel_id=1, source_target_pairs={{0,8},{4,12},{8,16},{12,20},{16,24},{20,28},{24,32},{28,36},{32,40... | collective-permute-start | bytes 491528 | tf_op jit(solution)/shard_map/ppermute | solution.py:300
  35.4 3.4 %collective-permute-start.1 = (bf16[2,64,640]{2,1,0:T(8,128)(2,1)S(1)}, bf16[2,64,640]{2,1,0:T(8,128)(2,1)S(1)}, u32[]{:S(2)}, u32[]{:S(2)}) collective-permute-start(bf16[2,64,640]{2,1,0:T(8,128)(2,1)S(1)} %get-tuple-element.10), channel_id=1, source_target_pairs={{0,4},{4,8},{8,12},{12,16},{16,20},{20,24},{24,28},{28,32},{32,36}... | collective-permute-start | bytes 491528 | tf_op jit(solution)/shard_map/ppermute | solution.py:300
  38.8 0.1 add_convert_fusion.sel_ref
  38.9 3.3 %rotate_queries.1.qr_ref = bf16[256,2048]{1,0:T(8,128)(2,1)} custom-call(bf16[256,1024]{1,0:T(8,128)(2,1)} %x_ref.1, f32[256,128]{1,0:T(8,128)} %get-tuple-element.26.cos_ref, f32[256,128]{1,0:T(8,128)} %get-tuple-element.27.sin_ref), custom_call_target="tpu_custom_call" | custom-call | flops 1048576 | bytes 1572864 | tf_op jit(solution)/shard_map/rotate_queries/pallas_call | solution.py:134
  42.2 6.9 %all-to-all-done.1 = bf16[32,4,2048]{2,1,0:T(4,128)(2,1)S(1)} async-done(((bf16[32,4,2048]{2,1,0:T(4,128)(2,1)}), bf16[32,4,2048]{2,1,0:T(4,128)(2,1)S(1)}, u32[]{:S(2)}, u32[]{:S(2)}) %all-to-all-start.1) | async-done | bytes 524320 | tf_op jit(solution)/shard_map/all_to_all | solution.py:51
  49.2 1.0 broadcast_in_dim.38
  50.2 9.3 %all-to-all-start = ((bf16[32,4,2048]{2,1,0:T(4,128)(2,1)}), bf16[32,4,2048]{2,1,0:T(4,128)(2,1)S(1)}, u32[]{:S(2)}, u32[]{:S(2)}) async-start(bf16[32,4,2048]{2,1,0:T(4,128)(2,1)} %broadcast_in_dim.38), calls=%async_computation | async-start | bytes 1048576 | tf_op jit(solution)/shard_map/all_to_all | solution.py:51
  59.6 0.0 collective-permute-done.2
  59.6 0.0 collective-permute-done.1
  59.6 0.1 pad_maximum_fusion
  59.6 2.5 %all-gather = bf16[6,2,64,640]{3,2,1,0:T(8,128)(2,1)S(1)} all-gather(bf16[3,2,64,640]{3,2,1,0:T(8,128)(2,1)S(1)} %pad_maximum_fusion), channel_id=2, replica_groups={{0,1},{2,3},{4,5},{6,7},{8,9},{10,11},{12,13},{14,15},{16,17},{18,19},{..., dimensions={0}, use_global_device_ids=true | all-gather | bytes 1474560 | tf_op jit(solution)/shard_map/all_gather | solution.py:302
  62.2 0.1 copy.16
  62.3 0.1 reshape.200.refs_0_.refs_5_
  62.4 1.9 %collective-permute-start.7 = (bf16[128,2048]{1,0:T(8,128)(2,1)S(1)}, bf16[128,2048]{1,0:T(8,128)(2,1)S(1)}, u32[]{:S(2)}, u32[]{:S(2)}) collective-permute-start(bf16[128,2048]{1,0:T(8,128)(2,1)S(1)} %reshape.200.refs_0_.refs_5_), channel_id=1, source_target_pairs={{0,48},{4,52},{8,56},{12,60},{16,0},{20,4},{24,8},{28,12},{32,16},... | collective-permute-start | bytes 1572872 | tf_op jit(solution)/shard_map/ppermute | solution.py:31
  64.3 0.9 fusion.47
  65.2 0.8 slice.77
  66.0 3.2 %collective-permute-start.10 = (bf16[64,2048]{1,0:T(8,128)(2,1)}, bf16[64,2048]{1,0:T(8,128)(2,1)S(1)}, u32[]{:S(2)}, u32[]{:S(2)}) collective-permute-start(bf16[64,2048]{1,0:T(8,128)(2,1)} %slice.77), channel_id=1, source_target_pairs={{0,64},{4,68},{8,72},{12,76},{16,80},{20,84},{24,88},{28,92},{32,9... | collective-permute-start | bytes 786440 | tf_op jit(solution)/shard_map/ppermute | solution.py:31
  69.2 1.5 %fusion.1.lat_ref = bf16[768,512]{1,0:T(8,128)(2,1)} fusion(bf16[768,640]{1,0:T(8,128)(2,1)S(1)} %bitcast.19, s32[512]{0:T(512)S(1)} %fusion.33), kind=kOutput, calls=%fused_computation.3 | convolution fusion | flops 402915328 | bytes 1574912 | tf_op jit(solution)/shard_map/dot_general | solution.py:311
  70.8 4.4 %collective-permute-start.8 = (bf16[128,2048]{1,0:T(8,128)(2,1)S(1)}, bf16[128,2048]{1,0:T(8,128)(2,1)S(1)}, u32[]{:S(2)}, u32[]{:S(2)}) collective-permute-start(bf16[128,2048]{1,0:T(8,128)(2,1)S(1)} %reshape.200.refs_0_.refs_5_), channel_id=1, source_target_pairs={{0,16},{4,20},{8,24},{12,28},{16,32},{20,36},{24,40},{28,44},{32,4... | collective-permute-start | bytes 1572872 | tf_op jit(solution)/shard_map/ppermute | solution.py:31
  75.2 0.0 all-to-all-done
  75.2 0.8 copy-done.3
  76.0 0.1 reshape.199.refs_0_.refs_5_
  76.1 4.5 %collective-permute-start.3 = (bf16[128,2048]{1,0:T(8,128)(2,1)S(1)}, bf16[128,2048]{1,0:T(8,128)(2,1)S(1)}, u32[]{:S(2)}, u32[]{:S(2)}) collective-permute-start(bf16[128,2048]{1,0:T(8,128)(2,1)S(1)} %reshape.199.refs_0_.refs_5_), channel_id=1, source_target_pairs={{0,448},{4,452},{8,456},{12,460},{16,464},{20,468},{24,472},{28,47... | collective-permute-start | bytes 1572872 | tf_op jit(solution)/shard_map/ppermute | solution.py:31
  80.6 1.9 %collective-permute-start.4 = (bf16[128,2048]{1,0:T(8,128)(2,1)S(1)}, bf16[128,2048]{1,0:T(8,128)(2,1)S(1)}, u32[]{:S(2)}, u32[]{:S(2)}) collective-permute-start(bf16[128,2048]{1,0:T(8,128)(2,1)S(1)} %reshape.199.refs_0_.refs_5_), channel_id=1, source_target_pairs={{0,64},{4,68},{8,72},{12,76},{16,80},{20,84},{24,88},{28,92},{32,9... | collective-permute-start | bytes 1572872 | tf_op jit(solution)/shard_map/ppermute | solution.py:31
  82.6 1.7 %slice.75 = bf16[64,2048]{1,0:T(8,128)(2,1)} reshape(bf16[16,4,2048]{2,1,0:T(4,128)(2,1)} %get-tuple-element.6) | data formatting | bytes 524288 | tf_op jit(solution)/shard_map/slice | solution.py:65
  84.3 0.0 collective-permute-done.10.refs_4_.refs_9_
  84.3 5.1 %collective-permute-start.9 = (bf16[64,2048]{1,0:T(8,128)(2,1)}, bf16[64,2048]{1,0:T(8,128)(2,1)}, u32[]{:S(2)}, u32[]{:S(2)}) collective-permute-start(bf16[64,2048]{1,0:T(8,128)(2,1)} %slice.75), channel_id=1, source_target_pairs={{0,448},{4,452},{8,456},{12,460},{16,464},{20,468},{24,472},{28,47... | collective-permute-start | bytes 786440 | tf_op jit(solution)/shard_map/ppermute | solution.py:31
  89.4 2.1 %fusion.48 = (bf16[16,4,2048]{2,1,0:T(4,128)(2,1)}, bf16[16,4,2048]{2,1,0:T(4,128)(2,1)}) fusion(bf16[32,4,2048]{2,1,0:T(4,128)(2,1)} %copy-done.3), kind=kLoop, calls=%fused_computation.103 | loop fusion | bytes 1048576 | tf_op jit(solution)/shard_map/slice | solution.py:66
  91.5 1.7 %slice.69 = bf16[64,2048]{1,0:T(8,128)(2,1)} reshape(bf16[16,4,2048]{2,1,0:T(4,128)(2,1)} %get-tuple-element.8) | data formatting | bytes 524288 | tf_op jit(solution)/shard_map/slice | solution.py:65
  93.2 1.7 %slice.71 = bf16[64,2048]{1,0:T(8,128)(2,1)} reshape(bf16[16,4,2048]{2,1,0:T(4,128)(2,1)} %get-tuple-element.7) | data formatting | bytes 524288 | tf_op jit(solution)/shard_map/slice | solution.py:66
  94.9 2.0 %collective-permute-done.9.refs_3_.refs_8_ = bf16[64,2048]{1,0:T(8,128)(2,1)} collective-permute-done((bf16[64,2048]{1,0:T(8,128)(2,1)}, bf16[64,2048]{1,0:T(8,128)(2,1)}, u32[]{:S(2)}, u32[]{:S(2)}) %collective-permute-start.9) | collective-permute-done | bytes 262176 | tf_op jit(solution)/shard_map/ppermute | solution.py:31
  97.0 1.9 %collective-permute-start.5 = (bf16[64,2048]{1,0:T(8,128)(2,1)}, bf16[64,2048]{1,0:T(8,128)(2,1)S(1)}, u32[]{:S(2)}, u32[]{:S(2)}) collective-permute-start(bf16[64,2048]{1,0:T(8,128)(2,1)} %slice.69), channel_id=1, source_target_pairs={{0,48},{4,52},{8,56},{12,60},{16,0},{20,4},{24,8},{28,12},{32,16},... | collective-permute-start | bytes 786440 | tf_op jit(solution)/shard_map/ppermute | solution.py:31
  98.9 0.0 collective-permute-done.7.refs_1_.refs_6_
  98.9 5.1 %collective-permute-start.6 = (bf16[64,2048]{1,0:T(8,128)(2,1)}, bf16[64,2048]{1,0:T(8,128)(2,1)S(1)}, u32[]{:S(2)}, u32[]{:S(2)}) collective-permute-start(bf16[64,2048]{1,0:T(8,128)(2,1)} %slice.71), channel_id=1, source_target_pairs={{0,16},{4,20},{8,24},{12,28},{16,32},{20,36},{24,40},{28,44},{32,4... | collective-permute-start | bytes 786440 | tf_op jit(solution)/shard_map/ppermute | solution.py:31
  104.0 1.8 %fusion.lat_ref = bf16[768,512]{1,0:T(8,128)(2,1)S(1)} fusion(bf16[768,640]{1,0:T(8,128)(2,1)} %bitcast.20, s32[512]{0:T(512)S(1)} %fusion.26), kind=kOutput, calls=%fused_computation.2 | convolution fusion | flops 402915328 | bytes 1574912 | tf_op jit(solution)/shard_map/dot_general | solution.py:311
  105.8 0.9 slice.81.rot_ref
  106.7 0.0 collective-permute-done.8.refs_2_.refs_7_
  106.8 1.1 copy-done.2
  107.9 8.1 %attend_0.1.refs_10_ = bf16[256,2048]{1,0:T(8,128)(2,1)} custom-call(s32[2]{0:T(128)S(1)} %add_convert_fusion.sel_ref, bf16[768,512]{1,0:T(8,128)(2,1)S(1)} %copy-done.2, bf16[768,128]{1,0:T(8,128)(2,1)S(1)} %slice.81.rot_ref, bf16[256,2048]{1,0:T(8,128)(2,1)S(1)} %copy-done.1, bf16[256,2048]{1,0:T(8,128)(2,1)S(1)} %copy-done, ...), custom_call_target="tpu_custom_call" | custom-call | flops 2315255808 | bytes 6750208 | tf_op jit(solution)/shard_map/attend_0/pallas_call | solution.py:252
  116.0 0.0 collective-permute-done.5.refs_3_.refs_8_
  116.0 0.0 collective-permute-done.6.refs_4_.refs_9_
  116.0 0.0 collective-permute-done.3.refs_1_.refs_6_
  116.1 8.0 %attend_1.1 = bf16[256,2048]{1,0:T(8,128)(2,1)} custom-call(s32[2]{0:T(128)S(1)} %add_convert_fusion.sel_ref, bf16[768,512]{1,0:T(8,128)(2,1)S(1)} %fusion.lat_ref, bf16[768,128]{1,0:T(8,128)(2,1)S(1)} %slice.81.rot_ref, bf16[256,2048]{1,0:T(8,128)(2,1)S(1)} %copy-done.1, bf16[256,2048]{1,0:T(8,128)(2,1)S(1)} %copy-done, ...), custom_call_target="tpu_custom_call", output_to_operand_aliasing={{}: (15, {})} | custom-call | flops 2315255808 | bytes 6750208 | tf_op jit(solution)/shard_map/attend_1/pallas_call | solution.py:252
  (23 shorter events, 0.2 us)
Async XLA Ops:
  0.0 1.4 %copy-start.6 = (bf16[64,64]{1,0:T(8,128)(2,1)S(1)}, bf16[64,64]{1,0:T(8,128)(2,1)}, u32[]{:S(2)}) copy-start(bf16[64,64]{1,0:T(8,128)(2,1)} %param.10) | copy-start | bytes 24580
  1.5 1.7 %copy-start.5 = (bf16[64,512]{1,0:T(8,128)(2,1)S(1)}, bf16[64,512]{1,0:T(8,128)(2,1)}, u32[]{:S(2)}) copy-start(bf16[64,512]{1,0:T(8,128)(2,1)} %param.9) | copy-start | bytes 196612
  3.2 7.9 %copy-start.7 = (bf16[4,2048]{1,0:T(4,128)(2,1)S(1)}, bf16[4,2048]{1,0:T(4,128)(2,1)}, u32[]{:S(2)}) copy-start(bf16[4,2048]{1,0:T(4,128)(2,1)} %param.12) | copy-start | bytes 49156
  3.2 7.9 %copy-start.8 = (bf16[4,2048]{1,0:T(4,128)(2,1)S(1)}, bf16[4,2048]{1,0:T(4,128)(2,1)}, u32[]{:S(2)}) copy-start(bf16[4,2048]{1,0:T(4,128)(2,1)} %param.13) | copy-start | bytes 49156
  3.3 27.5 %collective-permute-start = (bf16[64,640]{1,0:T(8,128)(2,1)S(1)}, bf16[64,640]{1,0:T(8,128)(2,1)S(1)}, u32[]{:S(2)}, u32[]{:S(2)}) collective-permute-start(bf16[64,640]{1,0:T(8,128)(2,1)S(1)} %concatenate.18), channel_id=1, source_target_pairs={{0,2},{2,0},{1,3},{3,1},{4,6},{6,4},{5,7},{7,5},{8,10},{10,8},{9,1... | collective-permute-start | bytes 245768 | tf_op jit(solution)/shard_map/ppermute | solution.py:294
  12.1 37.0 %all-to-all-start.1 = ((bf16[32,4,2048]{2,1,0:T(4,128)(2,1)}), bf16[32,4,2048]{2,1,0:T(4,128)(2,1)S(1)}, u32[]{:S(2)}, u32[]{:S(2)}) async-start(bf16[32,4,2048]{2,1,0:T(4,128)(2,1)} %broadcast_in_dim.39), calls=%async_computation.1 | async-start | bytes 1048576 | tf_op jit(solution)/shard_map/all_to_all | solution.py:51
  26.0 0.7 copy-start.9
  30.8 28.7 %collective-permute-start.2 = (bf16[2,64,640]{2,1,0:T(8,128)(2,1)S(1)}, bf16[2,64,640]{2,1,0:T(8,128)(2,1)S(1)}, u32[]{:S(2)}, u32[]{:S(2)}) collective-permute-start(bf16[2,64,640]{2,1,0:T(8,128)(2,1)S(1)} %get-tuple-element.10), channel_id=1, source_target_pairs={{0,8},{4,12},{8,16},{12,20},{16,24},{20,28},{24,32},{28,36},{32,40... | collective-permute-start | bytes 491528 | tf_op jit(solution)/shard_map/ppermute | solution.py:300
  35.4 24.1 %collective-permute-start.1 = (bf16[2,64,640]{2,1,0:T(8,128)(2,1)S(1)}, bf16[2,64,640]{2,1,0:T(8,128)(2,1)S(1)}, u32[]{:S(2)}, u32[]{:S(2)}) collective-permute-start(bf16[2,64,640]{2,1,0:T(8,128)(2,1)S(1)} %get-tuple-element.10), channel_id=1, source_target_pairs={{0,4},{4,8},{8,12},{12,16},{16,20},{20,24},{24,28},{28,32},{32,36}... | collective-permute-start | bytes 491528 | tf_op jit(solution)/shard_map/ppermute | solution.py:300
  50.2 25.0 %all-to-all-start = ((bf16[32,4,2048]{2,1,0:T(4,128)(2,1)}), bf16[32,4,2048]{2,1,0:T(4,128)(2,1)S(1)}, u32[]{:S(2)}, u32[]{:S(2)}) async-start(bf16[32,4,2048]{2,1,0:T(4,128)(2,1)} %broadcast_in_dim.38), calls=%async_computation | async-start | bytes 1048576 | tf_op jit(solution)/shard_map/all_to_all | solution.py:51
  62.3 7.0 %copy-start.4 = (bf16[2,3,2,64,640]{4,3,0,1,2:T(8,128)(2,1)}, bf16[2,3,2,64,640]{4,3,0,1,2:T(8,128)(2,1)S(1)}, u32[]{:S(2)}) copy-start(bf16[2,3,2,64,640]{4,3,0,1,2:T(8,128)(2,1)S(1)} %copy.16) | copy-start | bytes 2949124
  62.4 36.5 %collective-permute-start.7 = (bf16[128,2048]{1,0:T(8,128)(2,1)S(1)}, bf16[128,2048]{1,0:T(8,128)(2,1)S(1)}, u32[]{:S(2)}, u32[]{:S(2)}) collective-permute-start(bf16[128,2048]{1,0:T(8,128)(2,1)S(1)} %reshape.200.refs_0_.refs_5_), channel_id=1, source_target_pairs={{0,48},{4,52},{8,56},{12,60},{16,0},{20,4},{24,8},{28,12},{32,16},... | collective-permute-start | bytes 1572872 | tf_op jit(solution)/shard_map/ppermute | solution.py:31
  66.0 18.3 %collective-permute-start.10 = (bf16[64,2048]{1,0:T(8,128)(2,1)}, bf16[64,2048]{1,0:T(8,128)(2,1)S(1)}, u32[]{:S(2)}, u32[]{:S(2)}) collective-permute-start(bf16[64,2048]{1,0:T(8,128)(2,1)} %slice.77), channel_id=1, source_target_pairs={{0,64},{4,68},{8,72},{12,76},{16,80},{20,84},{24,88},{28,92},{32,9... | collective-permute-start | bytes 786440 | tf_op jit(solution)/shard_map/ppermute | solution.py:31
  70.8 36.0 %collective-permute-start.8 = (bf16[128,2048]{1,0:T(8,128)(2,1)S(1)}, bf16[128,2048]{1,0:T(8,128)(2,1)S(1)}, u32[]{:S(2)}, u32[]{:S(2)}) collective-permute-start(bf16[128,2048]{1,0:T(8,128)(2,1)S(1)} %reshape.200.refs_0_.refs_5_), channel_id=1, source_target_pairs={{0,16},{4,20},{8,24},{12,28},{16,32},{20,36},{24,40},{28,44},{32,4... | collective-permute-start | bytes 1572872 | tf_op jit(solution)/shard_map/ppermute | solution.py:31
  75.2 0.8 copy-start.3
  76.1 40.0 %collective-permute-start.3 = (bf16[128,2048]{1,0:T(8,128)(2,1)S(1)}, bf16[128,2048]{1,0:T(8,128)(2,1)S(1)}, u32[]{:S(2)}, u32[]{:S(2)}) collective-permute-start(bf16[128,2048]{1,0:T(8,128)(2,1)S(1)} %reshape.199.refs_0_.refs_5_), channel_id=1, source_target_pairs={{0,448},{4,452},{8,456},{12,460},{16,464},{20,468},{24,472},{28,47... | collective-permute-start | bytes 1572872 | tf_op jit(solution)/shard_map/ppermute | solution.py:31
  80.6 35.4 %collective-permute-start.4 = (bf16[128,2048]{1,0:T(8,128)(2,1)S(1)}, bf16[128,2048]{1,0:T(8,128)(2,1)S(1)}, u32[]{:S(2)}, u32[]{:S(2)}) collective-permute-start(bf16[128,2048]{1,0:T(8,128)(2,1)S(1)} %reshape.199.refs_0_.refs_5_), channel_id=1, source_target_pairs={{0,64},{4,68},{8,72},{12,76},{16,80},{20,84},{24,88},{28,92},{32,9... | collective-permute-start | bytes 1572872 | tf_op jit(solution)/shard_map/ppermute | solution.py:31
  84.3 12.7 %collective-permute-start.9 = (bf16[64,2048]{1,0:T(8,128)(2,1)}, bf16[64,2048]{1,0:T(8,128)(2,1)}, u32[]{:S(2)}, u32[]{:S(2)}) collective-permute-start(bf16[64,2048]{1,0:T(8,128)(2,1)} %slice.75), channel_id=1, source_target_pairs={{0,448},{4,452},{8,456},{12,460},{16,464},{20,468},{24,472},{28,47... | collective-permute-start | bytes 786440 | tf_op jit(solution)/shard_map/ppermute | solution.py:31
  94.9 11.8 %copy-start = (bf16[256,2048]{1,0:T(8,128)(2,1)S(1)}, bf16[256,2048]{1,0:T(8,128)(2,1)}, u32[]{:S(2)}) copy-start(bf16[256,2048]{1,0:T(8,128)(2,1)} %rotate_queries.1.qr_ref) | copy-start | bytes 3145732
  94.9 11.8 %copy-start.1 = (bf16[256,2048]{1,0:T(8,128)(2,1)S(1)}, bf16[256,2048]{1,0:T(8,128)(2,1)}, u32[]{:S(2)}) copy-start(bf16[256,2048]{1,0:T(8,128)(2,1)} %qn_ref.3) | copy-start | bytes 3145732
  97.0 19.1 %collective-permute-start.5 = (bf16[64,2048]{1,0:T(8,128)(2,1)}, bf16[64,2048]{1,0:T(8,128)(2,1)S(1)}, u32[]{:S(2)}, u32[]{:S(2)}) collective-permute-start(bf16[64,2048]{1,0:T(8,128)(2,1)} %slice.69), channel_id=1, source_target_pairs={{0,48},{4,52},{8,56},{12,60},{16,0},{20,4},{24,8},{28,12},{32,16},... | collective-permute-start | bytes 786440 | tf_op jit(solution)/shard_map/ppermute | solution.py:31
  98.9 17.1 %collective-permute-start.6 = (bf16[64,2048]{1,0:T(8,128)(2,1)}, bf16[64,2048]{1,0:T(8,128)(2,1)S(1)}, u32[]{:S(2)}, u32[]{:S(2)}) collective-permute-start(bf16[64,2048]{1,0:T(8,128)(2,1)} %slice.71), channel_id=1, source_target_pairs={{0,16},{4,20},{8,24},{12,28},{16,32},{20,36},{24,40},{28,44},{32,4... | collective-permute-start | bytes 786440 | tf_op jit(solution)/shard_map/ppermute | solution.py:31
  106.8 1.1 copy-start.2

commit v2 on v1

--- a/solution.py
+++ b/solution.py
@@ -12,6 +12,7 @@
 VDIM = 128
 STEPS = 3
 NZ, NX, NY = 8, 4, 4
+N_HEAD = 4
 HALF = 128
 LOG2E = 1.4426950408889634
 NEG = -1e30
@@ -19,16 +20,6 @@
 
 def place(z, x, y):
     return ((z % NZ) * NX + x % NX) * NY + y
-
-
-def shifted(value, dz, dx):
-    pairs = [
-        (place(z, x, y), place(z + dz, x + dx, y))
-        for z in range(NZ)
-        for x in range(NX)
-        for y in range(NY)
-    ]
-    return lax.ppermute(value, "ctx", pairs)
 
 
 def members(plan, colour):
@@ -37,34 +28,46 @@
     return [((colour - 2 * x) % 4 + 4 * far, x) for x in range(NX) for far in range(2)]
 
 
-def colour_groups(plan):
-    return [[place(z, x, y) for z, x in members(plan, c) for y in range(NY)] for c in range(4)]
+def plan_of(head):
+    return head % 2
 
 
 def colour_of(plan, z, x):
-    return (x + 2 * z) % 4 if plan == 0 else (z + 2 * x) % 4
-
-
-def gather_pieces(plan, shard):
-    groups = colour_groups(plan)
+    return jnp.where(plan == 0, x + 2 * z, z + 2 * x) % 4
+
+
+def gather_own(shard):
+    groups = [
+        [place(z, x, y) * N_HEAD + head for z, x in members(plan_of(head), c) for y in range(NY)]
+        for head in range(N_HEAD)
+        for c in range(4)
+    ]
     size = len(groups[0])
-    own = lax.all_to_all(
-        jnp.broadcast_to(shard[None], (size,) + shard.shape), "ctx", 0, 0, axis_index_groups=groups
+    return lax.all_to_all(
+        jnp.broadcast_to(shard[None], (size,) + shard.shape),
+        ("ctx", "head"),
+        0,
+        0,
+        axis_index_groups=groups,
     ).reshape(size * shard.shape[0], shard.shape[1])
-    mid = own.shape[0] // 2
-    if plan == 0:
-        up, down = (0, -1), (0, 1)
-        side, other = (-1, 0), (1, 0)
-    else:
-        up, down = (-1, 0), (1, 0)
-        side, other = (0, -1), (0, 1)
-    return (
-        own,
-        shifted(own, *up),
-        shifted(own, *down),
-        shifted(own[:mid], *side),
-        shifted(own[mid:], *other),
-    )
+
+
+def from_neighbour(value, step, along):
+    pairs = []
+    for head in range(N_HEAD):
+        on_x = (plan_of(head) == 0) == (along == 0)
+        dz, dx = (0, step) if on_x else (step, 0)
+        pairs += [
+            (place(z + dz, x + dx, y) * N_HEAD + head, place(z, x, y) * N_HEAD + head)
+            for z in range(NZ)
+            for x in range(NX)
+            for y in range(NY)
+        ]
+    return lax.ppermute(value, ("ctx", "head"), pairs)
+
+
+def gather_rest(own, side):
+    return (own, from_neighbour(own, 1, 0), from_neighbour(own, -1, 0), from_neighbour(own, side, 1))
 
 
 def row_order(plan, z, x, rows):
@@ -74,12 +77,8 @@
     step = jnp.where(piece < 2, piece, 5 - piece)
     colour = (colour_of(plan, z, x) + step) % 4
     member, inner = rest // (NY * rows), rest % (NY * rows)
-    if plan == 0:
-        mz = member
-        mx = (colour - 2 * mz) % 4
-    else:
-        mx = member // 2
-        mz = (colour - 2 * mx) % 4 + 4 * (member % 2)
+    mz = jnp.where(plan == 0, member, (colour - 2 * (member // 2)) % 4 + 4 * (member % 2))
+    mx = jnp.where(plan == 0, (colour - 2 * member) % 4, member // 2)
     return (mz * NX + mx) * (NY * rows) + inner
 
 
@@ -281,11 +280,13 @@
     lanes = 2
     lane_cols = all_cols // lanes
 
+    parts = [slice(lane * lane_cols, (lane + 1) * lane_cols) for lane in range(lanes)]
+    shard = jnp.concatenate([w[:, cols] for cols in parts for w in (w_uk, w_uv)], 1)
+    own_rows = gather_own(shard)
     pieces = []
     for lane in range(lanes):
-        cols = slice(lane * lane_cols, (lane + 1) * lane_cols)
-        shard = jnp.concatenate([w_uk[:, cols], w_uv[:, cols]], 1)
-        pieces.append(gather_pieces(lane, shard))
+        cols = slice(2 * lane * lane_cols, 2 * (lane + 1) * lane_cols)
+        pieces.append(gather_rest(own_rows[:, cols], 1 - 2 * (lane % 2)))
 
     own_pair = blocks[ctx_index]
     own_pos = shard_positions(own_pair, head_index * quarter, quarter, tok_len)
@@ -304,11 +305,9 @@
     depth = latent.shape[1]
     lat_all, rot_all = both[:, :depth], both[:, depth:]
 
-    lats = []
-    for lane in range(lanes):
-        order = row_order(lane, z, x, w_rows)
-        place_of = lax.broadcasted_iota(jnp.int32, (depth, depth), 0) == order[None, :]
-        lats.append(jnp.dot(lat_all, place_of.astype(jnp.bfloat16)))
+    order = row_order(plan_of(head_index), z, x, w_rows)
+    place_of = lax.broadcasted_iota(jnp.int32, (depth, depth), 0) == order[None, :]
+    lat_all = jnp.dot(lat_all, place_of.astype(jnp.bfloat16))
 
     query_pos = shard_positions(own_pair, 0, tok_len, tok_len)
     q_rot = rotate_queries(q_rope, angles_of(query_pos, ROPE))
@@ -321,7 +320,7 @@
     result = None
     for lane in range(lanes):
         result = attend(
-            lane, lanes, sel, lats[lane], rot_all, q_nope, q_rot, pieces[lane], result
+            lane, lanes, sel, lat_all, rot_all, q_nope, q_rot, pieces[lane], result
         )
     return result
 

time: 125 us -> 108 us (0.86)
  the two profiles are of different devices: /device:TPU:6 before, /device:TPU:1 now
where the time goes in v2:
time: 108 us
  starting transfers between devices  46.1 us (43%)
  waiting for transfers between devices  24.2 us (22%)
  Pallas kernels  19.2 us (18%)
  local copies, waits for them, and re-layouts  5.91 us (5%)
  other arithmetic  4.58 us (4%)
  blocking collectives  4.05 us (4%)
  between operations  3 us (3%)
    ppermute x6, starting transfers between devices, from_neighbour(): return lax.ppermute(value, ('ctx', 'head'), pairs)  19.5 us
    all_to_all x1, waiting for transfers between devices, gather_own(): lax.all_to_all(jnp.broadcast_to(shard[None], (size,) + shard.shape), ('ct...  18.9 us
    all_to_all x1, starting transfers between devices, gather_own(): lax.all_to_all(jnp.broadcast_to(shard[None], (size,) + shard.shape), ('ct...  16.9 us
    pallas_call x2, Pallas kernels, attend(): pl.pallas_call(functools.partial(attend_kernel, width, len(pieces)), grid...  15.9 us
    ppermute x2, waiting for transfers between devices, local(): visited.append(lax.ppermute(two, 'ctx', pairs))  5.27 us
    ppermute x2, starting transfers between devices, local(): visited.append(lax.ppermute(two, 'ctx', pairs))  4.92 us
    ppermute x1, starting transfers between devices, local(): across = lax.ppermute(own, 'head', [(0, 2), (2, 0), (1, 3), (3, 1)])  4.76 us
    all_gather x1, blocking collectives, local(): lax.all_gather(held, 'head', axis=0, axis_index_groups=[[0, 1], [2, 3]])  4.05 us
  transfers between devices with their start and end apart: 10, of which 2 were waited for; matrix products, arithmetic and copies ran while one was open for 7% of the time, Pallas kernels for 10%

profile of v2, /device:TPU:1, one launch (start us, length us, event | category | flops | bytes accessed | tf_op | source)
XLA Modules:
  0.0 107.6 jit_solution(6334790827040849726)
XLA Ops:
  0.0 0.8 fusion.41
  0.8 1.4 %broadcast_in_dim.31 = bf16[32,4,4096]{2,1,0:T(4,128)(2,1)} broadcast(bf16[4,4096]{1,0:T(4,128)(2,1)S(1)} %pad_maximum_fusion.4), dimensions={1,2} | broadcast | bytes 1081344 | tf_op jit(solution)/shard_map/broadcast_in_dim | solution.py:47
  2.2 0.0 copy-start.3
  2.2 16.9 %all-to-all-start = ((bf16[32,4,4096]{2,1,0:T(4,128)(2,1)}), bf16[32,4,4096]{2,1,0:T(4,128)(2,1)S(1)}, u32[]{:S(2)}, u32[]{:S(2)}) async-start(bf16[32,4,4096]{2,1,0:T(4,128)(2,1)} %broadcast_in_dim.31), calls=%async_computation | async-start | bytes 2097152 | tf_op jit(solution)/shard_map/all_to_all | solution.py:46
  19.1 0.0 copy-done.3
  19.1 0.1 copy.11
  19.2 0.0 copy-start.4
  19.2 0.0 copy-start.2
  19.3 0.6 copy-done.4
  19.9 0.1 constant_dynamic-slice_fusion.1
  20.0 0.6 fusion.43
  20.6 1.3 %fusion.38 = f32[64]{0:T(128)S(1)} fusion(s32[]{:T(128)} %bitcast.5, s32[]{:T(128)} %bitcast.1, s32[]{:T(128)S(6)} %mul.107), kind=kLoop, calls=%fused_computation.87 | loop fusion | flops 1088 | bytes 268 | tf_op jit(solution)/shard_map/convert_element_type | solution.py:88
  21.9 0.1 fusion.11
  22.0 0.1 copy.13
  22.1 0.1 copy.12
  22.2 0.0 copy-done.2
  22.3 0.1 concatenate.15
  22.4 4.8 %collective-permute-start = (bf16[64,640]{1,0:T(8,128)(2,1)S(1)}, bf16[64,640]{1,0:T(8,128)(2,1)S(1)}, u32[]{:S(2)}, u32[]{:S(2)}) collective-permute-start(bf16[64,640]{1,0:T(8,128)(2,1)S(1)} %concatenate.15), channel_id=1, source_target_pairs={{0,2},{2,0},{1,3},{3,1},{4,6},{6,4},{5,7},{7,5},{8,10},{10,8},{9,1... | collective-permute-start | bytes 245768 | tf_op jit(solution)/shard_map/ppermute | solution.py:295
  27.2 0.7 constant_dynamic-slice_fusion.2
  30.5 1.3 %fusion.34 = f32[256]{0:T(256)S(1)} fusion(s32[]{:T(128)} %bitcast.5, s32[]{:T(128)} %bitcast.1), kind=kLoop, calls=%fused_computation.80 | loop fusion | flops 2816 | bytes 1032 | tf_op jit(solution)/shard_map/convert_element_type | solution.py:88
  31.8 0.5 fusion.3
  32.3 1.0 pad_maximum_fusion.2
  33.3 18.9 %all-to-all-done = bf16[32,4,4096]{2,1,0:T(4,128)(2,1)S(1)} async-done(((bf16[32,4,4096]{2,1,0:T(4,128)(2,1)}), bf16[32,4,4096]{2,1,0:T(4,128)(2,1)S(1)}, u32[]{:S(2)}, u32[]{:S(2)}) %all-to-all-start) | async-done | bytes 1048608 | tf_op jit(solution)/shard_map/all_to_all | solution.py:46
  52.2 0.3 reshape.175
  52.5 0.1 fusion.40
  52.6 4.6 %collective-permute-start.8 = (bf16[128,2048]{1,0:T(8,128)(2,1)S(1)}, bf16[128,2048]{1,0:T(8,128)(2,1)S(1)}, u32[]{:S(2)}, u32[]{:S(2)}) collective-permute-start(bf16[128,2048]{1,0:T(8,128)(2,1)S(1)} %get-tuple-element.5.refs_0_.refs_4_), channel_id=1, source_target_pairs={{64,0},{68,4},{72,8},{76,12},{80,16},{84,20},{88,24},{92,28},{96,3... | collective-permute-start | bytes 1572872 | tf_op jit(solution)/shard_map/ppermute | solution.py:66
  57.2 0.0 collective-permute-done
  57.3 1.9 %collective-permute-start.1 = (bf16[2,64,640]{2,1,0:T(8,128)(2,1)S(1)}, bf16[2,64,640]{2,1,0:T(8,128)(2,1)S(1)}, u32[]{:S(2)}, u32[]{:S(2)}) collective-permute-start(bf16[2,64,640]{2,1,0:T(8,128)(2,1)S(1)} %get-tuple-element.8), channel_id=1, source_target_pairs={{0,4},{4,8},{8,12},{12,16},{16,20},{20,24},{24,28},{28,32},{32,36}... | collective-permute-start | bytes 491528 | tf_op jit(solution)/shard_map/ppermute | solution.py:301
  59.2 3.0 %collective-permute-start.2 = (bf16[2,64,640]{2,1,0:T(8,128)(2,1)S(1)}, bf16[2,64,640]{2,1,0:T(8,128)(2,1)S(1)}, u32[]{:S(2)}, u32[]{:S(2)}) collective-permute-start(bf16[2,64,640]{2,1,0:T(8,128)(2,1)S(1)} %get-tuple-element.8), channel_id=1, source_target_pairs={{0,8},{4,12},{8,16},{12,20},{16,24},{20,28},{24,32},{28,36},{32,40... | collective-permute-start | bytes 491528 | tf_op jit(solution)/shard_map/ppermute | solution.py:301
  62.2 0.1 add_convert_fusion.sel_ref
  62.3 3.3 %rotate_queries.1.qr_ref = bf16[256,2048]{1,0:T(8,128)(2,1)} custom-call(bf16[256,1024]{1,0:T(8,128)(2,1)} %x_ref.1, f32[256,128]{1,0:T(8,128)} %get-tuple-element.24.cos_ref, f32[256,128]{1,0:T(8,128)} %get-tuple-element.25.sin_ref), custom_call_target="tpu_custom_call" | custom-call | flops 1048576 | bytes 1572864 | tf_op jit(solution)/shard_map/rotate_queries/pallas_call | solution.py:133
  65.6 2.1 %collective-permute-start.7 = (bf16[128,2048]{1,0:T(8,128)(2,1)S(1)}, bf16[128,2048]{1,0:T(8,128)(2,1)S(1)}, u32[]{:S(2)}, u32[]{:S(2)}) collective-permute-start(bf16[128,2048]{1,0:T(8,128)(2,1)S(1)} %get-tuple-element.5.refs_0_.refs_4_), channel_id=1, source_target_pairs={{48,0},{52,4},{56,8},{60,12},{0,16},{4,20},{8,24},{12,28},{16,32},... | collective-permute-start | bytes 1572872 | tf_op jit(solution)/shard_map/ppermute | solution.py:66
  67.7 4.4 %collective-permute-start.6 = (bf16[128,2048]{1,0:T(8,128)(2,1)S(1)}, bf16[128,2048]{1,0:T(8,128)(2,1)S(1)}, u32[]{:S(2)}, u32[]{:S(2)}) collective-permute-start(bf16[128,2048]{1,0:T(8,128)(2,1)S(1)} %get-tuple-element.5.refs_0_.refs_4_), channel_id=1, source_target_pairs={{16,0},{20,4},{24,8},{28,12},{32,16},{36,20},{40,24},{44,28},{48,3... | collective-permute-start | bytes 1572872 | tf_op jit(solution)/shard_map/ppermute | solution.py:66
  72.2 0.0 collective-permute-done.1
  72.2 5.3 %collective-permute-done.2 = bf16[2,64,640]{2,1,0:T(8,128)(2,1)S(1)} collective-permute-done((bf16[2,64,640]{2,1,0:T(8,128)(2,1)S(1)}, bf16[2,64,640]{2,1,0:T(8,128)(2,1)S(1)}, u32[]{:S(2)}, u32[]{:S(2)}) %collective-permute-start.2) | collective-permute-done | bytes 163872 | tf_op jit(solution)/shard_map/ppermute | solution.py:301
  77.4 0.1 pad_maximum_fusion
  77.5 1.9 %collective-permute-start.5 = (bf16[128,2048]{1,0:T(8,128)(2,1)S(1)}, bf16[128,2048]{1,0:T(8,128)(2,1)S(1)}, u32[]{:S(2)}, u32[]{:S(2)}) collective-permute-start(bf16[128,2048]{1,0:T(8,128)(2,1)S(1)} %get-tuple-element.6.refs_0_.refs_4_), channel_id=1, source_target_pairs={{448,0},{452,4},{456,8},{460,12},{464,16},{468,20},{472,24},{476,2... | collective-permute-start | bytes 1572872 | tf_op jit(solution)/shard_map/ppermute | solution.py:66
  79.4 2.4 %collective-permute-start.4 = (bf16[128,2048]{1,0:T(8,128)(2,1)S(1)}, bf16[128,2048]{1,0:T(8,128)(2,1)S(1)}, u32[]{:S(2)}, u32[]{:S(2)}) collective-permute-start(bf16[128,2048]{1,0:T(8,128)(2,1)S(1)} %get-tuple-element.6.refs_0_.refs_4_), channel_id=1, source_target_pairs={{48,0},{52,4},{56,8},{60,12},{0,16},{4,20},{8,24},{12,28},{16,32},... | collective-permute-start | bytes 1572872 | tf_op jit(solution)/shard_map/ppermute | solution.py:66
  81.8 0.0 collective-permute-done.8.refs_3_.refs_7_
  81.8 4.1 %collective-permute-start.3 = (bf16[128,2048]{1,0:T(8,128)(2,1)S(1)}, bf16[128,2048]{1,0:T(8,128)(2,1)S(1)}, u32[]{:S(2)}, u32[]{:S(2)}) collective-permute-start(bf16[128,2048]{1,0:T(8,128)(2,1)S(1)} %get-tuple-element.6.refs_0_.refs_4_), channel_id=1, source_target_pairs={{16,0},{20,4},{24,8},{28,12},{32,16},{36,20},{40,24},{44,28},{48,3... | collective-permute-start | bytes 1572872 | tf_op jit(solution)/shard_map/ppermute | solution.py:66
  86.0 4.0 %all-gather = bf16[6,2,64,640]{3,2,1,0:T(8,128)(2,1)S(1)} all-gather(bf16[3,2,64,640]{3,2,1,0:T(8,128)(2,1)S(1)} %pad_maximum_fusion), channel_id=2, replica_groups={{0,1},{2,3},{4,5},{6,7},{8,9},{10,11},{12,13},{14,15},{16,17},{18,19},{..., dimensions={0}, use_global_device_ids=true | all-gather | bytes 1474560 | tf_op jit(solution)/shard_map/all_gather | solution.py:303
  90.0 0.1 copy.16
  90.1 0.0 copy-start
  90.1 0.0 copy-start.1
  90.1 0.6 fusion.lat_ref
  90.8 0.0 collective-permute-done.7.refs_2_.refs_6_
  90.8 0.0 collective-permute-done.6.refs_1_.refs_5_
  90.8 0.6 copy-done
  91.3 0.3 copy-done.1
  91.7 7.9 %attend_0.1.refs_8_ = bf16[256,2048]{1,0:T(8,128)(2,1)} custom-call(s32[2]{0:T(128)S(1)} %add_convert_fusion.sel_ref, bf16[768,512]{1,0:T(8,128)(2,1)S(1)} %fusion.lat_ref, bf16[768,128]{1,0:T(8,128)(2,1)S(1)} %slice.57.rot_ref, bf16[256,2048]{1,0:T(8,128)(2,1)S(1)} %copy-done.1, bf16[256,2048]{1,0:T(8,128)(2,1)S(1)} %copy-done, ...), custom_call_target="tpu_custom_call" | custom-call | flops 2315255808 | bytes 6750208 | tf_op jit(solution)/shard_map/attend_0/pallas_call | solution.py:251
  99.6 0.0 collective-permute-done.5.refs_3_.refs_7_
  99.6 0.0 collective-permute-done.4.refs_2_.refs_6_
  99.6 0.0 collective-permute-done.3.refs_1_.refs_5_
  99.6 8.0 %attend_1.1 = bf16[256,2048]{1,0:T(8,128)(2,1)} custom-call(s32[2]{0:T(128)S(1)} %add_convert_fusion.sel_ref, bf16[768,512]{1,0:T(8,128)(2,1)S(1)} %fusion.lat_ref, bf16[768,128]{1,0:T(8,128)(2,1)S(1)} %slice.57.rot_ref, bf16[256,2048]{1,0:T(8,128)(2,1)S(1)} %copy-done.1, bf16[256,2048]{1,0:T(8,128)(2,1)S(1)} %copy-done, ...), custom_call_target="tpu_custom_call", output_to_operand_aliasing={{}: (13, {})} | custom-call | flops 2315255808 | bytes 6750208 | tf_op jit(solution)/shard_map/attend_1/pallas_call | solution.py:251
  (7 shorter events, 0.1 us)
Async XLA Ops:
  2.2 16.9 %copy-start.3 = (bf16[64,64]{1,0:T(8,128)(2,1)S(1)}, bf16[64,64]{1,0:T(8,128)(2,1)}, u32[]{:S(2)}) copy-start(bf16[64,64]{1,0:T(8,128)(2,1)} %param.10) | copy-start | bytes 24580
  2.2 50.0 %all-to-all-start = ((bf16[32,4,4096]{2,1,0:T(4,128)(2,1)}), bf16[32,4,4096]{2,1,0:T(4,128)(2,1)S(1)}, u32[]{:S(2)}, u32[]{:S(2)}) async-start(bf16[32,4,4096]{2,1,0:T(4,128)(2,1)} %broadcast_in_dim.31), calls=%async_computation | async-start | bytes 2097152 | tf_op jit(solution)/shard_map/all_to_all | solution.py:46
  19.2 0.7 copy-start.4
  19.2 3.0 %copy-start.2 = (bf16[64,512]{1,0:T(8,128)(2,1)S(1)}, bf16[64,512]{1,0:T(8,128)(2,1)}, u32[]{:S(2)}) copy-start(bf16[64,512]{1,0:T(8,128)(2,1)} %param.9) | copy-start | bytes 196612
  22.4 34.8 %collective-permute-start = (bf16[64,640]{1,0:T(8,128)(2,1)S(1)}, bf16[64,640]{1,0:T(8,128)(2,1)S(1)}, u32[]{:S(2)}, u32[]{:S(2)}) collective-permute-start(bf16[64,640]{1,0:T(8,128)(2,1)S(1)} %concatenate.15), channel_id=1, source_target_pairs={{0,2},{2,0},{1,3},{3,1},{4,6},{6,4},{5,7},{7,5},{8,10},{10,8},{9,1... | collective-permute-start | bytes 245768 | tf_op jit(solution)/shard_map/ppermute | solution.py:295
  52.6 29.3 %collective-permute-start.8 = (bf16[128,2048]{1,0:T(8,128)(2,1)S(1)}, bf16[128,2048]{1,0:T(8,128)(2,1)S(1)}, u32[]{:S(2)}, u32[]{:S(2)}) collective-permute-start(bf16[128,2048]{1,0:T(8,128)(2,1)S(1)} %get-tuple-element.5.refs_0_.refs_4_), channel_id=1, source_target_pairs={{64,0},{68,4},{72,8},{76,12},{80,16},{84,20},{88,24},{92,28},{96,3... | collective-permute-start | bytes 1572872 | tf_op jit(solution)/shard_map/ppermute | solution.py:66
  57.3 14.9 %collective-permute-start.1 = (bf16[2,64,640]{2,1,0:T(8,128)(2,1)S(1)}, bf16[2,64,640]{2,1,0:T(8,128)(2,1)S(1)}, u32[]{:S(2)}, u32[]{:S(2)}) collective-permute-start(bf16[2,64,640]{2,1,0:T(8,128)(2,1)S(1)} %get-tuple-element.8), channel_id=1, source_target_pairs={{0,4},{4,8},{8,12},{12,16},{16,20},{20,24},{24,28},{28,32},{32,36}... | collective-permute-start | bytes 491528 | tf_op jit(solution)/shard_map/ppermute | solution.py:301
  59.2 18.2 %collective-permute-start.2 = (bf16[2,64,640]{2,1,0:T(8,128)(2,1)S(1)}, bf16[2,64,640]{2,1,0:T(8,128)(2,1)S(1)}, u32[]{:S(2)}, u32[]{:S(2)}) collective-permute-start(bf16[2,64,640]{2,1,0:T(8,128)(2,1)S(1)} %get-tuple-element.8), channel_id=1, source_target_pairs={{0,8},{4,12},{8,16},{12,20},{16,24},{20,28},{24,32},{28,36},{32,40... | collective-permute-start | bytes 491528 | tf_op jit(solution)/shard_map/ppermute | solution.py:301
  65.6 25.1 %collective-permute-start.7 = (bf16[128,2048]{1,0:T(8,128)(2,1)S(1)}, bf16[128,2048]{1,0:T(8,128)(2,1)S(1)}, u32[]{:S(2)}, u32[]{:S(2)}) collective-permute-start(bf16[128,2048]{1,0:T(8,128)(2,1)S(1)} %get-tuple-element.5.refs_0_.refs_4_), channel_id=1, source_target_pairs={{48,0},{52,4},{56,8},{60,12},{0,16},{4,20},{8,24},{12,28},{16,32},... | collective-permute-start | bytes 1572872 | tf_op jit(solution)/shard_map/ppermute | solution.py:66
  67.7 23.0 %collective-permute-start.6 = (bf16[128,2048]{1,0:T(8,128)(2,1)S(1)}, bf16[128,2048]{1,0:T(8,128)(2,1)S(1)}, u32[]{:S(2)}, u32[]{:S(2)}) collective-permute-start(bf16[128,2048]{1,0:T(8,128)(2,1)S(1)} %get-tuple-element.5.refs_0_.refs_4_), channel_id=1, source_target_pairs={{16,0},{20,4},{24,8},{28,12},{32,16},{36,20},{40,24},{44,28},{48,3... | collective-permute-start | bytes 1572872 | tf_op jit(solution)/shard_map/ppermute | solution.py:66
  77.5 22.1 %collective-permute-start.5 = (bf16[128,2048]{1,0:T(8,128)(2,1)S(1)}, bf16[128,2048]{1,0:T(8,128)(2,1)S(1)}, u32[]{:S(2)}, u32[]{:S(2)}) collective-permute-start(bf16[128,2048]{1,0:T(8,128)(2,1)S(1)} %get-tuple-element.6.refs_0_.refs_4_), channel_id=1, source_target_pairs={{448,0},{452,4},{456,8},{460,12},{464,16},{468,20},{472,24},{476,2... | collective-permute-start | bytes 1572872 | tf_op jit(solution)/shard_map/ppermute | solution.py:66
  79.4 20.1 %collective-permute-start.4 = (bf16[128,2048]{1,0:T(8,128)(2,1)S(1)}, bf16[128,2048]{1,0:T(8,128)(2,1)S(1)}, u32[]{:S(2)}, u32[]{:S(2)}) collective-permute-start(bf16[128,2048]{1,0:T(8,128)(2,1)S(1)} %get-tuple-element.6.refs_0_.refs_4_), channel_id=1, source_target_pairs={{48,0},{52,4},{56,8},{60,12},{0,16},{4,20},{8,24},{12,28},{16,32},... | collective-permute-start | bytes 1572872 | tf_op jit(solution)/shard_map/ppermute | solution.py:66
  81.8 17.8 %collective-permute-start.3 = (bf16[128,2048]{1,0:T(8,128)(2,1)S(1)}, bf16[128,2048]{1,0:T(8,128)(2,1)S(1)}, u32[]{:S(2)}, u32[]{:S(2)}) collective-permute-start(bf16[128,2048]{1,0:T(8,128)(2,1)S(1)} %get-tuple-element.6.refs_0_.refs_4_), channel_id=1, source_target_pairs={{16,0},{20,4},{24,8},{28,12},{32,16},{36,20},{40,24},{44,28},{48,3... | collective-permute-start | bytes 1572872 | tf_op jit(solution)/shard_map/ppermute | solution.py:66
  90.1 1.2 %copy-start = (bf16[256,2048]{1,0:T(8,128)(2,1)S(1)}, bf16[256,2048]{1,0:T(8,128)(2,1)}, u32[]{:S(2)}) copy-start(bf16[256,2048]{1,0:T(8,128)(2,1)} %rotate_queries.1.qr_ref) | copy-start | bytes 3145732
  90.1 1.5 %copy-start.1 = (bf16[256,2048]{1,0:T(8,128)(2,1)S(1)}, bf16[256,2048]{1,0:T(8,128)(2,1)}, u32[]{:S(2)}) copy-start(bf16[256,2048]{1,0:T(8,128)(2,1)} %qn_ref.3) | copy-start | bytes 3145732

commit v3 on v2

--- a/solution.py
+++ b/solution.py
@@ -52,30 +52,30 @@
     ).reshape(size * shard.shape[0], shard.shape[1])
 
 
-def from_neighbour(value, step, along):
-    pairs = []
+def gather_rest(own):
+    groups = []
     for head in range(N_HEAD):
-        on_x = (plan_of(head) == 0) == (along == 0)
-        dz, dx = (0, step) if on_x else (step, 0)
-        pairs += [
-            (place(z + dz, x + dx, y) * N_HEAD + head, place(z, x, y) * N_HEAD + head)
-            for z in range(NZ)
-            for x in range(NX)
-            for y in range(NY)
-        ]
-    return lax.ppermute(value, ("ctx", "head"), pairs)
-
-
-def gather_rest(own, side):
-    return (own, from_neighbour(own, 1, 0), from_neighbour(own, -1, 0), from_neighbour(own, side, 1))
+        shift = plan_of(head)
+        for z in range(shift, NZ, 2):
+            for x in range(shift, NX, 2):
+                for y in range(NY):
+                    block = [place(z + dz, x + dx, y) for dz in range(2) for dx in range(2)]
+                    groups.append([at * N_HEAD + head for at in block])
+    return lax.all_to_all(
+        jnp.broadcast_to(own[None], (4,) + own.shape),
+        ("ctx", "head"),
+        0,
+        0,
+        axis_index_groups=groups,
+    )
 
 
 def row_order(plan, z, x, rows):
     at = jnp.arange(NZ * NX * NY * rows, dtype=jnp.int32)
     quarter = at.shape[0] // 4
     piece, rest = at // quarter, at % quarter
-    step = jnp.where(piece < 2, piece, 5 - piece)
-    colour = (colour_of(plan, z, x) + step) % 4
+    corner_z, corner_x = z - (z + plan) % 2, x - (x + plan) % 2
+    colour = colour_of(plan, corner_z + piece // 2 + NZ, corner_x + piece % 2 + NX)
     member, inner = rest // (NY * rows), rest % (NY * rows)
     mz = jnp.where(plan == 0, member, (colour - 2 * (member // 2)) % 4 + 4 * (member % 2))
     mx = jnp.where(plan == 0, (colour - 2 * member) % 4, member // 2)
@@ -140,12 +140,11 @@
     )(q_rope, cos4, sin4)
 
 
-def attend_kernel(width, pieces, sel_ref, lat_ref, rot_ref, qn_ref, qr_ref, *refs):
-    k_refs, v_refs = refs[:pieces], refs[pieces : 2 * pieces]
+def attend_kernel(width, sel_ref, lat_ref, rot_ref, qn_ref, qr_ref, k_ref, v_ref, *refs):
     o_ref, key_s, val_s = refs[-3:]
     lat = lat_ref[...]
-    up_k = jnp.concatenate([r[...] for r in k_refs], 0)
-    up_v = jnp.concatenate([r[...] for r in v_refs], 0)
+    up_k = k_ref[...].reshape(lat.shape[1], k_ref.shape[2])
+    up_v = v_ref[...].reshape(lat.shape[1], v_ref.shape[2])
     key_s[...] = jnp.dot(lat, up_k, preferred_element_type=jnp.float32).astype(jnp.bfloat16)
     val_s[...] = jnp.dot(lat, up_v, preferred_element_type=jnp.float32).astype(jnp.bfloat16)
     coef = LOG2E / (NOPE + ROPE) ** 0.5
@@ -217,19 +216,18 @@
         o_ref[HALF:, cols] = (out_late / sum_late).astype(jnp.bfloat16)
 
 
-def attend(lane, lanes, sel, lat, rot, q_nope, q_rot, pieces, earlier):
+def attend(first, heads, sel, lat, rot, q_nope, q_rot, weights, earlier):
     tok_len, all_cols = q_nope.shape
-    lane_cols = all_cols // lanes
-    width = 2
+    width = 4
     cols = width * NOPE
-    steps = lane_cols // cols
+    steps = heads // width
     count, depth = lat.shape
 
     def whole(shape):
         return pl.BlockSpec(shape, lambda i: (0, 0))
 
     def mine(shape):
-        return pl.BlockSpec(shape, lambda i: (0, lane * steps + i))
+        return pl.BlockSpec(shape, lambda i: (0, first // width + i))
 
     in_specs = [
         pl.BlockSpec(memory_space=pltpu.SMEM),
@@ -238,18 +236,18 @@
         mine((tok_len, cols)),
         mine((tok_len, cols)),
     ]
-    in_specs += [pl.BlockSpec((p.shape[0], cols), lambda i: (0, i)) for p in pieces]
-    in_specs += [pl.BlockSpec((p.shape[0], cols), lambda i: (0, steps + i)) for p in pieces]
-    operands = [sel, lat, rot, q_nope, q_rot, *pieces, *pieces]
+    in_specs.append(pl.BlockSpec(weights.shape[:2] + (cols,), lambda i: (0, 0, i)))
+    in_specs.append(pl.BlockSpec(weights.shape[:2] + (cols,), lambda i: (0, 0, steps + i)))
+    operands = [sel, lat, rot, q_nope, q_rot, weights, weights]
     aliases = {}
     if earlier is not None:
         in_specs.append(pl.BlockSpec(memory_space=pl.ANY))
         aliases = {len(operands): 0}
         operands.append(earlier)
-    heads = lane_cols // NOPE
+    lane_cols = heads * NOPE
     flops = 4 * count * depth * lane_cols + heads * 7 * HALF * HALF * (2 * 256 + 2 * VDIM)
     return pl.pallas_call(
-        functools.partial(attend_kernel, width, len(pieces)),
+        functools.partial(attend_kernel, width),
         grid=(steps,),
         in_specs=in_specs,
         out_specs=mine((tok_len, cols)),
@@ -265,7 +263,7 @@
             bytes_accessed=2 * (4 * depth * lane_cols + 3 * tok_len * lane_cols + count * 640),
             transcendentals=heads * 7 * HALF * HALF,
         ),
-        name=f"attend_{lane}",
+        name=f"attend_{first}",
     )(*operands)
 
 
@@ -277,31 +275,28 @@
     ctx_index = lax.axis_index("ctx")
     head_index = lax.axis_index("head")
     z, x = ctx_index // (NX * NY), (ctx_index // NY) % NX
-    lanes = 2
-    lane_cols = all_cols // lanes
-
-    parts = [slice(lane * lane_cols, (lane + 1) * lane_cols) for lane in range(lanes)]
-    shard = jnp.concatenate([w[:, cols] for cols in parts for w in (w_uk, w_uv)], 1)
+    heads = all_cols // NOPE
+    parts = [(0, 3 * heads // 4), (3 * heads // 4, heads // 4)]
+
+    shard = jnp.concatenate(
+        [w[:, f * NOPE : (f + n) * NOPE] for f, n in parts for w in (w_uk, w_uv)], 1
+    )
     own_rows = gather_own(shard)
-    pieces = []
-    for lane in range(lanes):
-        cols = slice(2 * lane * lane_cols, 2 * (lane + 1) * lane_cols)
-        pieces.append(gather_rest(own_rows[:, cols], 1 - 2 * (lane % 2)))
 
     own_pair = blocks[ctx_index]
     own_pos = shard_positions(own_pair, head_index * quarter, quarter, tok_len)
     own_rot = rotate(k_rope.astype(jnp.float32), angles_of(own_pos, ROPE)).astype(jnp.bfloat16)
     own = jnp.concatenate([latent, own_rot, own_rot], 1)
-    across = lax.ppermute(own, "head", [(0, 2), (2, 0), (1, 3), (3, 1)])
-    upper = head_index // 2 == 0
-    two = jnp.stack([jnp.where(upper, own, across), jnp.where(upper, across, own)])
-    visited = [two]
+    visited = [own]
     for step in range(1, STEPS):
         pairs = [(source, (source + step) % n_ctx) for source in range(n_ctx)]
-        visited.append(lax.ppermute(two, "ctx", pairs))
+        visited.append(lax.ppermute(own, "ctx", pairs))
     held = jnp.stack(visited)
-    both = lax.all_gather(held, "head", axis=0, axis_index_groups=[[0, 1], [2, 3]])
-    both = both.transpose(2, 1, 0, 3, 4).reshape(STEPS * tok_len, own.shape[1])
+    across = lax.ppermute(held, "head", [(0, 2), (2, 0), (1, 3), (3, 1)])
+    upper = head_index // 2 == 0
+    two = jnp.stack([jnp.where(upper, held, across), jnp.where(upper, across, held)])
+    both = lax.all_gather(two, "head", axis=0, axis_index_groups=[[0, 1], [2, 3]])
+    both = both.transpose(1, 2, 0, 3, 4).reshape(STEPS * tok_len, own.shape[1])
     depth = latent.shape[1]
     lat_all, rot_all = both[:, :depth], both[:, depth:]
 
@@ -317,11 +312,12 @@
             for step in range(1, STEPS)
         ]
     )
+    zero = held[0, 0, 0] * 0 + held[1, 0, 0] * 0 + held[2, 0, 0] * 0 + q_rot[0, 0] * 0
     result = None
-    for lane in range(lanes):
-        result = attend(
-            lane, lanes, sel, lat_all, rot_all, q_nope, q_rot, pieces[lane], result
-        )
+    for first, count in parts:
+        cols = slice(2 * first * NOPE, 2 * (first + count) * NOPE)
+        weights = gather_rest(own_rows[:, cols] + zero)
+        result = attend(first, count, sel, lat_all, rot_all, q_nope, q_rot, weights, result)
     return result
 
 

time: 108 us -> 129 us (1.19)
  the two profiles are of different devices: /device:TPU:1 before, /device:TPU:6 now
where the time goes in v3:
time: 129 us; the launch traced here: 127 us
  waiting for transfers between devices  43.2 us (33%)
  starting transfers between devices  39 us (30%)
  Pallas kernels  17.5 us (14%)
  local copies, waits for them, and re-layouts  14.4 us (11%)
  between operations  5.26 us (4%)
  other arithmetic  4.48 us (3%)
  blocking collectives  2.64 us (2%)
    all_to_all x2, waiting for transfers between devices, gather_rest(): lax.all_to_all(jnp.broadcast_to(own[None], (4,) + own.shape), ('ctx', 'he...  20.2 us
    all_to_all x1, starting transfers between devices, gather_own(): lax.all_to_all(jnp.broadcast_to(shard[None], (size,) + shard.shape), ('ct...  14.6 us
    pallas_call x2, Pallas kernels, attend(): pl.pallas_call(functools.partial(attend_kernel, width), grid=(steps,), in...  14.1 us
    ppermute x2, waiting for transfers between devices, local(): visited.append(lax.ppermute(own, 'ctx', pairs))  11.7 us
    all_to_all x2, starting transfers between devices, gather_rest(): lax.all_to_all(jnp.broadcast_to(own[None], (4,) + own.shape), ('ctx', 'he...  11.4 us
    ppermute x1, waiting for transfers between devices, local(): across = lax.ppermute(held, 'head', [(0, 2), (2, 0), (1, 3), (3, 1)])  11.1 us
    ppermute x2, starting transfers between devices, local(): visited.append(lax.ppermute(own, 'ctx', pairs))  7.97 us
    ppermute x1, starting transfers between devices, local(): across = lax.ppermute(held, 'head', [(0, 2), (2, 0), (1, 3), (3, 1)])  5.04 us
  transfers between devices with their start and end apart: 6, of which 5 were waited for; matrix products, arithmetic and copies ran while one was open for 8% of the time, Pallas kernels for 11%

profile of v3, /device:TPU:6, one launch (start us, length us, event | category | flops | bytes accessed | tf_op | source)
XLA Modules:
  0.0 127.1 jit_solution(16122396807788160737)
XLA Ops:
  0.0 0.0 copy-start.5
  0.0 0.0 copy-start.6
  0.0 0.0 copy-start.4
  0.0 0.8 slice.60
  0.8 0.7 slice.62
  1.5 0.7 slice.61
  2.2 0.7 slice.63
  2.9 1.5 %broadcast_in_dim.43 = bf16[32,4,4096]{2,1,0:T(4,128)(2,1)} broadcast(bf16[4,4096]{1,0:T(4,128)(2,1)S(1)} %pad_maximum_fusion.4), dimensions={1,2} | broadcast | bytes 1081344 | tf_op jit(solution)/shard_map/broadcast_in_dim | solution.py:47
  4.3 14.6 %all-to-all-start = ((bf16[32,4,4096]{2,1,0:T(4,128)(2,1)}), bf16[32,4,4096]{2,1,0:T(4,128)(2,1)S(1)}, u32[]{:S(2)}, u32[]{:S(2)}) async-start(bf16[32,4,4096]{2,1,0:T(4,128)(2,1)} %broadcast_in_dim.43), calls=%async_computation | async-start | bytes 2097152 | tf_op jit(solution)/shard_map/all_to_all | solution.py:46
  18.9 0.0 copy-done.5
  19.0 0.1 copy.11
  19.1 0.0 copy-done.6
  19.1 0.1 constant_dynamic-slice_fusion.1
  19.2 0.5 fusion.47
  19.7 1.2 fusion.46
  20.9 0.1 fusion.11
  21.1 0.1 copy.12
  21.2 0.1 copy.13
  21.3 0.0 copy-done.4
  21.3 0.1 concatenate.15
  21.4 3.7 %collective-permute-start = (bf16[64,640]{1,0:T(8,128)(2,1)S(1)}, bf16[64,640]{1,0:T(8,128)(2,1)S(1)}, u32[]{:S(2)}, u32[]{:S(2)}) collective-permute-start(bf16[64,640]{1,0:T(8,128)(2,1)S(1)} %concatenate.15), channel_id=1, source_target_pairs={{0,4},{4,8},{8,12},{12,16},{16,20},{20,24},{24,28},{28,32},{32,36}... | collective-permute-start | bytes 245768 | tf_op jit(solution)/shard_map/ppermute | solution.py:293
  25.1 4.3 %collective-permute-start.1 = (bf16[64,640]{1,0:T(8,128)(2,1)S(1)}, bf16[64,640]{1,0:T(8,128)(2,1)S(1)}, u32[]{:S(2)}, u32[]{:S(2)}) collective-permute-start(bf16[64,640]{1,0:T(8,128)(2,1)S(1)} %concatenate.15), channel_id=1, source_target_pairs={{0,8},{4,12},{8,16},{12,20},{16,24},{20,28},{24,32},{28,36},{32,40... | collective-permute-start | bytes 245768 | tf_op jit(solution)/shard_map/ppermute | solution.py:293
  29.4 1.2 fusion.42
  30.6 0.5 fusion.3
  31.1 1.0 pad_maximum_fusion.2
  32.1 3.3 %rotate_queries.1.qr_ref = bf16[256,2048]{1,0:T(8,128)(2,1)} custom-call(bf16[256,1024]{1,0:T(8,128)(2,1)} %x_ref.1, f32[256,128]{1,0:T(8,128)} %get-tuple-element.16.cos_ref, f32[256,128]{1,0:T(8,128)} %get-tuple-element.17.sin_ref), custom_call_target="tpu_custom_call" | custom-call | flops 1048576 | bytes 1572864 | tf_op jit(solution)/shard_map/rotate_queries/pallas_call | solution.py:133
  35.4 1.3 slice.78
  36.7 0.5 slice.75
  37.8 4.0 %collective-permute-done = bf16[64,640]{1,0:T(8,128)(2,1)S(1)} collective-permute-done((bf16[64,640]{1,0:T(8,128)(2,1)S(1)}, bf16[64,640]{1,0:T(8,128)(2,1)S(1)}, u32[]{:S(2)}, u32[]{:S(2)}) %collective-permute-start) | collective-permute-done | bytes 81952 | tf_op jit(solution)/shard_map/ppermute | solution.py:293
  41.8 0.6 slice.76
  42.4 7.7 %collective-permute-done.1 = bf16[64,640]{1,0:T(8,128)(2,1)S(1)} collective-permute-done((bf16[64,640]{1,0:T(8,128)(2,1)S(1)}, bf16[64,640]{1,0:T(8,128)(2,1)S(1)}, u32[]{:S(2)}, u32[]{:S(2)}) %collective-permute-start.1) | collective-permute-done | bytes 81952 | tf_op jit(solution)/shard_map/ppermute | solution.py:293
  50.1 0.5 slice.77
  52.5 0.2 all-to-all-done
  52.7 0.3 reshape.218
  53.0 0.1 slice_add_fusion
  53.1 2.1 %broadcast_in_dim.45 = bf16[4,128,3072]{2,1,0:T(8,128)(2,1)} broadcast(bf16[128,3072]{1,0:T(8,128)(2,1)S(1)} %slice_add_fusion), dimensions={1,2} | broadcast | bytes 3932160 | tf_op jit(solution)/shard_map/broadcast_in_dim | solution.py:65
  55.1 6.1 %all-to-all-start.2 = ((bf16[4,128,3072]{2,1,0:T(8,128)(2,1)}), bf16[4,128,3072]{2,1,0:T(8,128)(2,1)}, u32[]{:S(2)}, u32[]{:S(2)}) async-start(bf16[4,128,3072]{2,1,0:T(8,128)(2,1)} %broadcast_in_dim.45), calls=%async_computation.2 | async-start | bytes 6291456 | tf_op jit(solution)/shard_map/all_to_all | solution.py:64
  61.2 20.2 %all-to-all-done.2.k_ref.v_ref = bf16[4,128,3072]{2,1,0:T(8,128)(2,1)} async-done(((bf16[4,128,3072]{2,1,0:T(8,128)(2,1)}), bf16[4,128,3072]{2,1,0:T(8,128)(2,1)}, u32[]{:S(2)}, u32[]{:S(2)}) %all-to-all-start.2) | async-done | bytes 3145760 | tf_op jit(solution)/shard_map/all_to_all | solution.py:64
  81.4 1.1 broadcast_in_dim.44
  82.5 5.4 %all-to-all-start.1 = ((bf16[4,128,1024]{2,1,0:T(8,128)(2,1)}), bf16[4,128,1024]{2,1,0:T(8,128)(2,1)S(1)}, u32[]{:S(2)}, u32[]{:S(2)}) async-start(bf16[4,128,1024]{2,1,0:T(8,128)(2,1)} %broadcast_in_dim.44), calls=%async_computation.1 | async-start | bytes 2097152 | tf_op jit(solution)/shard_map/all_to_all | solution.py:64
  87.9 5.0 %collective-permute-start.2 = (bf16[3,64,640]{2,1,0:T(8,128)(2,1)S(1)}, bf16[3,64,640]{2,1,0:T(8,128)(2,1)S(1)}, u32[]{:S(2)}, u32[]{:S(2)}) collective-permute-start(bf16[3,64,640]{2,1,0:T(8,128)(2,1)S(1)} %pad_maximum_fusion.1), channel_id=1, source_target_pairs={{0,2},{2,0},{1,3},{3,1},{4,6},{6,4},{5,7},{7,5},{8,10},{10,8},{9,1... | collective-permute-start | bytes 737288 | tf_op jit(solution)/shard_map/ppermute | solution.py:295
  93.1 0.7 constant_dynamic-slice_fusion.2
  96.1 0.1 add_convert_fusion.sel_ref
  96.2 11.1 %collective-permute-done.2 = bf16[3,64,640]{2,1,0:T(8,128)(2,1)S(1)} collective-permute-done((bf16[3,64,640]{2,1,0:T(8,128)(2,1)S(1)}, bf16[3,64,640]{2,1,0:T(8,128)(2,1)S(1)}, u32[]{:S(2)}, u32[]{:S(2)}) %collective-permute-start.2) | collective-permute-done | bytes 245792 | tf_op jit(solution)/shard_map/ppermute | solution.py:295
  107.4 0.1 select_bitcast_fusion.1
  107.5 0.1 pad_maximum_fusion
  107.5 0.0 copy-start
  107.5 0.0 copy-start.1
  107.5 2.6 %all-gather = bf16[4,3,64,640]{3,2,1,0:T(8,128)(2,1)S(1)} all-gather(bf16[2,3,64,640]{3,2,1,0:T(8,128)(2,1)S(1)} %pad_maximum_fusion), channel_id=2, replica_groups={{0,1},{2,3},{4,5},{6,7},{8,9},{10,11},{12,13},{14,15},{16,17},{18,19},{..., dimensions={0}, use_global_device_ids=true | all-gather | bytes 1474560 | tf_op jit(solution)/shard_map/all_gather | solution.py:298
  110.2 0.1 copy.16
  110.3 0.6 fusion.lat_ref
  110.9 0.0 copy-done
  110.9 0.0 copy-done.1
  111.0 10.2 %attend_0.1.refs_0_ = bf16[256,2048]{1,0:T(8,128)(2,1)} custom-call(s32[2]{0:T(128)S(1)} %add_convert_fusion.sel_ref, bf16[768,512]{1,0:T(8,128)(2,1)S(1)} %fusion.lat_ref, bf16[768,128]{1,0:T(8,128)(2,1)S(1)} %slice.73.rot_ref, bf16[256,2048]{1,0:T(8,128)(2,1)S(1)} %copy-done.1, bf16[256,2048]{1,0:T(8,128)(2,1)S(1)} %copy-done, ...), custom_call_target="tpu_custom_call" | custom-call | flops 3472883712 | bytes 9633792 | tf_op jit(solution)/shard_map/attend_0/pallas_call | solution.py:249
  121.2 0.0 copy-start.2
  121.2 0.9 copy-done.2
  122.0 0.0 all-to-all-done.1.k_ref.v_ref
  122.0 0.0 copy-start.3
  122.0 1.1 copy-done.3
  123.2 3.9 %attend_12.1 = bf16[256,2048]{1,0:T(8,128)(2,1)} custom-call(s32[2]{0:T(128)S(1)} %add_convert_fusion.sel_ref, bf16[768,512]{1,0:T(8,128)(2,1)S(1)} %copy-done.3, bf16[768,128]{1,0:T(8,128)(2,1)S(1)} %slice.73.rot_ref, bf16[256,2048]{1,0:T(8,128)(2,1)S(1)} %copy-done.1, bf16[256,2048]{1,0:T(8,128)(2,1)S(1)} %copy-done, ...), custom_call_target="tpu_custom_call", output_to_operand_aliasing={{}: (7, {})} | custom-call | flops 1157627904 | bytes 3866624 | tf_op jit(solution)/shard_map/attend_12/pallas_call | solution.py:249
  (7 shorter events, 0.1 us)
Async XLA Ops:
  0.0 18.9 %copy-start.5 = (bf16[64,64]{1,0:T(8,128)(2,1)S(1)}, bf16[64,64]{1,0:T(8,128)(2,1)}, u32[]{:S(2)}) copy-start(bf16[64,64]{1,0:T(8,128)(2,1)} %param.10) | copy-start | bytes 24580
  0.0 19.1 %copy-start.6 = (s32[128,2]{0,1:T(2,128)S(1)}, s32[128,2]{0,1:T(2,128)}, u32[]{:S(2)}) copy-start(s32[128,2]{0,1:T(2,128)} %param.11) | copy-start | bytes 3076
  0.0 21.3 %copy-start.4 = (bf16[64,512]{1,0:T(8,128)(2,1)S(1)}, bf16[64,512]{1,0:T(8,128)(2,1)}, u32[]{:S(2)}) copy-start(bf16[64,512]{1,0:T(8,128)(2,1)} %param.9) | copy-start | bytes 196612
  4.3 48.4 %all-to-all-start = ((bf16[32,4,4096]{2,1,0:T(4,128)(2,1)}), bf16[32,4,4096]{2,1,0:T(4,128)(2,1)S(1)}, u32[]{:S(2)}, u32[]{:S(2)}) async-start(bf16[32,4,4096]{2,1,0:T(4,128)(2,1)} %broadcast_in_dim.43), calls=%async_computation | async-start | bytes 2097152 | tf_op jit(solution)/shard_map/all_to_all | solution.py:46
  21.4 20.5 %collective-permute-start = (bf16[64,640]{1,0:T(8,128)(2,1)S(1)}, bf16[64,640]{1,0:T(8,128)(2,1)S(1)}, u32[]{:S(2)}, u32[]{:S(2)}) collective-permute-start(bf16[64,640]{1,0:T(8,128)(2,1)S(1)} %concatenate.15), channel_id=1, source_target_pairs={{0,4},{4,8},{8,12},{12,16},{16,20},{20,24},{24,28},{28,32},{32,36}... | collective-permute-start | bytes 245768 | tf_op jit(solution)/shard_map/ppermute | solution.py:293
  25.1 25.0 %collective-permute-start.1 = (bf16[64,640]{1,0:T(8,128)(2,1)S(1)}, bf16[64,640]{1,0:T(8,128)(2,1)S(1)}, u32[]{:S(2)}, u32[]{:S(2)}) collective-permute-start(bf16[64,640]{1,0:T(8,128)(2,1)S(1)} %concatenate.15), channel_id=1, source_target_pairs={{0,8},{4,12},{8,16},{12,20},{16,24},{20,28},{24,32},{28,36},{32,40... | collective-permute-start | bytes 245768 | tf_op jit(solution)/shard_map/ppermute | solution.py:293
  55.1 26.3 %all-to-all-start.2 = ((bf16[4,128,3072]{2,1,0:T(8,128)(2,1)}), bf16[4,128,3072]{2,1,0:T(8,128)(2,1)}, u32[]{:S(2)}, u32[]{:S(2)}) async-start(bf16[4,128,3072]{2,1,0:T(8,128)(2,1)} %broadcast_in_dim.45), calls=%async_computation.2 | async-start | bytes 6291456 | tf_op jit(solution)/shard_map/all_to_all | solution.py:64
  82.5 39.5 %all-to-all-start.1 = ((bf16[4,128,1024]{2,1,0:T(8,128)(2,1)}), bf16[4,128,1024]{2,1,0:T(8,128)(2,1)S(1)}, u32[]{:S(2)}, u32[]{:S(2)}) async-start(bf16[4,128,1024]{2,1,0:T(8,128)(2,1)} %broadcast_in_dim.44), calls=%async_computation.1 | async-start | bytes 2097152 | tf_op jit(solution)/shard_map/all_to_all | solution.py:64
  87.9 19.4 %collective-permute-start.2 = (bf16[3,64,640]{2,1,0:T(8,128)(2,1)S(1)}, bf16[3,64,640]{2,1,0:T(8,128)(2,1)S(1)}, u32[]{:S(2)}, u32[]{:S(2)}) collective-permute-start(bf16[3,64,640]{2,1,0:T(8,128)(2,1)S(1)} %pad_maximum_fusion.1), channel_id=1, source_target_pairs={{0,2},{2,0},{1,3},{3,1},{4,6},{6,4},{5,7},{7,5},{8,10},{10,8},{9,1... | collective-permute-start | bytes 737288 | tf_op jit(solution)/shard_map/ppermute | solution.py:295
  107.5 3.4 %copy-start = (bf16[256,2048]{1,0:T(8,128)(2,1)S(1)}, bf16[256,2048]{1,0:T(8,128)(2,1)}, u32[]{:S(2)}) copy-start(bf16[256,2048]{1,0:T(8,128)(2,1)} %rotate_queries.1.qr_ref) | copy-start | bytes 3145732
  107.5 3.4 %copy-start.1 = (bf16[256,2048]{1,0:T(8,128)(2,1)S(1)}, bf16[256,2048]{1,0:T(8,128)(2,1)}, u32[]{:S(2)}) copy-start(bf16[256,2048]{1,0:T(8,128)(2,1)} %qn_ref.3) | copy-start | bytes 3145732
  121.2 0.9 copy-start.2
  122.0 1.1 copy-start.3

commit v4 on v2

v4 whole, which is shorter than its diff:
```python
import functools

import jax
import jax.numpy as jnp
from jax import lax
from jax.experimental import pallas as pl
from jax.experimental.pallas import tpu as pltpu
from jax.sharding import PartitionSpec as P

ROPE = 64
NOPE = 128
VDIM = 128
STEPS = 3
NZ, NX, NY = 8, 4, 4
N_HEAD = 4
HALF = 128
CHUNK = 32
LOG2E = 1.4426950408889634
NEG = -1e30


def place(z, x, y):
    return ((z % NZ) * NX + x % NX) * NY + y


def members(plan, colour):
    if plan == 0:
        return [(z, (colour - 2 * z) % NX) for z in range(NZ)]
    return [((colour - 2 * x) % 4 + 4 * far, x) for x in range(NX) for far in range(2)]


def plan_of(head):
    return head % 2


def colour_of(plan, z, x):
    return jnp.where(plan == 0, x + 2 * z, z + 2 * x) % 4


def gather_own(shard):
    groups = [
        [place(z, x, y) * N_HEAD + head for z, x in members(plan_of(head), c) for y in range(NY)]
        for head in range(N_HEAD)
        for c in range(4)
    ]
    size = len(groups[0])
    return lax.all_to_all(
        jnp.broadcast_to(shard[None], (size,) + shard.shape),
        ("ctx", "head"),
        0,
        0,
        axis_index_groups=groups,
    ).reshape(size * shard.shape[0], shard.shape[1])


def from_neighbour(value, step, along):
    pairs = []
    for head in range(N_HEAD):
        on_x = (plan_of(head) == 0) == (along == 0)
        dz, dx = (0, step) if on_x else (step, 0)
        pairs += [
            (place(z + dz, x + dx, y) * N_HEAD + head, place(z, x, y) * N_HEAD + head)
            for z in range(NZ)
            for x in range(NX)
            for y in range(NY)
        ]
    return lax.ppermute(value, ("ctx", "head"), pairs)


def gather_rest(own):
    mid = own.shape[0] // 2
    return (
        own,
        from_neighbour(own, 1, 0),
        from_neighbour(own, -1, 0),
        from_neighbour(own[:mid], 1, 1),
        from_neighbour(own[mid:], -1, 1),
    )


def row_order(plan, z, x, rows):
    at = jnp.arange(NZ * NX * NY * rows, dtype=jnp.int32)
    quarter = at.shape[0] // 4
    piece, rest = at // quarter, at % quarter
    step = jnp.where(piece < 2, piece, 5 - piece)
    colour = (colour_of(plan, z, x) + step) % 4
    member, inner = rest // (NY * rows), rest % (NY * rows)
    mz = jnp.where(plan == 0, member, (colour - 2 * (member // 2)) % 4 + 4 * (member % 2))
    mx = jnp.where(plan == 0, (colour - 2 * member) % 4, member // 2)
    return (mz * NX + mx) * (NY * rows) + inner


def angles_of(pos, width):
    half = width // 2
    freq = 10000.0 ** (-(2.0 * jnp.arange(half, dtype=jnp.float32)) / width)
    return pos.astype(jnp.float32)[..., None] * freq


def turned(x, cosine, sine):
    lane = lax.broadcasted_iota(jnp.int32, x.shape, 1)
    swapped = jnp.where(lane % 64 < 32, pltpu.roll(x, 96, 1), pltpu.roll(x, 32, 1))
    return x * cosine + swapped * sine


def rotate_queries_kernel(x_ref, cos_ref, sin_ref, o_ref):
    rows = x_ref.shape[0]
    left = lax.broadcasted_iota(jnp.int32, (rows, 128), 1) < 64

    def own(ref):
        return jnp.concatenate([ref[:HALF], ref[STEPS * HALF : (STEPS + 1) * HALF]], 0)

    cosine, sine = own(cos_ref), own(sin_ref)
    for pair in range(x_ref.shape[1] // 128):
        x = turned(x_ref[:, pair * 128 : (pair + 1) * 128].astype(jnp.float32), cosine, sine)
        high = x.astype(jnp.bfloat16).astype(jnp.float32)
        rest = x - high
        first = jnp.where(left, high, pltpu.roll(rest, 64, 1))
        second = jnp.where(left, pltpu.roll(high, 64, 1), rest)
        o_ref[:, pair * 256 : pair * 256 + 128] = first.astype(jnp.bfloat16)
        o_ref[:, pair * 256 + 128 : pair * 256 + 256] = second.astype(jnp.bfloat16)


def rotate_queries(q_rope, cosine, sine):
    tok_len, width = q_rope.shape
    return pl.pallas_call(
        rotate_queries_kernel,
        out_shape=jax.ShapeDtypeStruct((tok_len, 2 * width), jnp.bfloat16),
        cost_estimate=pl.CostEstimate(
            flops=4 * tok_len * width, bytes_accessed=6 * tok_len * width, transcendentals=0
        ),
        name="rotate_queries",
    )(q_rope, cosine, sine)


def prepare_keys_kernel(held_ref, order_ref, cos_ref, sin_ref, lat_ref, rot_ref):
    cores, halves, steps, _, _ = held_ref.shape
    depth = lat_ref.shape[1]
    held = jnp.concatenate(
        [
            held_ref[core, half, step]
            for half in range(halves)
            for step in range(steps)
            for core in range(cores)
        ],
        0,
    )
    at = lax.broadcasted_iota(jnp.int32, (depth, depth), 0)
    place_of = (at == order_ref[...]).astype(jnp.float32).astype(jnp.bfloat16)
    lat = jnp.dot(held[:, :depth], place_of, preferred_element_type=jnp.float32)
    lat_ref[...] = lat.astype(jnp.bfloat16)
    rot = turned(held[:, depth:].astype(jnp.float32), cos_ref[...], sin_ref[...])
    rot_ref[...] = rot.astype(jnp.bfloat16)


def prepare_keys(held, order, cosine, sine):
    depth = order.shape[0]
    count = cosine.shape[0]
    return pl.pallas_call(
        prepare_keys_kernel,
        out_shape=(
            jax.ShapeDtypeStruct((count, depth), jnp.bfloat16),
            jax.ShapeDtypeStruct((count, 128), jnp.bfloat16),
        ),
        cost_estimate=pl.CostEstimate(
            flops=2 * count * depth * depth, bytes_accessed=6 * count * 640, transcendentals=0
        ),
        compiler_params=pltpu.CompilerParams(vmem_limit_bytes=32 * 1024 * 1024),
        name="prepare_keys",
    )(held, order[None, :], cosine, sine)


def attend_kernel(width, sel_ref, lat_ref, rot_ref, qn_ref, qr_ref, *refs):
    o_ref, key_s, val_s, score_s, prob_s, sum_s = refs[-6:]
    lat = lat_ref[...]
    pieces = (len(refs) - 6) // 2
    up_k = jnp.concatenate([r[...] for r in refs[:pieces]], 0)
    up_v = jnp.concatenate([r[...] for r in refs[pieces : 2 * pieces]], 0)
    key_s[...] = jnp.dot(lat, up_k, preferred_element_type=jnp.float32).astype(jnp.bfloat16)
    val_s[...] = jnp.dot(lat, up_v, preferred_element_type=jnp.float32).astype(jnp.bfloat16)
    coef = LOG2E / (NOPE + ROPE) ** 0.5
    contract = (((1,), (1,)), ((), ()))
    early = [sel_ref[j] != 0 for j in range(STEPS - 1)]
    q_at = [pl.multiple_of(jnp.where(e, 0, HALF), HALF) for e in early]
    k_at = [
        pl.multiple_of(jnp.where(e, j + 1, STEPS + j + 1) * HALF, HALF)
        for j, e in enumerate(early)
    ]
    full = (STEPS + 1) * HALF
    chosen_at = [full + (j + 1) * HALF for j in range(STEPS - 1)]

    for h in range(width):
        cols = slice(h * NOPE, (h + 1) * NOPE)

        def scores(at, q_start, k_start, count):
            q_rows, k_rows = pl.ds(q_start, HALF), pl.ds(k_start, count)
            q = jnp.concatenate([qn_ref[q_rows, cols], qr_ref[q_rows, cols]], 1)
            k = jnp.concatenate([key_s[k_rows, cols], rot_ref[k_rows, :]], 1)
            score_s[h, :, at : at + count] = lax.dot_general(
                q, k, contract, preferred_element_type=jnp.float32
            )

        scores(0, HALF, 0, full)
        scores(full, 0, 0, HALF)
        for j in range(STEPS - 1):
            scores(chosen_at[j], q_at[j], k_at[j], HALF)

    for h in range(width):
        cols = slice(h * NOPE, (h + 1) * NOPE)
        for start in range(0, HALF, CHUNK):
            rows = slice(start, start + CHUNK)
            row = lax.broadcasted_iota(jnp.int32, (CHUNK, HALF), 0) + start
            causal = lax.broadcasted_iota(jnp.int32, (CHUNK, HALF), 1) <= row
            late = [score_s[h, rows, i * HALF : (i + 1) * HALF] for i in range(STEPS + 1)]
            late[STEPS] = jnp.where(causal, late[STEPS], NEG)
            first = jnp.where(causal, score_s[h, rows, full : full + HALF], NEG)
            chosen = [score_s[h, rows, at : at + HALF] for at in chosen_at]
            top_late = functools.reduce(jnp.maximum, late)
            top_first = first
            for e, s in zip(early, chosen):
                top_late = jnp.maximum(top_late, jnp.where(e, NEG, s))
                top_first = jnp.maximum(top_first, jnp.where(e, s, NEG))
            top_late = jnp.max(top_late, axis=1, keepdims=True)
            top_first = jnp.max(top_first, axis=1, keepdims=True)
            sum_late = jnp.zeros((CHUNK, HALF), jnp.float32)
            for i, s in enumerate(late):
                p = jnp.exp2((s - top_late) * coef)
                sum_late = sum_late + p
                prob_s[h, rows, i * HALF : (i + 1) * HALF] = p.astype(jnp.bfloat16)
            p = jnp.exp2((first - top_first) * coef)
            sum_first = p
            prob_s[h, rows, full : full + HALF] = p.astype(jnp.bfloat16)
            for e, s, at in zip(early, chosen, chosen_at):
                p = jnp.exp2((s - jnp.where(e, top_first, top_late)) * coef)
                sum_late = sum_late + jnp.where(e, 0.0, p)
                sum_first = sum_first + jnp.where(e, p, 0.0)
                prob_s[h, rows, at : at + HALF] = p.astype(jnp.bfloat16)
            sum_s[h, 0, rows, :] = jnp.sum(sum_late, axis=1, keepdims=True)
            sum_s[h, 1, rows, :] = jnp.sum(sum_first, axis=1, keepdims=True)

        def weighted(at, k_start, count):
            return jnp.dot(
                prob_s[h, :, at : at + count],
                val_s[pl.ds(k_start, count), cols],
                preferred_element_type=jnp.float32,
            )

        out_late = weighted(0, 0, full)
        out_first = weighted(full, 0, HALF)
        for j, e in enumerate(early):
            part = weighted(chosen_at[j], k_at[j], HALF)
            out_late = out_late + jnp.where(e, 0.0, part)
            out_first = out_first + jnp.where(e, part, 0.0)
        o_ref[:HALF, cols] = (out_first / sum_s[h, 1]).astype(jnp.bfloat16)
        o_ref[HALF:, cols] = (out_late / sum_s[h, 0]).astype(jnp.bfloat16)


def attend(sel, lat, rot, q_nope, q_rot, weights):
    tok_len, all_cols = q_nope.shape
    width = 4
    cols = width * NOPE
    heads = all_cols // NOPE
    steps = heads // width
    count, depth = lat.shape
    blocks = 2 * STEPS + 1

    def whole(shape):
        return pl.BlockSpec(shape, lambda i: (0, 0))

    def mine(shape):
        return pl.BlockSpec(shape, lambda i: (0, i))

    in_specs = [
        pl.BlockSpec(memory_space=pltpu.SMEM),
        whole(lat.shape),
        whole(rot.shape),
        mine((tok_len, cols)),
        mine((tok_len, cols)),
    ]
    in_specs += [pl.BlockSpec((w.shape[0], cols), lambda i: (0, i)) for w in weights]
    in_specs += [pl.BlockSpec((w.shape[0], cols), lambda i: (0, steps + i)) for w in weights]
    flops = 4 * count * depth * all_cols + heads * blocks * HALF * HALF * (2 * 256 + 2 * VDIM)
    return pl.pallas_call(
        functools.partial(attend_kernel, width),
        grid=(steps,),
        in_specs=in_specs,
        out_specs=mine((tok_len, cols)),
        out_shape=jax.ShapeDtypeStruct((tok_len, all_cols), jnp.bfloat16),
        scratch_shapes=[
            pltpu.VMEM((count, cols), jnp.bfloat16),
            pltpu.VMEM((count, cols), jnp.bfloat16),
            pltpu.VMEM((width, HALF, blocks * HALF), jnp.float32),
            pltpu.VMEM((width, HALF, blocks * HALF), jnp.bfloat16),
            pltpu.VMEM((width, 2, HALF, 1), jnp.float32),
        ],
        compiler_params=pltpu.CompilerParams(vmem_limit_bytes=40 * 1024 * 1024),
        cost_estimate=pl.CostEstimate(
            flops=flops,
            bytes_accessed=2 * (4 * depth * all_cols + 3 * tok_len * all_cols + count * 640),
            transcendentals=heads * blocks * HALF * HALF,
        ),
        name="attend",
    )(sel, lat, rot, q_nope, q_rot, *weights, *weights)


def local(q_nope, q_rope, latent, k_rope, blocks, w_uk, w_uv):
    w_rows = w_uk.shape[0]
    n_ctx = lax.axis_size("ctx")
    ctx_index = lax.axis_index("ctx")
    head_index = lax.axis_index("head")
    z, x = ctx_index // (NX * NY), (ctx_index // NY) % NX
    own = jnp.concatenate([latent, k_rope, k_rope], 1)
    visited = [own]
    for step in range(1, STEPS):
        pairs = [(source, (source + step) % n_ctx) for source in range(n_ctx)]
        visited.append(lax.ppermute(own, "ctx", pairs))
    held = jnp.stack(visited)

    own_rows = gather_own(jnp.concatenate([w_uk, w_uv], 1))

    shards = [(ctx_index - step) % n_ctx for step in range(STEPS)]
    rows = jnp.arange(HALF, dtype=jnp.int32)
    pos = jnp.concatenate([blocks[c, half] * HALF + rows for half in range(2) for c in shards])
    angles = angles_of(pos, ROPE)
    cosine, sine = jnp.cos(angles), jnp.sin(angles)
    cosine = jnp.concatenate([cosine] * 4, 1)
    sine = jnp.concatenate([-sine, sine, -sine, sine], 1)
    q_rot = rotate_queries(q_rope, cosine, sine)
    sel = jnp.stack([(blocks[c, 0] < blocks[ctx_index, 0]).astype(jnp.int32) for c in shards[1:]])

    zero = held[0, 0, 0] * 0 + held[1, 0, 0] * 0 + held[2, 0, 0] * 0 + q_rot[0, 0] * 0
    weights = gather_rest(own_rows + zero)

    across = lax.ppermute(held, "head", [(0, 2), (2, 0), (1, 3), (3, 1)])
    upper = head_index // 2 == 0
    two = jnp.stack([jnp.where(upper, held, across), jnp.where(upper, across, held)])
    both = lax.all_gather(two, "head", axis=0, axis_index_groups=[[0, 1], [2, 3]])
    order = row_order(plan_of(head_index), z, x, w_rows)
    lat, rot = prepare_keys(both, order, cosine, sine)
    return attend(sel, lat, rot, q_nope, q_rot, weights)


def solution(mesh):
    in_specs = (
        P("ctx", "head"),
        P("ctx", "head"),
        P(("ctx", "head"), None),
        P(("ctx", "head"), None),
        P(),
        P("ctx", "head"),
        P("ctx", "head"),
    )
    out_specs = P("ctx", "head")
    return jax.shard_map(local, mesh=mesh, in_specs=in_specs, out_specs=out_specs, check_vma=False)
```

time: 108 us -> 103 us (0.954)
  the two profiles are of different devices: /device:TPU:1 before, /device:TPU:6 now
where the time goes in v4:
time: 103 us; the launch traced here: 102 us
  starting transfers between devices  44.4 us (43%)
  Pallas kernels  15.1 us (15%)
  local copies, waits for them, and re-layouts  13.7 us (13%)
  waiting for transfers between devices  11.1 us (11%)
  between operations  9.01 us (9%)
  other arithmetic  5.93 us (6%)
  blocking collectives  2.64 us (3%)
    ppermute x4, starting transfers between devices, from_neighbour(): return lax.ppermute(value, ('ctx', 'head'), pairs)  16.7 us
    all_to_all x1, starting transfers between devices, gather_own(): lax.all_to_all(jnp.broadcast_to(shard[None], (size,) + shard.shape), ('ct...  14.7 us
    pallas_call x1, Pallas kernels, attend(): pl.pallas_call(functools.partial(attend_kernel, width), grid=(steps,), in...  11.1 us
    ppermute x2, starting transfers between devices, local(): visited.append(lax.ppermute(own, 'ctx', pairs))  7.96 us
    ppermute x2, waiting for transfers between devices, local(): visited.append(lax.ppermute(own, 'ctx', pairs))  5.89 us
    ppermute x4, waiting for transfers between devices, from_neighbour(): return lax.ppermute(value, ('ctx', 'head'), pairs)  5.17 us
    ppermute x1, starting transfers between devices, local(): across = lax.ppermute(held, 'head', [(0, 2), (2, 0), (1, 3), (3, 1)])  5.04 us
    slice x2, local copies, waits for them, and re-layouts, gather_rest(): own[mid:]  4.78 us
  transfers between devices with their start and end apart: 8, of which 3 were waited for; matrix products, arithmetic and copies ran while one was open for 15% of the time, Pallas kernels for 4%

profile of v4, /device:TPU:6, one launch (start us, length us, event | category | flops | bytes accessed | tf_op | source)
XLA Modules:
  0.0 101.9 jit_solution(7513918216514513915)
XLA Ops:
  0.0 0.8 pad_maximum_fusion.5
  0.8 1.5 %broadcast_in_dim.2 = bf16[32,4,4096]{2,1,0:T(4,128)(2,1)} broadcast(bf16[4,4096]{1,0:T(4,128)(2,1)S(1)} %pad_maximum_fusion.5), dimensions={1,2} | broadcast | bytes 1081344 | tf_op jit(solution)/shard_map/broadcast_in_dim | solution.py:48
  2.2 0.0 copy-start.5
  2.2 0.0 copy-start.6
  2.2 14.7 %all-to-all-start = ((bf16[32,4,4096]{2,1,0:T(4,128)(2,1)}), bf16[32,4,4096]{2,1,0:T(4,128)(2,1)S(1)}, u32[]{:S(2)}, u32[]{:S(2)}) async-start(bf16[32,4,4096]{2,1,0:T(4,128)(2,1)} %broadcast_in_dim.2), calls=%async_computation | async-start | bytes 2097152 | tf_op jit(solution)/shard_map/all_to_all | solution.py:47
  17.0 0.0 copy-done.5
  17.0 0.0 copy-done.6
  17.0 0.1 fusion.8
  17.1 3.7 %collective-permute-start = (bf16[64,640]{1,0:T(8,128)(2,1)S(1)}, bf16[64,640]{1,0:T(8,128)(2,1)S(1)}, u32[]{:S(2)}, u32[]{:S(2)}) collective-permute-start(bf16[64,640]{1,0:T(8,128)(2,1)S(1)} %get-tuple-element.14), channel_id=1, source_target_pairs={{0,4},{4,8},{8,12},{12,16},{16,20},{20,24},{24,28},{28,32},{32,36}... | collective-permute-start | bytes 245768 | tf_op jit(solution)/shard_map/ppermute | solution.py:315
  20.8 4.3 %collective-permute-start.1 = (bf16[64,640]{1,0:T(8,128)(2,1)S(1)}, bf16[64,640]{1,0:T(8,128)(2,1)S(1)}, u32[]{:S(2)}, u32[]{:S(2)}) collective-permute-start(bf16[64,640]{1,0:T(8,128)(2,1)S(1)} %get-tuple-element.14), channel_id=1, source_target_pairs={{0,8},{4,12},{8,16},{12,20},{16,24},{20,28},{24,32},{28,36},{32,40... | collective-permute-start | bytes 245768 | tf_op jit(solution)/shard_map/ppermute | solution.py:315
  25.2 0.0 copy-start.7
  25.2 0.7 copy-done.7
  25.8 0.7 constant_dynamic-slice_fusion.4
  32.7 0.5 slice.32
  33.2 1.5 %fusion = (f32[768,32]{1,0:T(8,128)S(1)}, f32[768,32]{1,0:T(8,128)S(1)}, f32[768,32]{1,0:T(8,128)S(1)}) fusion(f32[32]{0:T(128)S(1)} %multiply_power_fusion, f32[768]{0:T(1024)S(1)} %convert_element_type.11), kind=kLoop, calls=%fused_computation.9 | loop fusion | flops 49152 | bytes 298112 | tf_op jit(solution)/shard_map/neg | solution.py:326
  34.7 1.6 %pad_maximum_fusion.1 = (f32[768,128]{1,0:T(8,128)}, f32[768,128]{1,0:T(8,128)}) fusion(f32[768,32]{1,0:T(8,128)S(1)} %get-tuple-element.17, f32[768,32]{1,0:T(8,128)S(1)} %get-tuple-element.16, f32[768,32]{1,0:T(8,128)S(1)} %get-tuple-element.15), kind=kLoop, calls=%fused_computation.4 | loop fusion | flops 589824 | bytes 1081344 | tf_op jit(solution)/shard_map/concatenate | solution.py:325
  36.2 3.5 %rotate_queries.1.qr_ref = bf16[256,2048]{1,0:T(8,128)(2,1)} custom-call(bf16[256,1024]{1,0:T(8,128)(2,1)} %x_ref.1, f32[768,128]{1,0:T(8,128)} %get-tuple-element.25.cos_ref, f32[768,128]{1,0:T(8,128)} %get-tuple-element.26.sin_ref), custom_call_target="tpu_custom_call" | custom-call | flops 1048576 | bytes 1572864 | tf_op jit(solution)/shard_map/rotate_queries/pallas_call | solution.py:125
  39.7 1.3 %slice.35 = bf16[1,1]{1,0:T(2,128)(2,1)} slice(bf16[256,2048]{1,0:T(8,128)(2,1)} %rotate_queries.1.qr_ref), slice={[0:1], [0:1]} | slice | bytes 4 | tf_op jit(solution)/shard_map/slice | solution.py:330
  41.6 0.1 fusion.2.order_ref
  41.6 0.1 add_convert_fusion.sel_ref
  41.7 0.0 collective-permute-done
  41.7 0.5 slice.33
  42.3 5.9 %collective-permute-done.1 = bf16[64,640]{1,0:T(8,128)(2,1)S(1)} collective-permute-done((bf16[64,640]{1,0:T(8,128)(2,1)S(1)}, bf16[64,640]{1,0:T(8,128)(2,1)S(1)}, u32[]{:S(2)}, u32[]{:S(2)}) %collective-permute-start.1) | collective-permute-done | bytes 81952 | tf_op jit(solution)/shard_map/ppermute | solution.py:315
  48.1 0.6 slice.34
  48.7 0.7 pad_maximum_fusion.3
  49.5 5.0 %collective-permute-start.2 = (bf16[3,64,640]{2,1,0:T(8,128)(2,1)}, bf16[3,64,640]{2,1,0:T(8,128)(2,1)}, u32[]{:S(2)}, u32[]{:S(2)}) collective-permute-start(bf16[3,64,640]{2,1,0:T(8,128)(2,1)} %pad_maximum_fusion.3), channel_id=1, source_target_pairs={{0,2},{2,0},{1,3},{3,1},{4,6},{6,4},{5,7},{7,5},{8,10},{10,8},{9,1... | collective-permute-start | bytes 737288 | tf_op jit(solution)/shard_map/ppermute | solution.py:333
  56.4 0.0 all-to-all-done
  56.4 0.1 broadcast_add_fusion
  56.5 0.0 copy-start.4
  56.5 1.0 copy-done.4
  57.5 0.3 add.303.refs_0_.refs_5_
  57.8 9.0 %collective-permute-start.4 = (bf16[128,4096]{1,0:T(8,128)(2,1)S(1)}, bf16[128,4096]{1,0:T(8,128)(2,1)S(1)}, u32[]{:S(2)}, u32[]{:S(2)}) collective-permute-start(bf16[128,4096]{1,0:T(8,128)(2,1)S(1)} %add.303.refs_0_.refs_5_), channel_id=1, source_target_pairs={{48,0},{52,4},{56,8},{60,12},{0,16},{4,20},{8,24},{12,28},{16,32},... | collective-permute-start | bytes 3145736 | tf_op jit(solution)/shard_map/ppermute | solution.py:67
  66.8 1.9 %collective-permute-start.3 = (bf16[128,4096]{1,0:T(8,128)(2,1)S(1)}, bf16[128,4096]{1,0:T(8,128)(2,1)S(1)}, u32[]{:S(2)}, u32[]{:S(2)}) collective-permute-start(bf16[128,4096]{1,0:T(8,128)(2,1)S(1)} %add.303.refs_0_.refs_5_), channel_id=1, source_target_pairs={{16,0},{20,4},{24,8},{28,12},{32,16},{36,20},{40,24},{44,28},{48,3... | collective-permute-start | bytes 3145736 | tf_op jit(solution)/shard_map/ppermute | solution.py:67
  68.7 2.8 %fusion.9 = (bf16[16,4,4096]{2,1,0:T(4,128)(2,1)}, bf16[16,4,4096]{2,1,0:T(4,128)(2,1)}) fusion(bf16[32,4,4096]{2,1,0:T(4,128)(2,1)} %bitcast.23), kind=kLoop, calls=%fused_computation.62 | loop fusion | bytes 2097152 | tf_op jit(solution)/shard_map/slice | solution.py:77
  71.5 2.0 %slice.31 = bf16[64,4096]{1,0:T(8,128)(2,1)} reshape(bf16[16,4,4096]{2,1,0:T(4,128)(2,1)} %get-tuple-element.9) | data formatting | bytes 1048576 | tf_op jit(solution)/shard_map/slice | solution.py:77
  73.5 2.0 %slice.29 = bf16[64,4096]{1,0:T(8,128)(2,1)} reshape(bf16[16,4,4096]{2,1,0:T(4,128)(2,1)} %get-tuple-element.10) | data formatting | bytes 1048576 | tf_op jit(solution)/shard_map/slice | solution.py:76
  75.4 2.9 %collective-permute-start.5 = (bf16[64,4096]{1,0:T(8,128)(2,1)}, bf16[64,4096]{1,0:T(8,128)(2,1)S(1)}, u32[]{:S(2)}, u32[]{:S(2)}) collective-permute-start(bf16[64,4096]{1,0:T(8,128)(2,1)} %slice.29), channel_id=1, source_target_pairs={{64,0},{68,4},{72,8},{76,12},{80,16},{84,20},{88,24},{92,28},{96,3... | collective-permute-start | bytes 1572872 | tf_op jit(solution)/shard_map/ppermute | solution.py:67
  78.3 3.0 %collective-permute-start.6 = (bf16[64,4096]{1,0:T(8,128)(2,1)}, bf16[64,4096]{1,0:T(8,128)(2,1)S(1)}, u32[]{:S(2)}, u32[]{:S(2)}) collective-permute-start(bf16[64,4096]{1,0:T(8,128)(2,1)} %slice.31), channel_id=1, source_target_pairs={{448,0},{452,4},{456,8},{460,12},{464,16},{468,20},{472,24},{476,2... | collective-permute-start | bytes 1572872 | tf_op jit(solution)/shard_map/ppermute | solution.py:67
  81.3 0.0 collective-permute-done.2
  81.3 1.0 select_bitcast_fusion.1
  82.3 0.1 pad_maximum_fusion
  82.4 0.0 copy-start
  82.4 0.0 copy-start.1
  82.4 0.0 copy-start.3
  82.4 2.6 %all-gather = bf16[4,3,64,640]{3,2,1,0:T(8,128)(2,1)S(1)} all-gather(bf16[2,3,64,640]{3,2,1,0:T(8,128)(2,1)S(1)} %pad_maximum_fusion), channel_id=2, replica_groups={{0,1},{2,3},{4,5},{6,7},{8,9},{10,11},{12,13},{14,15},{16,17},{18,19},{..., dimensions={0}, use_global_device_ids=true | all-gather | bytes 1474560 | tf_op jit(solution)/shard_map/all_gather | solution.py:336
  85.0 0.0 copy-start.2
  85.0 0.0 copy-done
  85.0 0.0 copy-done.1
  85.0 0.6 prepare_keys.1
  85.6 1.1 %collective-permute-done.5.refs_3_.refs_8_ = bf16[64,4096]{1,0:T(8,128)(2,1)S(1)} collective-permute-done((bf16[64,4096]{1,0:T(8,128)(2,1)}, bf16[64,4096]{1,0:T(8,128)(2,1)S(1)}, u32[]{:S(2)}, u32[]{:S(2)}) %collective-permute-start.5) | collective-permute-done | bytes 524320 | tf_op jit(solution)/shard_map/ppermute | solution.py:67
  86.7 4.1 %collective-permute-done.6.refs_4_.refs_9_ = bf16[64,4096]{1,0:T(8,128)(2,1)S(1)} collective-permute-done((bf16[64,4096]{1,0:T(8,128)(2,1)}, bf16[64,4096]{1,0:T(8,128)(2,1)S(1)}, u32[]{:S(2)}, u32[]{:S(2)}) %collective-permute-start.6) | collective-permute-done | bytes 524320 | tf_op jit(solution)/shard_map/ppermute | solution.py:67
  90.8 0.0 collective-permute-done.4.refs_2_.refs_7_
  90.8 0.0 collective-permute-done.3.refs_1_.refs_6_
  90.8 0.0 copy-done.3
  90.8 0.0 copy-done.2
  90.8 11.1 %attend.1 = bf16[256,2048]{1,0:T(8,128)(2,1)} custom-call(s32[2]{0:T(128)S(1)} %add_convert_fusion.sel_ref, bf16[768,512]{1,0:T(8,128)(2,1)S(1)} %get-tuple-element.7.lat_ref, bf16[768,128]{1,0:T(8,128)(2,1)S(1)} %get-tuple-element.8.rot_ref, bf16[256,2048]{1,0:T(8,128)(2,1)S(1)} %copy-done.3, bf16[256,2048]{1,0:T(8,128)(2,1)S(1)} %copy-done.2, ...), custom_call_target="tpu_custom_call" | custom-call | flops 4630511616 | bytes 12517376 | tf_op jit(solution)/shard_map/attend/pallas_call | solution.py:282
  (9 shorter events, 0.1 us)
Async XLA Ops:
  2.2 14.7 %copy-start.5 = (bf16[64,512]{1,0:T(8,128)(2,1)S(1)}, bf16[64,512]{1,0:T(8,128)(2,1)}, u32[]{:S(2)}) copy-start(bf16[64,512]{1,0:T(8,128)(2,1)} %param.9) | copy-start | bytes 196612
  2.2 14.7 %copy-start.6 = (bf16[64,64]{1,0:T(8,128)(2,1)S(1)}, bf16[64,64]{1,0:T(8,128)(2,1)}, u32[]{:S(2)}) copy-start(bf16[64,64]{1,0:T(8,128)(2,1)} %param.10) | copy-start | bytes 24580
  2.2 54.2 %all-to-all-start = ((bf16[32,4,4096]{2,1,0:T(4,128)(2,1)}), bf16[32,4,4096]{2,1,0:T(4,128)(2,1)S(1)}, u32[]{:S(2)}, u32[]{:S(2)}) async-start(bf16[32,4,4096]{2,1,0:T(4,128)(2,1)} %broadcast_in_dim.2), calls=%async_computation | async-start | bytes 2097152 | tf_op jit(solution)/shard_map/all_to_all | solution.py:47
  17.1 24.7 %collective-permute-start = (bf16[64,640]{1,0:T(8,128)(2,1)S(1)}, bf16[64,640]{1,0:T(8,128)(2,1)S(1)}, u32[]{:S(2)}, u32[]{:S(2)}) collective-permute-start(bf16[64,640]{1,0:T(8,128)(2,1)S(1)} %get-tuple-element.14), channel_id=1, source_target_pairs={{0,4},{4,8},{8,12},{12,16},{16,20},{20,24},{24,28},{28,32},{32,36}... | collective-permute-start | bytes 245768 | tf_op jit(solution)/shard_map/ppermute | solution.py:315
  20.8 27.4 %collective-permute-start.1 = (bf16[64,640]{1,0:T(8,128)(2,1)S(1)}, bf16[64,640]{1,0:T(8,128)(2,1)S(1)}, u32[]{:S(2)}, u32[]{:S(2)}) collective-permute-start(bf16[64,640]{1,0:T(8,128)(2,1)S(1)} %get-tuple-element.14), channel_id=1, source_target_pairs={{0,8},{4,12},{8,16},{12,20},{16,24},{20,28},{24,32},{28,36},{32,40... | collective-permute-start | bytes 245768 | tf_op jit(solution)/shard_map/ppermute | solution.py:315
  25.2 0.7 copy-start.7
  49.5 31.8 %collective-permute-start.2 = (bf16[3,64,640]{2,1,0:T(8,128)(2,1)}, bf16[3,64,640]{2,1,0:T(8,128)(2,1)}, u32[]{:S(2)}, u32[]{:S(2)}) collective-permute-start(bf16[3,64,640]{2,1,0:T(8,128)(2,1)} %pad_maximum_fusion.3), channel_id=1, source_target_pairs={{0,2},{2,0},{1,3},{3,1},{4,6},{6,4},{5,7},{7,5},{8,10},{10,8},{9,1... | collective-permute-start | bytes 737288 | tf_op jit(solution)/shard_map/ppermute | solution.py:333
  56.5 1.0 copy-start.4
  57.8 33.0 %collective-permute-start.4 = (bf16[128,4096]{1,0:T(8,128)(2,1)S(1)}, bf16[128,4096]{1,0:T(8,128)(2,1)S(1)}, u32[]{:S(2)}, u32[]{:S(2)}) collective-permute-start(bf16[128,4096]{1,0:T(8,128)(2,1)S(1)} %add.303.refs_0_.refs_5_), channel_id=1, source_target_pairs={{48,0},{52,4},{56,8},{60,12},{0,16},{4,20},{8,24},{12,28},{16,32},... | collective-permute-start | bytes 3145736 | tf_op jit(solution)/shard_map/ppermute | solution.py:67
  66.8 24.0 %collective-permute-start.3 = (bf16[128,4096]{1,0:T(8,128)(2,1)S(1)}, bf16[128,4096]{1,0:T(8,128)(2,1)S(1)}, u32[]{:S(2)}, u32[]{:S(2)}) collective-permute-start(bf16[128,4096]{1,0:T(8,128)(2,1)S(1)} %add.303.refs_0_.refs_5_), channel_id=1, source_target_pairs={{16,0},{20,4},{24,8},{28,12},{32,16},{36,20},{40,24},{44,28},{48,3... | collective-permute-start | bytes 3145736 | tf_op jit(solution)/shard_map/ppermute | solution.py:67
  75.4 11.3 %collective-permute-start.5 = (bf16[64,4096]{1,0:T(8,128)(2,1)}, bf16[64,4096]{1,0:T(8,128)(2,1)S(1)}, u32[]{:S(2)}, u32[]{:S(2)}) collective-permute-start(bf16[64,4096]{1,0:T(8,128)(2,1)} %slice.29), channel_id=1, source_target_pairs={{64,0},{68,4},{72,8},{76,12},{80,16},{84,20},{88,24},{92,28},{96,3... | collective-permute-start | bytes 1572872 | tf_op jit(solution)/shard_map/ppermute | solution.py:67
  78.3 12.5 %collective-permute-start.6 = (bf16[64,4096]{1,0:T(8,128)(2,1)}, bf16[64,4096]{1,0:T(8,128)(2,1)S(1)}, u32[]{:S(2)}, u32[]{:S(2)}) collective-permute-start(bf16[64,4096]{1,0:T(8,128)(2,1)} %slice.31), channel_id=1, source_target_pairs={{448,0},{452,4},{456,8},{460,12},{464,16},{468,20},{472,24},{476,2... | collective-permute-start | bytes 1572872 | tf_op jit(solution)/shard_map/ppermute | solution.py:67
  82.4 2.7 %copy-start = (f32[768,128]{1,0:T(8,128)S(1)}, f32[768,128]{1,0:T(8,128)}, u32[]{:S(2)}) copy-start(f32[768,128]{1,0:T(8,128)} %get-tuple-element.25.cos_ref) | copy-start | bytes 1179652
  82.4 2.7 %copy-start.1 = (f32[768,128]{1,0:T(8,128)S(1)}, f32[768,128]{1,0:T(8,128)}, u32[]{:S(2)}) copy-start(f32[768,128]{1,0:T(8,128)} %get-tuple-element.26.sin_ref) | copy-start | bytes 1179652
  82.4 8.4 %copy-start.3 = (bf16[256,2048]{1,0:T(8,128)(2,1)S(1)}, bf16[256,2048]{1,0:T(8,128)(2,1)}, u32[]{:S(2)}) copy-start(bf16[256,2048]{1,0:T(8,128)(2,1)} %qn_ref.1) | copy-start | bytes 3145732
  85.0 5.8 %copy-start.2 = (bf16[256,2048]{1,0:T(8,128)(2,1)S(1)}, bf16[256,2048]{1,0:T(8,128)(2,1)}, u32[]{:S(2)}) copy-start(bf16[256,2048]{1,0:T(8,128)(2,1)} %rotate_queries.1.qr_ref) | copy-start | bytes 3145732

commit v5 on v4

--- a/solution.py
+++ b/solution.py
@@ -37,20 +37,31 @@
     return jnp.where(plan == 0, x + 2 * z, z + 2 * x) % 4
 
 
-def gather_own(shard):
-    groups = [
-        [place(z, x, y) * N_HEAD + head for z, x in members(plan_of(head), c) for y in range(NY)]
-        for head in range(N_HEAD)
-        for c in range(4)
-    ]
+def spread(value, groups):
     size = len(groups[0])
     return lax.all_to_all(
-        jnp.broadcast_to(shard[None], (size,) + shard.shape),
+        jnp.broadcast_to(value[None], (size,) + value.shape),
         ("ctx", "head"),
         0,
         0,
         axis_index_groups=groups,
-    ).reshape(size * shard.shape[0], shard.shape[1])
+    ).reshape(size * value.shape[0], value.shape[1])
+
+
+def gather_own(shard):
+    lines = [
+        [place(z, x, y) * N_HEAD + head for y in range(NY)]
+        for head in range(N_HEAD)
+        for z in range(NZ)
+        for x in range(NX)
+    ]
+    colours = [
+        [place(z, x, y) * N_HEAD + head for z, x in members(plan_of(head), c)]
+        for head in range(N_HEAD)
+        for c in range(4)
+        for y in range(NY)
+    ]
+    return spread(spread(shard, lines), colours)
 
 
 def from_neighbour(value, step, along):
@@ -67,15 +78,8 @@
     return lax.ppermute(value, ("ctx", "head"), pairs)
 
 
-def gather_rest(own):
-    mid = own.shape[0] // 2
-    return (
-        own,
-        from_neighbour(own, 1, 0),
-        from_neighbour(own, -1, 0),
-        from_neighbour(own[:mid], 1, 1),
-        from_neighbour(own[mid:], -1, 1),
-    )
+def gather_rest(own, side):
+    return own, from_neighbour(own, 1, 0), from_neighbour(own, -1, 0), from_neighbour(own, side, 1)
 
 
 def row_order(plan, z, x, rows):
@@ -90,10 +94,11 @@
     return (mz * NX + mx) * (NY * rows) + inner
 
 
-def angles_of(pos, width):
-    half = width // 2
-    freq = 10000.0 ** (-(2.0 * jnp.arange(half, dtype=jnp.float32)) / width)
-    return pos.astype(jnp.float32)[..., None] * freq
+def factors(cosine, sine):
+    return (
+        jnp.concatenate([cosine] * 4, 0).T,
+        jnp.concatenate([-sine, sine, -sine, sine], 0).T,
+    )
 
 
 def turned(x, cosine, sine):
@@ -102,14 +107,19 @@
     return x * cosine + swapped * sine
 
 
-def rotate_queries_kernel(x_ref, cos_ref, sin_ref, o_ref):
+def rotate_queries_kernel(x_ref, cos_ref, sin_ref, o_ref, cos_s, sin_s):
     rows = x_ref.shape[0]
     left = lax.broadcasted_iota(jnp.int32, (rows, 128), 1) < 64
 
-    def own(ref):
-        return jnp.concatenate([ref[:HALF], ref[STEPS * HALF : (STEPS + 1) * HALF]], 0)
-
-    cosine, sine = own(cos_ref), own(sin_ref)
+    @pl.when(pl.program_id(0) == 0)
+    def _():
+        def own(ref):
+            late = STEPS * HALF
+            return jnp.concatenate([ref[:, :HALF], ref[:, late : late + HALF]], 1)
+
+        cos_s[...], sin_s[...] = factors(own(cos_ref), own(sin_ref))
+
+    cosine, sine = cos_s[...], sin_s[...]
     for pair in range(x_ref.shape[1] // 128):
         x = turned(x_ref[:, pair * 128 : (pair + 1) * 128].astype(jnp.float32), cosine, sine)
         high = x.astype(jnp.bfloat16).astype(jnp.float32)
@@ -124,7 +134,15 @@
     tok_len, width = q_rope.shape
     return pl.pallas_call(
         rotate_queries_kernel,
+        grid=(4,),
+        in_specs=[
+            pl.BlockSpec((tok_len, width // 4), lambda i: (0, i)),
+            pl.BlockSpec(cosine.shape, lambda i: (0, 0)),
+            pl.BlockSpec(sine.shape, lambda i: (0, 0)),
+        ],
+        out_specs=pl.BlockSpec((tok_len, width // 2), lambda i: (0, i)),
         out_shape=jax.ShapeDtypeStruct((tok_len, 2 * width), jnp.bfloat16),
+        scratch_shapes=[pltpu.VMEM((tok_len, 128), jnp.float32)] * 2,
         cost_estimate=pl.CostEstimate(
             flops=4 * tok_len * width, bytes_accessed=6 * tok_len * width, transcendentals=0
         ),
@@ -148,13 +166,13 @@
     place_of = (at == order_ref[...]).astype(jnp.float32).astype(jnp.bfloat16)
     lat = jnp.dot(held[:, :depth], place_of, preferred_element_type=jnp.float32)
     lat_ref[...] = lat.astype(jnp.bfloat16)
-    rot = turned(held[:, depth:].astype(jnp.float32), cos_ref[...], sin_ref[...])
+    rot = turned(held[:, depth:].astype(jnp.float32), *factors(cos_ref[...], sin_ref[...]))
     rot_ref[...] = rot.astype(jnp.bfloat16)
 
 
 def prepare_keys(held, order, cosine, sine):
     depth = order.shape[0]
-    count = cosine.shape[0]
+    count = cosine.shape[1]
     return pl.pallas_call(
         prepare_keys_kernel,
         out_shape=(
@@ -172,7 +190,7 @@
 def attend_kernel(width, sel_ref, lat_ref, rot_ref, qn_ref, qr_ref, *refs):
     o_ref, key_s, val_s, score_s, prob_s, sum_s = refs[-6:]
     lat = lat_ref[...]
-    pieces = (len(refs) - 6) // 2
+    pieces = 4
     up_k = jnp.concatenate([r[...] for r in refs[:pieces]], 0)
     up_v = jnp.concatenate([r[...] for r in refs[pieces : 2 * pieces]], 0)
     key_s[...] = jnp.dot(lat, up_k, preferred_element_type=jnp.float32).astype(jnp.bfloat16)
@@ -254,11 +272,10 @@
         o_ref[HALF:, cols] = (out_late / sum_s[h, 0]).astype(jnp.bfloat16)
 
 
-def attend(sel, lat, rot, q_nope, q_rot, weights):
+def attend(first, heads, sel, lat, rot, q_nope, q_rot, weights, earlier):
     tok_len, all_cols = q_nope.shape
     width = 4
     cols = width * NOPE
-    heads = all_cols // NOPE
     steps = heads // width
     count, depth = lat.shape
     blocks = 2 * STEPS + 1
@@ -267,7 +284,7 @@
         return pl.BlockSpec(shape, lambda i: (0, 0))
 
     def mine(shape):
-        return pl.BlockSpec(shape, lambda i: (0, i))
+        return pl.BlockSpec(shape, lambda i: (0, first // width + i))
 
     in_specs = [
         pl.BlockSpec(memory_space=pltpu.SMEM),
@@ -278,7 +295,14 @@
     ]
     in_specs += [pl.BlockSpec((w.shape[0], cols), lambda i: (0, i)) for w in weights]
     in_specs += [pl.BlockSpec((w.shape[0], cols), lambda i: (0, steps + i)) for w in weights]
-    flops = 4 * count * depth * all_cols + heads * blocks * HALF * HALF * (2 * 256 + 2 * VDIM)
+    operands = [sel, lat, rot, q_nope, q_rot, *weights, *weights]
+    aliases = {}
+    if earlier is not None:
+        in_specs.append(pl.BlockSpec(memory_space=pl.ANY))
+        aliases = {len(operands): 0}
+        operands.append(earlier)
+    some = heads * NOPE
+    flops = 4 * count * depth * some + heads * blocks * HALF * HALF * (2 * 256 + 2 * VDIM)
     return pl.pallas_call(
         functools.partial(attend_kernel, width),
         grid=(steps,),
@@ -292,18 +316,20 @@
             pltpu.VMEM((width, HALF, blocks * HALF), jnp.bfloat16),
             pltpu.VMEM((width, 2, HALF, 1), jnp.float32),
         ],
+        input_output_aliases=aliases,
         compiler_params=pltpu.CompilerParams(vmem_limit_bytes=40 * 1024 * 1024),
         cost_estimate=pl.CostEstimate(
             flops=flops,
-            bytes_accessed=2 * (4 * depth * all_cols + 3 * tok_len * all_cols + count * 640),
+            bytes_accessed=2 * (4 * depth * some + 3 * tok_len * some + count * 640),
             transcendentals=heads * blocks * HALF * HALF,
         ),
-        name="attend",
-    )(sel, lat, rot, q_nope, q_rot, *weights, *weights)
+        name=f"attend_{first}",
+    )(*operands)
 
 
 def local(q_nope, q_rope, latent, k_rope, blocks, w_uk, w_uv):
     w_rows = w_uk.shape[0]
+    parts = [(0, 12), (12, 4)]
     n_ctx = lax.axis_size("ctx")
     ctx_index = lax.axis_index("ctx")
     head_index = lax.axis_index("head")
@@ -315,28 +341,37 @@
         visited.append(lax.ppermute(own, "ctx", pairs))
     held = jnp.stack(visited)
 
-    own_rows = gather_own(jnp.concatenate([w_uk, w_uv], 1))
-
-    shards = [(ctx_index - step) % n_ctx for step in range(STEPS)]
+    own_rows = gather_own(
+        jnp.concatenate([w[:, f * NOPE : (f + n) * NOPE] for f, n in parts for w in (w_uk, w_uv)], 1)
+    )
+
+    shards = (ctx_index - jnp.arange(STEPS, dtype=jnp.int32)) % n_ctx
+    at = jnp.arange(n_ctx, dtype=jnp.int32)[:, None] == shards[None, :]
+    pairs_of = jnp.sum(jnp.where(at[:, None, :], blocks[:, :, None], 0), axis=0)
     rows = jnp.arange(HALF, dtype=jnp.int32)
-    pos = jnp.concatenate([blocks[c, half] * HALF + rows for half in range(2) for c in shards])
-    angles = angles_of(pos, ROPE)
+    pos = (pairs_of[:, :, None] * HALF + rows).reshape(-1)
+    half = ROPE // 2
+    freq = 10000.0 ** (-(2.0 * jnp.arange(half, dtype=jnp.float32)) / ROPE)
+    angles = pos.astype(jnp.float32)[None, :] * freq[:, None]
     cosine, sine = jnp.cos(angles), jnp.sin(angles)
-    cosine = jnp.concatenate([cosine] * 4, 1)
-    sine = jnp.concatenate([-sine, sine, -sine, sine], 1)
     q_rot = rotate_queries(q_rope, cosine, sine)
-    sel = jnp.stack([(blocks[c, 0] < blocks[ctx_index, 0]).astype(jnp.int32) for c in shards[1:]])
-
-    zero = held[0, 0, 0] * 0 + held[1, 0, 0] * 0 + held[2, 0, 0] * 0 + q_rot[0, 0] * 0
-    weights = gather_rest(own_rows + zero)
+    sel = (pairs_of[0, 1:] < pairs_of[0, 0]).astype(jnp.int32)
 
     across = lax.ppermute(held, "head", [(0, 2), (2, 0), (1, 3), (3, 1)])
     upper = head_index // 2 == 0
+    weights = []
+    for i, (first, count) in enumerate(parts):
+        cols = slice(2 * first * NOPE, 2 * (first + count) * NOPE)
+        some = own_rows[:, cols] if i else lax.optimization_barrier(own_rows)[:, cols] + q_rot[0, 0] * 0
+        weights.append(gather_rest(some, 1 - 2 * i))
     two = jnp.stack([jnp.where(upper, held, across), jnp.where(upper, across, held)])
     both = lax.all_gather(two, "head", axis=0, axis_index_groups=[[0, 1], [2, 3]])
     order = row_order(plan_of(head_index), z, x, w_rows)
     lat, rot = prepare_keys(both, order, cosine, sine)
-    return attend(sel, lat, rot, q_nope, q_rot, weights)
+    result = None
+    for (first, count), some in zip(parts, weights):
+        result = attend(first, count, sel, lat, rot, q_nope, q_rot, some, result)
+    return result
 
 
 def solution(mesh):

time: 103 us -> 94.5 us (0.917)
  blocking collectives: 2.64 us -> 13.4 us
  between operations: 9.01 us -> 0.89 us
  local copies, waits for them, and re-layouts: 13.7 us -> 6.42 us
  starting transfers between devices: 44.4 us -> 40.2 us
  Pallas kernels: 15.1 us -> 16.9 us
  other arithmetic: 5.93 us -> 4.18 us
    all_to_all x0 -> x1, blocking collectives: none -> 10.7 us  [spread(): lax.all_to_all(jnp.broadcast_to(value[None], (size,) + value.shape), ('ct...]
    all_to_all x1, waiting for transfers between devices: 0.01 us -> 10.5 us  [spread(): lax.all_to_all(jnp.broadcast_to(value[None], (size,) + value.shape), ('ct...]
    slice x6 -> x10, local copies, waits for them, and re-layouts: 8.37 us -> 2.26 us  [the longest x1 0.97 us: local(): own_rows[:, cols]]
    ppermute x2, waiting for transfers between devices: 5.89 us -> 0.6 us  [local(): visited.append(lax.ppermute(own, 'ctx', pairs))]
    ppermute x4 -> x6, waiting for transfers between devices: 5.17 us -> 0.02 us  [from_neighbour(): return lax.ppermute(value, ('ctx', 'head'), pairs)]
    all_to_all x1, starting transfers between devices: 14.7 us -> 11.3 us  [spread(): lax.all_to_all(jnp.broadcast_to(value[None], (size,) + value.shape), ('ct...]
    concatenate x3 -> x1, other arithmetic: 2.33 us -> 0.02 us  [local(): jnp.concatenate([w[:, f * NOPE:(f + n) * NOPE] for f, n in parts for w in...]
    ppermute x2, starting transfers between devices: 7.96 us -> 5.82 us  [local(): visited.append(lax.ppermute(own, 'ctx', pairs))]
  transfers between devices with their start and end apart: 8 -> 10, of which waited for: 3 -> 2; matrix products, arithmetic and copies ran while one was open for 15% -> 8% of each run, Pallas kernels for 4% -> 14%
where the time goes in v5:
time: 94.5 us; the launch traced here: 93.1 us
  starting transfers between devices  40.2 us (43%)
  Pallas kernels  16.9 us (18%)
  blocking collectives  13.4 us (14%)
  waiting for transfers between devices  11.1 us (12%)
  local copies, waits for them, and re-layouts  6.42 us (7%)
  other arithmetic  4.18 us (4%)
    ppermute x6, starting transfers between devices, from_neighbour(): return lax.ppermute(value, ('ctx', 'head'), pairs)  17.5 us
    pallas_call x2, Pallas kernels, attend(): pl.pallas_call(functools.partial(attend_kernel, width), grid=(steps,), in...  12.1 us
    all_to_all x1, starting transfers between devices, spread(): lax.all_to_all(jnp.broadcast_to(value[None], (size,) + value.shape), ('ct...  11.3 us
    all_to_all x1, blocking collectives, spread(): lax.all_to_all(jnp.broadcast_to(value[None], (size,) + value.shape), ('ct...  10.7 us
    all_to_all x1, waiting for transfers between devices, spread(): lax.all_to_all(jnp.broadcast_to(value[None], (size,) + value.shape), ('ct...  10.5 us
    ppermute x2, starting transfers between devices, local(): visited.append(lax.ppermute(own, 'ctx', pairs))  5.82 us
    ppermute x1, starting transfers between devices, local(): across = lax.ppermute(held, 'head', [(0, 2), (2, 0), (1, 3), (3, 1)])  5.52 us
    pallas_call x1, Pallas kernels, rotate_queries(): pl.pallas_call(rotate_queries_kernel, grid=(4,), in_specs=[pl.BlockSpec((...  4.15 us
  transfers between devices with their start and end apart: 10, of which 2 were waited for; matrix products, arithmetic and copies ran while one was open for 8% of the time, Pallas kernels for 14%

profile of v5, /device:TPU:6, one launch (start us, length us, event | category | flops | bytes accessed | tf_op | source)
XLA Modules:
  0.0 93.1 jit_solution(8322395212422950061)
XLA Ops:
  0.0 0.0 slice-start.3
  0.0 0.0 slice-start
  0.0 0.0 slice-start.1
  0.0 0.0 slice-start.2
  0.0 0.7 slice-done.3
  0.7 0.0 slice-done
  0.7 0.0 slice-done.1
  0.7 0.0 slice-done.2
  0.8 10.7 %all_to_all.10 = bf16[4,4,4096]{2,1,0:T(4,128)(2,1)S(1)} all-to-all(bf16[4,4,4096]{2,1,0:T(4,128)(2,1)S(1)} %broadcast_in_dim.29), channel_id=1, replica_groups={{0,4,8,12},{16,20,24,28},{32,36,40,44},{48,52,56,60},{64,68,72,76},{80,..., dimensions={0} | all-to-all | bytes 262144 | tf_op jit(solution)/shard_map/all_to_all | solution.py:42
  11.6 1.1 %broadcast_in_dim.47 = bf16[8,16,4096]{2,1,0:T(8,128)(2,1)} broadcast(bf16[16,4096]{1,0:T(8,128)(2,1)S(1)} %broadcast_in_dim.46), dimensions={1,2} | broadcast | bytes 1179648 | tf_op jit(solution)/shard_map/broadcast_in_dim | solution.py:43
  12.7 0.0 copy-start.5
  12.7 0.0 copy-start.6
  12.7 11.3 %all-to-all-start.1 = ((bf16[8,16,4096]{2,1,0:T(8,128)(2,1)}), bf16[8,16,4096]{2,1,0:T(8,128)(2,1)S(1)}, u32[]{:S(2)}, u32[]{:S(2)}) async-start(bf16[8,16,4096]{2,1,0:T(8,128)(2,1)} %broadcast_in_dim.47), calls=%async_computation.1 | async-start | bytes 2097152 | tf_op jit(solution)/shard_map/all_to_all | solution.py:42
  24.0 0.0 copy-done.5
  24.0 0.0 copy-done.6
  24.0 0.1 fusion.9
  24.1 3.0 %collective-permute-start = (bf16[64,640]{1,0:T(8,128)(2,1)S(1)}, bf16[64,640]{1,0:T(8,128)(2,1)S(1)}, u32[]{:S(2)}, u32[]{:S(2)}) collective-permute-start(bf16[64,640]{1,0:T(8,128)(2,1)S(1)} %get-tuple-element.12), channel_id=1, source_target_pairs={{0,4},{4,8},{8,12},{12,16},{16,20},{20,24},{24,28},{28,32},{32,36}... | collective-permute-start | bytes 245768 | tf_op jit(solution)/shard_map/ppermute | solution.py:341
  27.1 2.8 %collective-permute-start.1 = (bf16[64,640]{1,0:T(8,128)(2,1)S(1)}, bf16[64,640]{1,0:T(8,128)(2,1)S(1)}, u32[]{:S(2)}, u32[]{:S(2)}) collective-permute-start(bf16[64,640]{1,0:T(8,128)(2,1)S(1)} %get-tuple-element.12), channel_id=1, source_target_pairs={{0,8},{4,12},{8,16},{12,20},{16,24},{20,28},{24,32},{28,36},{32,40... | collective-permute-start | bytes 245768 | tf_op jit(solution)/shard_map/ppermute | solution.py:341
  29.9 0.0 copy-start.7
  30.0 0.1 iota_compare_fusion
  30.0 0.6 copy-done.7
  30.6 0.1 select_reduce_fusion
  30.8 0.1 copy.13
  30.9 0.1 add_convert_fusion
  31.0 1.1 %multiply_sine_fusion = (f32[32,768]{1,0:T(8,128)}, f32[32,768]{1,0:T(8,128)}) fusion(f32[32]{0:T(128)S(1)} %multiply_power_fusion, f32[768]{0:T(1024)S(1)} %convert_element_type.18), kind=kLoop, calls=%fused_computation.5 | loop fusion | flops 24576 | bytes 199808 | tf_op jit(solution)/shard_map/sin | solution.py:356
  32.1 4.2 %rotate_queries.1.qr_ref = bf16[256,2048]{1,0:T(8,128)(2,1)} custom-call(bf16[256,1024]{1,0:T(8,128)(2,1)} %x_ref.1, f32[32,768]{1,0:T(8,128)} %get-tuple-element.14.cos_ref, f32[32,768]{1,0:T(8,128)} %get-tuple-element.13.sin_ref), custom_call_target="tpu_custom_call" | custom-call | flops 1048576 | bytes 1572864 | tf_op jit(solution)/shard_map/rotate_queries/pallas_call | solution.py:135
  36.2 1.2 %slice.38 = bf16[1,1]{1,0:T(2,128)(2,1)} slice(bf16[256,2048]{1,0:T(8,128)(2,1)} %rotate_queries.1.qr_ref), slice={[0:1], [0:1]} | slice | bytes 4 | tf_op jit(solution)/shard_map/slice | solution.py:365
  38.1 0.0 collective-permute-done
  38.1 0.6 collective-permute-done.1
  38.7 0.7 pad_maximum_fusion.1
  39.5 5.5 %collective-permute-start.2 = (bf16[3,64,640]{2,1,0:T(8,128)(2,1)}, bf16[3,64,640]{2,1,0:T(8,128)(2,1)}, u32[]{:S(2)}, u32[]{:S(2)}) collective-permute-start(bf16[3,64,640]{2,1,0:T(8,128)(2,1)} %pad_maximum_fusion.1), channel_id=1, source_target_pairs={{0,2},{2,0},{1,3},{3,1},{4,6},{6,4},{5,7},{7,5},{8,10},{10,8},{9,1... | collective-permute-start | bytes 737288 | tf_op jit(solution)/shard_map/ppermute | solution.py:360
  45.0 10.5 %all-to-all-done.1 = bf16[8,16,4096]{2,1,0:T(8,128)(2,1)S(1)} async-done(((bf16[8,16,4096]{2,1,0:T(8,128)(2,1)}), bf16[8,16,4096]{2,1,0:T(8,128)(2,1)S(1)}, u32[]{:S(2)}, u32[]{:S(2)}) %all-to-all-start.1) | async-done | bytes 1048608 | tf_op jit(solution)/shard_map/all_to_all | solution.py:42
  55.5 1.0 %copy-done.4 = bf16[8,16,4096]{2,1,0:T(8,128)(2,1)} copy-done((bf16[8,16,4096]{2,1,0:T(8,128)(2,1)}, bf16[8,16,4096]{2,1,0:T(8,128)(2,1)S(1)}, u32[]{:S(2)}) %copy-start.4) | copy-done | bytes 1048600
  56.5 0.1 slice_add_fusion.refs_0_.refs_4_
  56.5 1.9 %collective-permute-start.8 = (bf16[128,3072]{1,0:T(8,128)(2,1)S(1)}, bf16[128,3072]{1,0:T(8,128)(2,1)S(1)}, u32[]{:S(2)}, u32[]{:S(2)}) collective-permute-start(bf16[128,3072]{1,0:T(8,128)(2,1)S(1)} %slice_add_fusion.refs_0_.refs_4_), channel_id=1, source_target_pairs={{64,0},{68,4},{72,8},{76,12},{80,16},{84,20},{88,24},{92,28},{96,3... | collective-permute-start | bytes 2359304 | tf_op jit(solution)/shard_map/ppermute | solution.py:78
  58.5 1.9 %collective-permute-start.7 = (bf16[128,3072]{1,0:T(8,128)(2,1)S(1)}, bf16[128,3072]{1,0:T(8,128)(2,1)S(1)}, u32[]{:S(2)}, u32[]{:S(2)}) collective-permute-start(bf16[128,3072]{1,0:T(8,128)(2,1)S(1)} %slice_add_fusion.refs_0_.refs_4_), channel_id=1, source_target_pairs={{48,0},{52,4},{56,8},{60,12},{0,16},{4,20},{8,24},{12,28},{16,32},... | collective-permute-start | bytes 2359304 | tf_op jit(solution)/shard_map/ppermute | solution.py:78
  60.4 3.9 %collective-permute-start.6 = (bf16[128,3072]{1,0:T(8,128)(2,1)S(1)}, bf16[128,3072]{1,0:T(8,128)(2,1)S(1)}, u32[]{:S(2)}, u32[]{:S(2)}) collective-permute-start(bf16[128,3072]{1,0:T(8,128)(2,1)S(1)} %slice_add_fusion.refs_0_.refs_4_), channel_id=1, source_target_pairs={{16,0},{20,4},{24,8},{28,12},{32,16},{36,20},{40,24},{44,28},{48,3... | collective-permute-start | bytes 2359304 | tf_op jit(solution)/shard_map/ppermute | solution.py:78
  64.3 0.1 fusion.1.order_ref
  64.4 0.6 slice.28
  65.0 0.7 fusion.7.sel_ref
  65.7 0.0 collective-permute-done.2
  65.7 1.0 %select_bitcast_fusion.1 = (bf16[1,3,64,640]{3,2,1,0:T(8,128)(2,1)S(1)}, bf16[1,3,64,640]{3,2,1,0:T(8,128)(2,1)S(1)}) fusion(bf16[3,64,640]{2,1,0:T(8,128)(2,1)} %collective-permute-done.2, pred[]{:T(512)S(6)} %eq.41, bf16[1,64,640]{2,1,0:T(8,128)(2,1)S(1)} %bitcast.18, bf16[1,64,640]{2,1,0:T(8,128)(2,1)S(1)} %bitcast.16, ...), kind=kLoop, calls=%fused_computation.4 | loop fusion | flops 491520 | bytes 983041 | tf_op jit(solution)/shard_map/stack | solution.py:367
  66.7 0.1 pad_maximum_fusion
  66.8 0.0 copy-start.2
  66.8 0.0 copy-start.3
  66.8 0.0 copy-start.1
  66.8 2.6 %all-gather = bf16[4,3,64,640]{3,2,1,0:T(8,128)(2,1)S(1)} all-gather(bf16[2,3,64,640]{3,2,1,0:T(8,128)(2,1)S(1)} %pad_maximum_fusion), channel_id=2, replica_groups={{0,1},{2,3},{4,5},{6,7},{8,9},{10,11},{12,13},{14,15},{16,17},{18,19},{..., dimensions={0}, use_global_device_ids=true | all-gather | bytes 1474560 | tf_op jit(solution)/shard_map/all_gather | solution.py:368
  69.4 0.0 copy-done.2
  69.4 0.0 copy-done.3
  69.5 0.6 prepare_keys.1
  70.1 1.0 %slice.36.refs_0_.refs_4_ = bf16[128,1024]{1,0:T(8,128)(2,1)S(1)} slice(bf16[128,4096]{1,0:T(8,128)(2,1)} %bitcast.14), slice={[0:128], [3072:4096]} | slice | bytes 524288 | tf_op jit(solution)/shard_map/slice | solution.py:365
  71.1 3.9 %collective-permute-start.5 = (bf16[128,1024]{1,0:T(8,128)(2,1)S(1)}, bf16[128,1024]{1,0:T(8,128)(2,1)S(1)}, u32[]{:S(2)}, u32[]{:S(2)}) collective-permute-start(bf16[128,1024]{1,0:T(8,128)(2,1)S(1)} %slice.36.refs_0_.refs_4_), channel_id=1, source_target_pairs={{448,0},{452,4},{456,8},{460,12},{464,16},{468,20},{472,24},{476,2... | collective-permute-start | bytes 786440 | tf_op jit(solution)/shard_map/ppermute | solution.py:78
  75.0 3.1 %collective-permute-start.4 = (bf16[128,1024]{1,0:T(8,128)(2,1)S(1)}, bf16[128,1024]{1,0:T(8,128)(2,1)S(1)}, u32[]{:S(2)}, u32[]{:S(2)}) collective-permute-start(bf16[128,1024]{1,0:T(8,128)(2,1)S(1)} %slice.36.refs_0_.refs_4_), channel_id=1, source_target_pairs={{48,0},{52,4},{56,8},{60,12},{0,16},{4,20},{8,24},{12,28},{16,32},... | collective-permute-start | bytes 786440 | tf_op jit(solution)/shard_map/ppermute | solution.py:78
  78.1 0.0 collective-permute-done.8.refs_3_.refs_7_
  78.1 2.7 %collective-permute-start.3 = (bf16[128,1024]{1,0:T(8,128)(2,1)S(1)}, bf16[128,1024]{1,0:T(8,128)(2,1)S(1)}, u32[]{:S(2)}, u32[]{:S(2)}) collective-permute-start(bf16[128,1024]{1,0:T(8,128)(2,1)S(1)} %slice.36.refs_0_.refs_4_), channel_id=1, source_target_pairs={{16,0},{20,4},{24,8},{28,12},{32,16},{36,20},{40,24},{44,28},{48,3... | collective-permute-start | bytes 786440 | tf_op jit(solution)/shard_map/ppermute | solution.py:78
  80.9 0.0 collective-permute-done.7.refs_2_.refs_6_
  80.9 0.0 collective-permute-done.6.refs_1_.refs_5_
  80.9 0.0 copy-done.1
  80.9 0.0 copy-done
  80.9 8.6 %attend_0.1.refs_8_ = bf16[256,2048]{1,0:T(8,128)(2,1)} custom-call(s32[2]{0:T(128)S(1)} %fusion.7.sel_ref, bf16[768,512]{1,0:T(8,128)(2,1)S(1)} %get-tuple-element.7.lat_ref, bf16[768,128]{1,0:T(8,128)(2,1)S(1)} %get-tuple-element.8.rot_ref, bf16[256,2048]{1,0:T(8,128)(2,1)S(1)} %copy-done.1, bf16[256,2048]{1,0:T(8,128)(2,1)S(1)} %copy-done, ...), custom_call_target="tpu_custom_call" | custom-call | flops 3472883712 | bytes 9633792 | tf_op jit(solution)/shard_map/attend_0/pallas_call | solution.py:306
  89.5 0.0 collective-permute-done.5.refs_3_.refs_7_
  89.5 0.0 collective-permute-done.4.refs_2_.refs_6_
  89.5 0.0 collective-permute-done.3.refs_1_.refs_5_
  89.5 3.6 %attend_12.1 = bf16[256,2048]{1,0:T(8,128)(2,1)} custom-call(s32[2]{0:T(128)S(1)} %fusion.7.sel_ref, bf16[768,512]{1,0:T(8,128)(2,1)S(1)} %get-tuple-element.7.lat_ref, bf16[768,128]{1,0:T(8,128)(2,1)S(1)} %get-tuple-element.8.rot_ref, bf16[256,2048]{1,0:T(8,128)(2,1)S(1)} %copy-done.1, ...), custom_call_target="tpu_custom_call", output_to_operand_aliasing={{}: (13, {})} | custom-call | flops 1157627904 | bytes 3866624 | tf_op jit(solution)/shard_map/attend_12/pallas_call | solution.py:306
  (9 shorter events, 0.1 us)
Async XLA Ops:
  0.0 0.7 slice-start.3
  0.0 0.7 slice-start
  0.0 0.7 slice-start.1
  0.0 0.7 slice-start.2
  12.7 11.3 %copy-start.5 = (bf16[64,512]{1,0:T(8,128)(2,1)S(1)}, bf16[64,512]{1,0:T(8,128)(2,1)}, u32[]{:S(2)}) copy-start(bf16[64,512]{1,0:T(8,128)(2,1)} %param.9) | copy-start | bytes 196612
  12.7 11.3 %copy-start.6 = (bf16[64,64]{1,0:T(8,128)(2,1)S(1)}, bf16[64,64]{1,0:T(8,128)(2,1)}, u32[]{:S(2)}) copy-start(bf16[64,64]{1,0:T(8,128)(2,1)} %param.10) | copy-start | bytes 24580
  12.7 42.8 %all-to-all-start.1 = ((bf16[8,16,4096]{2,1,0:T(8,128)(2,1)}), bf16[8,16,4096]{2,1,0:T(8,128)(2,1)S(1)}, u32[]{:S(2)}, u32[]{:S(2)}) async-start(bf16[8,16,4096]{2,1,0:T(8,128)(2,1)} %broadcast_in_dim.47), calls=%async_computation.1 | async-start | bytes 2097152 | tf_op jit(solution)/shard_map/all_to_all | solution.py:42
  24.1 14.0 %collective-permute-start = (bf16[64,640]{1,0:T(8,128)(2,1)S(1)}, bf16[64,640]{1,0:T(8,128)(2,1)S(1)}, u32[]{:S(2)}, u32[]{:S(2)}) collective-permute-start(bf16[64,640]{1,0:T(8,128)(2,1)S(1)} %get-tuple-element.12), channel_id=1, source_target_pairs={{0,4},{4,8},{8,12},{12,16},{16,20},{20,24},{24,28},{28,32},{32,36}... | collective-permute-start | bytes 245768 | tf_op jit(solution)/shard_map/ppermute | solution.py:341
  27.1 11.6 %collective-permute-start.1 = (bf16[64,640]{1,0:T(8,128)(2,1)S(1)}, bf16[64,640]{1,0:T(8,128)(2,1)S(1)}, u32[]{:S(2)}, u32[]{:S(2)}) collective-permute-start(bf16[64,640]{1,0:T(8,128)(2,1)S(1)} %get-tuple-element.12), channel_id=1, source_target_pairs={{0,8},{4,12},{8,16},{12,20},{16,24},{20,28},{24,32},{28,36},{32,40... | collective-permute-start | bytes 245768 | tf_op jit(solution)/shard_map/ppermute | solution.py:341
  29.9 0.7 copy-start.7
  39.5 26.2 %collective-permute-start.2 = (bf16[3,64,640]{2,1,0:T(8,128)(2,1)}, bf16[3,64,640]{2,1,0:T(8,128)(2,1)}, u32[]{:S(2)}, u32[]{:S(2)}) collective-permute-start(bf16[3,64,640]{2,1,0:T(8,128)(2,1)} %pad_maximum_fusion.1), channel_id=1, source_target_pairs={{0,2},{2,0},{1,3},{3,1},{4,6},{6,4},{5,7},{7,5},{8,10},{10,8},{9,1... | collective-permute-start | bytes 737288 | tf_op jit(solution)/shard_map/ppermute | solution.py:360
  55.5 1.0 %copy-start.4 = (bf16[8,16,4096]{2,1,0:T(8,128)(2,1)}, bf16[8,16,4096]{2,1,0:T(8,128)(2,1)S(1)}, u32[]{:S(2)}) copy-start(bf16[8,16,4096]{2,1,0:T(8,128)(2,1)S(1)} %all-to-all-done.1) | copy-start | bytes 3145732
  56.5 21.6 %collective-permute-start.8 = (bf16[128,3072]{1,0:T(8,128)(2,1)S(1)}, bf16[128,3072]{1,0:T(8,128)(2,1)S(1)}, u32[]{:S(2)}, u32[]{:S(2)}) collective-permute-start(bf16[128,3072]{1,0:T(8,128)(2,1)S(1)} %slice_add_fusion.refs_0_.refs_4_), channel_id=1, source_target_pairs={{64,0},{68,4},{72,8},{76,12},{80,16},{84,20},{88,24},{92,28},{96,3... | collective-permute-start | bytes 2359304 | tf_op jit(solution)/shard_map/ppermute | solution.py:78
  58.5 22.4 %collective-permute-start.7 = (bf16[128,3072]{1,0:T(8,128)(2,1)S(1)}, bf16[128,3072]{1,0:T(8,128)(2,1)S(1)}, u32[]{:S(2)}, u32[]{:S(2)}) collective-permute-start(bf16[128,3072]{1,0:T(8,128)(2,1)S(1)} %slice_add_fusion.refs_0_.refs_4_), channel_id=1, source_target_pairs={{48,0},{52,4},{56,8},{60,12},{0,16},{4,20},{8,24},{12,28},{16,32},... | collective-permute-start | bytes 2359304 | tf_op jit(solution)/shard_map/ppermute | solution.py:78
  60.4 20.5 %collective-permute-start.6 = (bf16[128,3072]{1,0:T(8,128)(2,1)S(1)}, bf16[128,3072]{1,0:T(8,128)(2,1)S(1)}, u32[]{:S(2)}, u32[]{:S(2)}) collective-permute-start(bf16[128,3072]{1,0:T(8,128)(2,1)S(1)} %slice_add_fusion.refs_0_.refs_4_), channel_id=1, source_target_pairs={{16,0},{20,4},{24,8},{28,12},{32,16},{36,20},{40,24},{44,28},{48,3... | collective-permute-start | bytes 2359304 | tf_op jit(solution)/shard_map/ppermute | solution.py:78
  66.8 2.7 %copy-start.2 = (f32[32,768]{1,0:T(8,128)S(1)}, f32[32,768]{1,0:T(8,128)}, u32[]{:S(2)}) copy-start(f32[32,768]{1,0:T(8,128)} %get-tuple-element.13.sin_ref) | copy-start | bytes 294916
  66.8 2.7 %copy-start.3 = (f32[32,768]{1,0:T(8,128)S(1)}, f32[32,768]{1,0:T(8,128)}, u32[]{:S(2)}) copy-start(f32[32,768]{1,0:T(8,128)} %get-tuple-element.14.cos_ref) | copy-start | bytes 294916
  66.8 14.1 %copy-start.1 = (bf16[256,2048]{1,0:T(8,128)(2,1)S(1)}, bf16[256,2048]{1,0:T(8,128)(2,1)}, u32[]{:S(2)}) copy-start(bf16[256,2048]{1,0:T(8,128)(2,1)} %qn_ref.3) | copy-start | bytes 3145732
  69.4 11.5 %copy-start = (bf16[256,2048]{1,0:T(8,128)(2,1)S(1)}, bf16[256,2048]{1,0:T(8,128)(2,1)}, u32[]{:S(2)}) copy-start(bf16[256,2048]{1,0:T(8,128)(2,1)} %rotate_queries.1.qr_ref) | copy-start | bytes 3145732
  71.1 18.4 %collective-permute-start.5 = (bf16[128,1024]{1,0:T(8,128)(2,1)S(1)}, bf16[128,1024]{1,0:T(8,128)(2,1)S(1)}, u32[]{:S(2)}, u32[]{:S(2)}) collective-permute-start(bf16[128,1024]{1,0:T(8,128)(2,1)S(1)} %slice.36.refs_0_.refs_4_), channel_id=1, source_target_pairs={{448,0},{452,4},{456,8},{460,12},{464,16},{468,20},{472,24},{476,2... | collective-permute-start | bytes 786440 | tf_op jit(solution)/shard_map/ppermute | solution.py:78
  75.0 14.5 %collective-permute-start.4 = (bf16[128,1024]{1,0:T(8,128)(2,1)S(1)}, bf16[128,1024]{1,0:T(8,128)(2,1)S(1)}, u32[]{:S(2)}, u32[]{:S(2)}) collective-permute-start(bf16[128,1024]{1,0:T(8,128)(2,1)S(1)} %slice.36.refs_0_.refs_4_), channel_id=1, source_target_pairs={{48,0},{52,4},{56,8},{60,12},{0,16},{4,20},{8,24},{12,28},{16,32},... | collective-permute-start | bytes 786440 | tf_op jit(solution)/shard_map/ppermute | solution.py:78
  78.1 11.4 %collective-permute-start.3 = (bf16[128,1024]{1,0:T(8,128)(2,1)S(1)}, bf16[128,1024]{1,0:T(8,128)(2,1)S(1)}, u32[]{:S(2)}, u32[]{:S(2)}) collective-permute-start(bf16[128,1024]{1,0:T(8,128)(2,1)S(1)} %slice.36.refs_0_.refs_4_), channel_id=1, source_target_pairs={{16,0},{20,4},{24,8},{28,12},{32,16},{36,20},{40,24},{44,28},{48,3... | collective-permute-start | bytes 786440 | tf_op jit(solution)/shard_map/ppermute | solution.py:78

commit v6 on v5

--- a/solution.py
+++ b/solution.py
@@ -359,11 +359,11 @@
 
     across = lax.ppermute(held, "head", [(0, 2), (2, 0), (1, 3), (3, 1)])
     upper = head_index // 2 == 0
+    zero = q_rot[0, 0] * 0
     weights = []
     for i, (first, count) in enumerate(parts):
         cols = slice(2 * first * NOPE, 2 * (first + count) * NOPE)
-        some = own_rows[:, cols] if i else lax.optimization_barrier(own_rows)[:, cols] + q_rot[0, 0] * 0
-        weights.append(gather_rest(some, 1 - 2 * i))
+        weights.append(gather_rest(own_rows[:, cols] + zero, 1 - 2 * i))
     two = jnp.stack([jnp.where(upper, held, across), jnp.where(upper, across, held)])
     both = lax.all_gather(two, "head", axis=0, axis_index_groups=[[0, 1], [2, 3]])
     order = row_order(plan_of(head_index), z, x, w_rows)

time: 94.5 us -> 92.8 us (0.982)
  the two profiles are of different devices: /device:TPU:6 before, /device:TPU:8 now
where the time goes in v6:
time: 92.8 us; the launch traced here: 92.1 us
  starting transfers between devices  47.6 us (51%)
  Pallas kernels  16.9 us (18%)
  blocking collectives  16 us (17%)
  local copies, waits for them, and re-layouts  4.44 us (5%)
  waiting for transfers between devices  3.57 us (4%)
  other arithmetic  2.64 us (3%)
  between operations  0.98 us (1%)
    ppermute x6, starting transfers between devices, from_neighbour(): return lax.ppermute(value, ('ctx', 'head'), pairs)  25.1 us
    all_to_all x1, blocking collectives, spread(): lax.all_to_all(jnp.broadcast_to(value[None], (size,) + value.shape), ('ct...  13.4 us
    pallas_call x2, Pallas kernels, attend(): pl.pallas_call(functools.partial(attend_kernel, width), grid=(steps,), in...  12.1 us
    all_to_all x1, starting transfers between devices, spread(): lax.all_to_all(jnp.broadcast_to(value[None], (size,) + value.shape), ('ct...  9.82 us
    ppermute x2, starting transfers between devices, local(): visited.append(lax.ppermute(own, 'ctx', pairs))  7.11 us
    ppermute x1, starting transfers between devices, local(): across = lax.ppermute(held, 'head', [(0, 2), (2, 0), (1, 3), (3, 1)])  5.56 us
    pallas_call x1, Pallas kernels, rotate_queries(): pl.pallas_call(rotate_queries_kernel, grid=(4,), in_specs=[pl.BlockSpec((...  4.15 us
    all_to_all x1, waiting for transfers between devices, spread(): lax.all_to_all(jnp.broadcast_to(value[None], (size,) + value.shape), ('ct...  3.55 us
  transfers between devices with their start and end apart: 10, of which 1 were waited for; matrix products, arithmetic and copies ran while one was open for 5% of the time, Pallas kernels for 15%

profile of v6, /device:TPU:8, one launch (start us, length us, event | category | flops | bytes accessed | tf_op | source)
XLA Modules:
  0.0 92.1 jit_solution(8598422798698715005)
XLA Ops:
  0.0 0.0 slice-start.3
  0.0 0.0 slice-start
  0.0 0.0 slice-start.1
  0.0 0.0 slice-start.2
  0.0 0.7 slice-done.3
  0.7 0.0 slice-done
  0.7 0.0 slice-done.1
  0.7 0.0 slice-done.2
  0.8 13.4 %all_to_all.10 = bf16[4,4,4096]{2,1,0:T(4,128)(2,1)S(1)} all-to-all(bf16[4,4,4096]{2,1,0:T(4,128)(2,1)S(1)} %broadcast_in_dim.29), channel_id=1, replica_groups={{0,4,8,12},{16,20,24,28},{32,36,40,44},{48,52,56,60},{64,68,72,76},{80,..., dimensions={0} | all-to-all | bytes 262144 | tf_op jit(solution)/shard_map/all_to_all | solution.py:42
  14.2 1.1 %broadcast_in_dim.47 = bf16[8,16,4096]{2,1,0:T(8,128)(2,1)} broadcast(bf16[16,4096]{1,0:T(8,128)(2,1)S(1)} %broadcast_in_dim.46), dimensions={1,2} | broadcast | bytes 1179648 | tf_op jit(solution)/shard_map/broadcast_in_dim | solution.py:43
  15.3 0.0 copy-start.4
  15.3 0.0 copy-start.5
  15.3 9.8 %all-to-all-start.1 = ((bf16[8,16,4096]{2,1,0:T(8,128)(2,1)}), bf16[8,16,4096]{2,1,0:T(8,128)(2,1)S(1)}, u32[]{:S(2)}, u32[]{:S(2)}) async-start(bf16[8,16,4096]{2,1,0:T(8,128)(2,1)} %broadcast_in_dim.47), calls=%async_computation.1 | async-start | bytes 2097152 | tf_op jit(solution)/shard_map/all_to_all | solution.py:42
  25.1 0.0 copy-done.4
  25.1 0.0 copy-done.5
  25.1 0.1 fusion.9
  25.2 2.1 %collective-permute-start = (bf16[64,640]{1,0:T(8,128)(2,1)S(1)}, bf16[64,640]{1,0:T(8,128)(2,1)S(1)}, u32[]{:S(2)}, u32[]{:S(2)}) collective-permute-start(bf16[64,640]{1,0:T(8,128)(2,1)S(1)} %get-tuple-element.12), channel_id=1, source_target_pairs={{0,4},{4,8},{8,12},{12,16},{16,20},{20,24},{24,28},{28,32},{32,36}... | collective-permute-start | bytes 245768 | tf_op jit(solution)/shard_map/ppermute | solution.py:341
  27.3 5.0 %collective-permute-start.1 = (bf16[64,640]{1,0:T(8,128)(2,1)S(1)}, bf16[64,640]{1,0:T(8,128)(2,1)S(1)}, u32[]{:S(2)}, u32[]{:S(2)}) collective-permute-start(bf16[64,640]{1,0:T(8,128)(2,1)S(1)} %get-tuple-element.12), channel_id=1, source_target_pairs={{0,8},{4,12},{8,16},{12,20},{16,24},{20,28},{24,32},{28,36},{32,40... | collective-permute-start | bytes 245768 | tf_op jit(solution)/shard_map/ppermute | solution.py:341
  32.4 0.0 copy-start.6
  32.5 0.1 iota_compare_fusion
  32.5 0.6 copy-done.6
  33.1 0.1 select_reduce_fusion
  33.3 0.6 slice.28
  33.9 0.1 copy.13
  34.0 0.1 add_convert_fusion
  34.1 1.1 %multiply_sine_fusion = (f32[32,768]{1,0:T(8,128)}, f32[32,768]{1,0:T(8,128)}) fusion(f32[32]{0:T(128)S(1)} %multiply_power_fusion, f32[768]{0:T(1024)S(1)} %convert_element_type.18), kind=kLoop, calls=%fused_computation.6 | loop fusion | flops 24576 | bytes 199808 | tf_op jit(solution)/shard_map/sin | solution.py:356
  35.2 4.2 %rotate_queries.1.qr_ref = bf16[256,2048]{1,0:T(8,128)(2,1)} custom-call(bf16[256,1024]{1,0:T(8,128)(2,1)} %x_ref.1, f32[32,768]{1,0:T(8,128)} %get-tuple-element.14.cos_ref, f32[32,768]{1,0:T(8,128)} %get-tuple-element.13.sin_ref), custom_call_target="tpu_custom_call" | custom-call | flops 1048576 | bytes 1572864 | tf_op jit(solution)/shard_map/rotate_queries/pallas_call | solution.py:135
  39.4 1.2 %slice.37 = bf16[1,1]{1,0:T(2,128)(2,1)} slice(bf16[256,2048]{1,0:T(8,128)(2,1)} %rotate_queries.1.qr_ref), slice={[0:1], [0:1]} | slice | bytes 4 | tf_op jit(solution)/shard_map/slice | solution.py:362
  41.2 0.8 fusion.7.sel_ref
  42.0 0.1 fusion.1.order_ref
  42.1 0.0 collective-permute-done
  42.1 0.0 collective-permute-done.1
  42.1 5.6 %collective-permute-start.2 = (bf16[3,64,640]{2,1,0:T(8,128)(2,1)S(1)}, bf16[3,64,640]{2,1,0:T(8,128)(2,1)S(1)}, u32[]{:S(2)}, u32[]{:S(2)}) collective-permute-start(bf16[3,64,640]{2,1,0:T(8,128)(2,1)S(1)} %pad_maximum_fusion.1), channel_id=1, source_target_pairs={{0,2},{2,0},{1,3},{3,1},{4,6},{6,4},{5,7},{7,5},{8,10},{10,8},{9,1... | collective-permute-start | bytes 737288 | tf_op jit(solution)/shard_map/ppermute | solution.py:360
  47.7 3.5 %all-to-all-done.1 = bf16[8,16,4096]{2,1,0:T(8,128)(2,1)S(1)} async-done(((bf16[8,16,4096]{2,1,0:T(8,128)(2,1)}), bf16[8,16,4096]{2,1,0:T(8,128)(2,1)S(1)}, u32[]{:S(2)}, u32[]{:S(2)}) %all-to-all-start.1) | async-done | bytes 1048608 | tf_op jit(solution)/shard_map/all_to_all | solution.py:42
  51.2 0.1 slice_add_fusion.refs_0_.refs_4_
  51.3 2.9 %collective-permute-start.8 = (bf16[128,3072]{1,0:T(8,128)(2,1)S(1)}, bf16[128,3072]{1,0:T(8,128)(2,1)S(1)}, u32[]{:S(2)}, u32[]{:S(2)}) collective-permute-start(bf16[128,3072]{1,0:T(8,128)(2,1)S(1)} %slice_add_fusion.refs_0_.refs_4_), channel_id=1, source_target_pairs={{64,0},{68,4},{72,8},{76,12},{80,16},{84,20},{88,24},{92,28},{96,3... | collective-permute-start | bytes 2359304 | tf_op jit(solution)/shard_map/ppermute | solution.py:78
  54.2 3.6 %collective-permute-start.7 = (bf16[128,3072]{1,0:T(8,128)(2,1)S(1)}, bf16[128,3072]{1,0:T(8,128)(2,1)S(1)}, u32[]{:S(2)}, u32[]{:S(2)}) collective-permute-start(bf16[128,3072]{1,0:T(8,128)(2,1)S(1)} %slice_add_fusion.refs_0_.refs_4_), channel_id=1, source_target_pairs={{48,0},{52,4},{56,8},{60,12},{0,16},{4,20},{8,24},{12,28},{16,32},... | collective-permute-start | bytes 2359304 | tf_op jit(solution)/shard_map/ppermute | solution.py:78
  57.8 3.9 %collective-permute-start.6 = (bf16[128,3072]{1,0:T(8,128)(2,1)S(1)}, bf16[128,3072]{1,0:T(8,128)(2,1)S(1)}, u32[]{:S(2)}, u32[]{:S(2)}) collective-permute-start(bf16[128,3072]{1,0:T(8,128)(2,1)S(1)} %slice_add_fusion.refs_0_.refs_4_), channel_id=1, source_target_pairs={{16,0},{20,4},{24,8},{28,12},{32,16},{36,20},{40,24},{44,28},{48,3... | collective-permute-start | bytes 2359304 | tf_op jit(solution)/shard_map/ppermute | solution.py:78
  61.8 0.0 collective-permute-done.2
  61.8 0.1 select_bitcast_fusion.1
  61.8 0.1 pad_maximum_fusion
  61.9 0.0 copy-start.2
  61.9 0.0 copy-start.3
  61.9 0.0 copy-start.1
  61.9 2.6 %all-gather = bf16[4,3,64,640]{3,2,1,0:T(8,128)(2,1)S(1)} all-gather(bf16[2,3,64,640]{3,2,1,0:T(8,128)(2,1)S(1)} %pad_maximum_fusion), channel_id=2, replica_groups={{0,1},{2,3},{4,5},{6,7},{8,9},{10,11},{12,13},{14,15},{16,17},{18,19},{..., dimensions={0}, use_global_device_ids=true | all-gather | bytes 1474560 | tf_op jit(solution)/shard_map/all_gather | solution.py:368
  64.6 0.0 copy-start
  64.6 0.0 copy-done.2
  64.6 0.0 copy-done.3
  64.6 0.6 prepare_keys.1
  65.3 3.9 %collective-permute-start.5 = (bf16[128,1024]{1,0:T(8,128)(2,1)S(1)}, bf16[128,1024]{1,0:T(8,128)(2,1)S(1)}, u32[]{:S(2)}, u32[]{:S(2)}) collective-permute-start(bf16[128,1024]{1,0:T(8,128)(2,1)S(1)} %slice_add_fusion.1.refs_0_.refs_4_), channel_id=1, source_target_pairs={{448,0},{452,4},{456,8},{460,12},{464,16},{468,20},{472,24},{476,2... | collective-permute-start | bytes 786440 | tf_op jit(solution)/shard_map/ppermute | solution.py:78
  69.2 2.2 %collective-permute-start.4 = (bf16[128,1024]{1,0:T(8,128)(2,1)S(1)}, bf16[128,1024]{1,0:T(8,128)(2,1)S(1)}, u32[]{:S(2)}, u32[]{:S(2)}) collective-permute-start(bf16[128,1024]{1,0:T(8,128)(2,1)S(1)} %slice_add_fusion.1.refs_0_.refs_4_), channel_id=1, source_target_pairs={{48,0},{52,4},{56,8},{60,12},{0,16},{4,20},{8,24},{12,28},{16,32},... | collective-permute-start | bytes 786440 | tf_op jit(solution)/shard_map/ppermute | solution.py:78
  71.3 0.0 collective-permute-done.8.refs_3_.refs_7_
  71.4 8.6 %collective-permute-start.3 = (bf16[128,1024]{1,0:T(8,128)(2,1)S(1)}, bf16[128,1024]{1,0:T(8,128)(2,1)S(1)}, u32[]{:S(2)}, u32[]{:S(2)}) collective-permute-start(bf16[128,1024]{1,0:T(8,128)(2,1)S(1)} %slice_add_fusion.1.refs_0_.refs_4_), channel_id=1, source_target_pairs={{16,0},{20,4},{24,8},{28,12},{32,16},{36,20},{40,24},{44,28},{48,3... | collective-permute-start | bytes 786440 | tf_op jit(solution)/shard_map/ppermute | solution.py:78
  79.9 0.0 collective-permute-done.7.refs_2_.refs_6_
  79.9 0.0 collective-permute-done.6.refs_1_.refs_5_
  80.0 0.0 copy-done.1
  80.0 0.0 copy-done
  80.0 8.6 %attend_0.1.refs_8_ = bf16[256,2048]{1,0:T(8,128)(2,1)} custom-call(s32[2]{0:T(128)S(1)} %fusion.7.sel_ref, bf16[768,512]{1,0:T(8,128)(2,1)S(1)} %get-tuple-element.7.lat_ref, bf16[768,128]{1,0:T(8,128)(2,1)S(1)} %get-tuple-element.8.rot_ref, bf16[256,2048]{1,0:T(8,128)(2,1)S(1)} %copy-done.1, bf16[256,2048]{1,0:T(8,128)(2,1)S(1)} %copy-done, ...), custom_call_target="tpu_custom_call" | custom-call | flops 3472883712 | bytes 9633792 | tf_op jit(solution)/shard_map/attend_0/pallas_call | solution.py:306
  88.6 0.0 collective-permute-done.5.refs_3_.refs_7_
  88.6 0.0 collective-permute-done.4.refs_2_.refs_6_
  88.6 0.0 collective-permute-done.3.refs_1_.refs_5_
  88.6 3.6 %attend_12.1 = bf16[256,2048]{1,0:T(8,128)(2,1)} custom-call(s32[2]{0:T(128)S(1)} %fusion.7.sel_ref, bf16[768,512]{1,0:T(8,128)(2,1)S(1)} %get-tuple-element.7.lat_ref, bf16[768,128]{1,0:T(8,128)(2,1)S(1)} %get-tuple-element.8.rot_ref, bf16[256,2048]{1,0:T(8,128)(2,1)S(1)} %copy-done.1, ...), custom_call_target="tpu_custom_call", output_to_operand_aliasing={{}: (13, {})} | custom-call | flops 1157627904 | bytes 3866624 | tf_op jit(solution)/shard_map/attend_12/pallas_call | solution.py:306
  (9 shorter events, 0.2 us)
Async XLA Ops:
  0.0 0.7 slice-start.3
  0.0 0.7 slice-start
  0.0 0.7 slice-start.1
  0.0 0.7 slice-start.2
  15.3 9.8 %copy-start.4 = (bf16[64,512]{1,0:T(8,128)(2,1)S(1)}, bf16[64,512]{1,0:T(8,128)(2,1)}, u32[]{:S(2)}) copy-start(bf16[64,512]{1,0:T(8,128)(2,1)} %param.9) | copy-start | bytes 196612
  15.3 9.8 %copy-start.5 = (bf16[64,64]{1,0:T(8,128)(2,1)S(1)}, bf16[64,64]{1,0:T(8,128)(2,1)}, u32[]{:S(2)}) copy-start(bf16[64,64]{1,0:T(8,128)(2,1)} %param.10) | copy-start | bytes 24580
  15.3 35.9 %all-to-all-start.1 = ((bf16[8,16,4096]{2,1,0:T(8,128)(2,1)}), bf16[8,16,4096]{2,1,0:T(8,128)(2,1)S(1)}, u32[]{:S(2)}, u32[]{:S(2)}) async-start(bf16[8,16,4096]{2,1,0:T(8,128)(2,1)} %broadcast_in_dim.47), calls=%async_computation.1 | async-start | bytes 2097152 | tf_op jit(solution)/shard_map/all_to_all | solution.py:42
  25.2 16.8 %collective-permute-start = (bf16[64,640]{1,0:T(8,128)(2,1)S(1)}, bf16[64,640]{1,0:T(8,128)(2,1)S(1)}, u32[]{:S(2)}, u32[]{:S(2)}) collective-permute-start(bf16[64,640]{1,0:T(8,128)(2,1)S(1)} %get-tuple-element.12), channel_id=1, source_target_pairs={{0,4},{4,8},{8,12},{12,16},{16,20},{20,24},{24,28},{28,32},{32,36}... | collective-permute-start | bytes 245768 | tf_op jit(solution)/shard_map/ppermute | solution.py:341
  27.3 14.7 %collective-permute-start.1 = (bf16[64,640]{1,0:T(8,128)(2,1)S(1)}, bf16[64,640]{1,0:T(8,128)(2,1)S(1)}, u32[]{:S(2)}, u32[]{:S(2)}) collective-permute-start(bf16[64,640]{1,0:T(8,128)(2,1)S(1)} %get-tuple-element.12), channel_id=1, source_target_pairs={{0,8},{4,12},{8,16},{12,20},{16,24},{20,28},{24,32},{28,36},{32,40... | collective-permute-start | bytes 245768 | tf_op jit(solution)/shard_map/ppermute | solution.py:341
  32.4 0.7 copy-start.6
  42.1 19.6 %collective-permute-start.2 = (bf16[3,64,640]{2,1,0:T(8,128)(2,1)S(1)}, bf16[3,64,640]{2,1,0:T(8,128)(2,1)S(1)}, u32[]{:S(2)}, u32[]{:S(2)}) collective-permute-start(bf16[3,64,640]{2,1,0:T(8,128)(2,1)S(1)} %pad_maximum_fusion.1), channel_id=1, source_target_pairs={{0,2},{2,0},{1,3},{3,1},{4,6},{6,4},{5,7},{7,5},{8,10},{10,8},{9,1... | collective-permute-start | bytes 737288 | tf_op jit(solution)/shard_map/ppermute | solution.py:360
  51.3 20.0 %collective-permute-start.8 = (bf16[128,3072]{1,0:T(8,128)(2,1)S(1)}, bf16[128,3072]{1,0:T(8,128)(2,1)S(1)}, u32[]{:S(2)}, u32[]{:S(2)}) collective-permute-start(bf16[128,3072]{1,0:T(8,128)(2,1)S(1)} %slice_add_fusion.refs_0_.refs_4_), channel_id=1, source_target_pairs={{64,0},{68,4},{72,8},{76,12},{80,16},{84,20},{88,24},{92,28},{96,3... | collective-permute-start | bytes 2359304 | tf_op jit(solution)/shard_map/ppermute | solution.py:78
  54.2 25.7 %collective-permute-start.7 = (bf16[128,3072]{1,0:T(8,128)(2,1)S(1)}, bf16[128,3072]{1,0:T(8,128)(2,1)S(1)}, u32[]{:S(2)}, u32[]{:S(2)}) collective-permute-start(bf16[128,3072]{1,0:T(8,128)(2,1)S(1)} %slice_add_fusion.refs_0_.refs_4_), channel_id=1, source_target_pairs={{48,0},{52,4},{56,8},{60,12},{0,16},{4,20},{8,24},{12,28},{16,32},... | collective-permute-start | bytes 2359304 | tf_op jit(solution)/shard_map/ppermute | solution.py:78
  57.8 22.1 %collective-permute-start.6 = (bf16[128,3072]{1,0:T(8,128)(2,1)S(1)}, bf16[128,3072]{1,0:T(8,128)(2,1)S(1)}, u32[]{:S(2)}, u32[]{:S(2)}) collective-permute-start(bf16[128,3072]{1,0:T(8,128)(2,1)S(1)} %slice_add_fusion.refs_0_.refs_4_), channel_id=1, source_target_pairs={{16,0},{20,4},{24,8},{28,12},{32,16},{36,20},{40,24},{44,28},{48,3... | collective-permute-start | bytes 2359304 | tf_op jit(solution)/shard_map/ppermute | solution.py:78
  61.9 2.7 %copy-start.2 = (f32[32,768]{1,0:T(8,128)S(1)}, f32[32,768]{1,0:T(8,128)}, u32[]{:S(2)}) copy-start(f32[32,768]{1,0:T(8,128)} %get-tuple-element.13.sin_ref) | copy-start | bytes 294916
  61.9 2.7 %copy-start.3 = (f32[32,768]{1,0:T(8,128)S(1)}, f32[32,768]{1,0:T(8,128)}, u32[]{:S(2)}) copy-start(f32[32,768]{1,0:T(8,128)} %get-tuple-element.14.cos_ref) | copy-start | bytes 294916
  61.9 18.0 %copy-start.1 = (bf16[256,2048]{1,0:T(8,128)(2,1)S(1)}, bf16[256,2048]{1,0:T(8,128)(2,1)}, u32[]{:S(2)}) copy-start(bf16[256,2048]{1,0:T(8,128)(2,1)} %qn_ref.3) | copy-start | bytes 3145732
  64.6 15.4 %copy-start = (bf16[256,2048]{1,0:T(8,128)(2,1)S(1)}, bf16[256,2048]{1,0:T(8,128)(2,1)}, u32[]{:S(2)}) copy-start(bf16[256,2048]{1,0:T(8,128)(2,1)} %rotate_queries.1.qr_ref) | copy-start | bytes 3145732
  65.3 23.3 %collective-permute-start.5 = (bf16[128,1024]{1,0:T(8,128)(2,1)S(1)}, bf16[128,1024]{1,0:T(8,128)(2,1)S(1)}, u32[]{:S(2)}, u32[]{:S(2)}) collective-permute-start(bf16[128,1024]{1,0:T(8,128)(2,1)S(1)} %slice_add_fusion.1.refs_0_.refs_4_), channel_id=1, source_target_pairs={{448,0},{452,4},{456,8},{460,12},{464,16},{468,20},{472,24},{476,2... | collective-permute-start | bytes 786440 | tf_op jit(solution)/shard_map/ppermute | solution.py:78
  69.2 19.4 %collective-permute-start.4 = (bf16[128,1024]{1,0:T(8,128)(2,1)S(1)}, bf16[128,1024]{1,0:T(8,128)(2,1)S(1)}, u32[]{:S(2)}, u32[]{:S(2)}) collective-permute-start(bf16[128,1024]{1,0:T(8,128)(2,1)S(1)} %slice_add_fusion.1.refs_0_.refs_4_), channel_id=1, source_target_pairs={{48,0},{52,4},{56,8},{60,12},{0,16},{4,20},{8,24},{12,28},{16,32},... | collective-permute-start | bytes 786440 | tf_op jit(solution)/shard_map/ppermute | solution.py:78
  71.4 17.2 %collective-permute-start.3 = (bf16[128,1024]{1,0:T(8,128)(2,1)S(1)}, bf16[128,1024]{1,0:T(8,128)(2,1)S(1)}, u32[]{:S(2)}, u32[]{:S(2)}) collective-permute-start(bf16[128,1024]{1,0:T(8,128)(2,1)S(1)} %slice_add_fusion.1.refs_0_.refs_4_), channel_id=1, source_target_pairs={{16,0},{20,4},{24,8},{28,12},{32,16},{36,20},{40,24},{44,28},{48,3... | collective-permute-start | bytes 786440 | tf_op jit(solution)/shard_map/ppermute | solution.py:78

commit v7 on v6

--- a/solution.py
+++ b/solution.py
@@ -274,7 +274,7 @@
 
 def attend(first, heads, sel, lat, rot, q_nope, q_rot, weights, earlier):
     tok_len, all_cols = q_nope.shape
-    width = 4
+    width = 6 if heads % 6 == 0 and first % 6 == 0 else 4
     cols = width * NOPE
     steps = heads // width
     count, depth = lat.shape

time: 92.8 us -> 92.4 us (level)
  transfers between devices with their start and end apart: 10 -> 10, of which waited for: 1 -> 1; matrix products, arithmetic and copies ran while one was open for 5% -> 5% of each run, Pallas kernels for 15% -> 14%
where the time goes in v7:
time: 92.4 us; the launch traced here: 91.8 us
  starting transfers between devices  47.6 us (52%)
  Pallas kernels  16.6 us (18%)
  blocking collectives  16 us (17%)
  local copies, waits for them, and re-layouts  4.44 us (5%)
  waiting for transfers between devices  3.57 us (4%)
  other arithmetic  2.64 us (3%)
  between operations  0.98 us (1%)
    ppermute x6, starting transfers between devices, from_neighbour(): return lax.ppermute(value, ('ctx', 'head'), pairs)  25.1 us
    all_to_all x1, blocking collectives, spread(): lax.all_to_all(jnp.broadcast_to(value[None], (size,) + value.shape), ('ct...  13.4 us
    pallas_call x2, Pallas kernels, attend(): pl.pallas_call(functools.partial(attend_kernel, width), grid=(steps,), in...  11.8 us
    all_to_all x1, starting transfers between devices, spread(): lax.all_to_all(jnp.broadcast_to(value[None], (size,) + value.shape), ('ct...  9.82 us
    ppermute x2, starting transfers between devices, local(): visited.append(lax.ppermute(own, 'ctx', pairs))  7.11 us
    ppermute x1, starting transfers between devices, local(): across = lax.ppermute(held, 'head', [(0, 2), (2, 0), (1, 3), (3, 1)])  5.56 us
    pallas_call x1, Pallas kernels, rotate_queries(): pl.pallas_call(rotate_queries_kernel, grid=(4,), in_specs=[pl.BlockSpec((...  4.15 us
    all_to_all x1, waiting for transfers between devices, spread(): lax.all_to_all(jnp.broadcast_to(value[None], (size,) + value.shape), ('ct...  3.55 us
  transfers between devices with their start and end apart: 10, of which 1 were waited for; matrix products, arithmetic and copies ran while one was open for 5% of the time, Pallas kernels for 14%

profile of v7, /device:TPU:8, one launch (start us, length us, event | category | flops | bytes accessed | tf_op | source)
XLA Modules:
  0.0 91.8 jit_solution(14472735071902489996)
XLA Ops:
  0.0 0.0 slice-start.3
  0.0 0.0 slice-start
  0.0 0.0 slice-start.1
  0.0 0.0 slice-start.2
  0.0 0.7 slice-done.3
  0.7 0.0 slice-done
  0.7 0.0 slice-done.1
  0.7 0.0 slice-done.2
  0.8 13.4 %all_to_all.10 = bf16[4,4,4096]{2,1,0:T(4,128)(2,1)S(1)} all-to-all(bf16[4,4,4096]{2,1,0:T(4,128)(2,1)S(1)} %broadcast_in_dim.29), channel_id=1, replica_groups={{0,4,8,12},{16,20,24,28},{32,36,40,44},{48,52,56,60},{64,68,72,76},{80,..., dimensions={0} | all-to-all | bytes 262144 | tf_op jit(solution)/shard_map/all_to_all | solution.py:42
  14.2 1.1 %broadcast_in_dim.47 = bf16[8,16,4096]{2,1,0:T(8,128)(2,1)} broadcast(bf16[16,4096]{1,0:T(8,128)(2,1)S(1)} %broadcast_in_dim.46), dimensions={1,2} | broadcast | bytes 1179648 | tf_op jit(solution)/shard_map/broadcast_in_dim | solution.py:43
  15.3 0.0 copy-start.4
  15.3 0.0 copy-start.5
  15.3 9.8 %all-to-all-start.1 = ((bf16[8,16,4096]{2,1,0:T(8,128)(2,1)}), bf16[8,16,4096]{2,1,0:T(8,128)(2,1)S(1)}, u32[]{:S(2)}, u32[]{:S(2)}) async-start(bf16[8,16,4096]{2,1,0:T(8,128)(2,1)} %broadcast_in_dim.47), calls=%async_computation.1 | async-start | bytes 2097152 | tf_op jit(solution)/shard_map/all_to_all | solution.py:42
  25.1 0.0 copy-done.4
  25.1 0.0 copy-done.5
  25.1 0.1 fusion.9
  25.2 2.1 %collective-permute-start = (bf16[64,640]{1,0:T(8,128)(2,1)S(1)}, bf16[64,640]{1,0:T(8,128)(2,1)S(1)}, u32[]{:S(2)}, u32[]{:S(2)}) collective-permute-start(bf16[64,640]{1,0:T(8,128)(2,1)S(1)} %get-tuple-element.12), channel_id=1, source_target_pairs={{0,4},{4,8},{8,12},{12,16},{16,20},{20,24},{24,28},{28,32},{32,36}... | collective-permute-start | bytes 245768 | tf_op jit(solution)/shard_map/ppermute | solution.py:341
  27.3 5.0 %collective-permute-start.1 = (bf16[64,640]{1,0:T(8,128)(2,1)S(1)}, bf16[64,640]{1,0:T(8,128)(2,1)S(1)}, u32[]{:S(2)}, u32[]{:S(2)}) collective-permute-start(bf16[64,640]{1,0:T(8,128)(2,1)S(1)} %get-tuple-element.12), channel_id=1, source_target_pairs={{0,8},{4,12},{8,16},{12,20},{16,24},{20,28},{24,32},{28,36},{32,40... | collective-permute-start | bytes 245768 | tf_op jit(solution)/shard_map/ppermute | solution.py:341
  32.4 0.0 copy-start.6
  32.5 0.1 iota_compare_fusion
  32.5 0.6 copy-done.6
  33.1 0.1 select_reduce_fusion
  33.3 0.6 slice.28
  33.9 0.1 copy.13
  34.0 0.1 add_convert_fusion
  34.1 1.1 %multiply_sine_fusion = (f32[32,768]{1,0:T(8,128)}, f32[32,768]{1,0:T(8,128)}) fusion(f32[32]{0:T(128)S(1)} %multiply_power_fusion, f32[768]{0:T(1024)S(1)} %convert_element_type.18), kind=kLoop, calls=%fused_computation.6 | loop fusion | flops 24576 | bytes 199808 | tf_op jit(solution)/shard_map/sin | solution.py:356
  35.2 4.2 %rotate_queries.1.qr_ref = bf16[256,2048]{1,0:T(8,128)(2,1)} custom-call(bf16[256,1024]{1,0:T(8,128)(2,1)} %x_ref.1, f32[32,768]{1,0:T(8,128)} %get-tuple-element.14.cos_ref, f32[32,768]{1,0:T(8,128)} %get-tuple-element.13.sin_ref), custom_call_target="tpu_custom_call" | custom-call | flops 1048576 | bytes 1572864 | tf_op jit(solution)/shard_map/rotate_queries/pallas_call | solution.py:135
  39.4 1.2 %slice.37 = bf16[1,1]{1,0:T(2,128)(2,1)} slice(bf16[256,2048]{1,0:T(8,128)(2,1)} %rotate_queries.1.qr_ref), slice={[0:1], [0:1]} | slice | bytes 4 | tf_op jit(solution)/shard_map/slice | solution.py:362
  41.2 0.8 fusion.7.sel_ref
  42.0 0.1 fusion.1.order_ref
  42.1 0.0 collective-permute-done
  42.1 0.0 collective-permute-done.1
  42.1 5.6 %collective-permute-start.2 = (bf16[3,64,640]{2,1,0:T(8,128)(2,1)S(1)}, bf16[3,64,640]{2,1,0:T(8,128)(2,1)S(1)}, u32[]{:S(2)}, u32[]{:S(2)}) collective-permute-start(bf16[3,64,640]{2,1,0:T(8,128)(2,1)S(1)} %pad_maximum_fusion.1), channel_id=1, source_target_pairs={{0,2},{2,0},{1,3},{3,1},{4,6},{6,4},{5,7},{7,5},{8,10},{10,8},{9,1... | collective-permute-start | bytes 737288 | tf_op jit(solution)/shard_map/ppermute | solution.py:360
  47.7 3.5 %all-to-all-done.1 = bf16[8,16,4096]{2,1,0:T(8,128)(2,1)S(1)} async-done(((bf16[8,16,4096]{2,1,0:T(8,128)(2,1)}), bf16[8,16,4096]{2,1,0:T(8,128)(2,1)S(1)}, u32[]{:S(2)}, u32[]{:S(2)}) %all-to-all-start.1) | async-done | bytes 1048608 | tf_op jit(solution)/shard_map/all_to_all | solution.py:42
  51.2 0.1 slice_add_fusion.refs_0_.refs_4_
  51.3 2.9 %collective-permute-start.8 = (bf16[128,3072]{1,0:T(8,128)(2,1)S(1)}, bf16[128,3072]{1,0:T(8,128)(2,1)S(1)}, u32[]{:S(2)}, u32[]{:S(2)}) collective-permute-start(bf16[128,3072]{1,0:T(8,128)(2,1)S(1)} %slice_add_fusion.refs_0_.refs_4_), channel_id=1, source_target_pairs={{64,0},{68,4},{72,8},{76,12},{80,16},{84,20},{88,24},{92,28},{96,3... | collective-permute-start | bytes 2359304 | tf_op jit(solution)/shard_map/ppermute | solution.py:78
  54.2 3.6 %collective-permute-start.7 = (bf16[128,3072]{1,0:T(8,128)(2,1)S(1)}, bf16[128,3072]{1,0:T(8,128)(2,1)S(1)}, u32[]{:S(2)}, u32[]{:S(2)}) collective-permute-start(bf16[128,3072]{1,0:T(8,128)(2,1)S(1)} %slice_add_fusion.refs_0_.refs_4_), channel_id=1, source_target_pairs={{48,0},{52,4},{56,8},{60,12},{0,16},{4,20},{8,24},{12,28},{16,32},... | collective-permute-start | bytes 2359304 | tf_op jit(solution)/shard_map/ppermute | solution.py:78
  57.8 3.9 %collective-permute-start.6 = (bf16[128,3072]{1,0:T(8,128)(2,1)S(1)}, bf16[128,3072]{1,0:T(8,128)(2,1)S(1)}, u32[]{:S(2)}, u32[]{:S(2)}) collective-permute-start(bf16[128,3072]{1,0:T(8,128)(2,1)S(1)} %slice_add_fusion.refs_0_.refs_4_), channel_id=1, source_target_pairs={{16,0},{20,4},{24,8},{28,12},{32,16},{36,20},{40,24},{44,28},{48,3... | collective-permute-start | bytes 2359304 | tf_op jit(solution)/shard_map/ppermute | solution.py:78
  61.8 0.0 collective-permute-done.2
  61.8 0.1 select_bitcast_fusion.1
  61.8 0.1 pad_maximum_fusion
  61.9 0.0 copy-start.2
  61.9 0.0 copy-start.3
  61.9 0.0 copy-start.1
  61.9 2.6 %all-gather = bf16[4,3,64,640]{3,2,1,0:T(8,128)(2,1)S(1)} all-gather(bf16[2,3,64,640]{3,2,1,0:T(8,128)(2,1)S(1)} %pad_maximum_fusion), channel_id=2, replica_groups={{0,1},{2,3},{4,5},{6,7},{8,9},{10,11},{12,13},{14,15},{16,17},{18,19},{..., dimensions={0}, use_global_device_ids=true | all-gather | bytes 1474560 | tf_op jit(solution)/shard_map/all_gather | solution.py:368
  64.6 0.0 copy-start
  64.6 0.0 copy-done.2
  64.6 0.0 copy-done.3
  64.6 0.6 prepare_keys.1
  65.3 3.9 %collective-permute-start.5 = (bf16[128,1024]{1,0:T(8,128)(2,1)S(1)}, bf16[128,1024]{1,0:T(8,128)(2,1)S(1)}, u32[]{:S(2)}, u32[]{:S(2)}) collective-permute-start(bf16[128,1024]{1,0:T(8,128)(2,1)S(1)} %slice_add_fusion.1.refs_0_.refs_4_), channel_id=1, source_target_pairs={{448,0},{452,4},{456,8},{460,12},{464,16},{468,20},{472,24},{476,2... | collective-permute-start | bytes 786440 | tf_op jit(solution)/shard_map/ppermute | solution.py:78
  69.2 2.2 %collective-permute-start.4 = (bf16[128,1024]{1,0:T(8,128)(2,1)S(1)}, bf16[128,1024]{1,0:T(8,128)(2,1)S(1)}, u32[]{:S(2)}, u32[]{:S(2)}) collective-permute-start(bf16[128,1024]{1,0:T(8,128)(2,1)S(1)} %slice_add_fusion.1.refs_0_.refs_4_), channel_id=1, source_target_pairs={{48,0},{52,4},{56,8},{60,12},{0,16},{4,20},{8,24},{12,28},{16,32},... | collective-permute-start | bytes 786440 | tf_op jit(solution)/shard_map/ppermute | solution.py:78
  71.3 0.0 collective-permute-done.8.refs_3_.refs_7_
  71.4 8.6 %collective-permute-start.3 = (bf16[128,1024]{1,0:T(8,128)(2,1)S(1)}, bf16[128,1024]{1,0:T(8,128)(2,1)S(1)}, u32[]{:S(2)}, u32[]{:S(2)}) collective-permute-start(bf16[128,1024]{1,0:T(8,128)(2,1)S(1)} %slice_add_fusion.1.refs_0_.refs_4_), channel_id=1, source_target_pairs={{16,0},{20,4},{24,8},{28,12},{32,16},{36,20},{40,24},{44,28},{48,3... | collective-permute-start | bytes 786440 | tf_op jit(solution)/shard_map/ppermute | solution.py:78
  79.9 0.0 collective-permute-done.7.refs_2_.refs_6_
  79.9 0.0 collective-permute-done.6.refs_1_.refs_5_
  80.0 0.0 copy-done.1
  80.0 0.0 copy-done
  80.0 8.3 %attend_0.1.refs_8_ = bf16[256,2048]{1,0:T(8,128)(2,1)} custom-call(s32[2]{0:T(128)S(1)} %fusion.7.sel_ref, bf16[768,512]{1,0:T(8,128)(2,1)S(1)} %get-tuple-element.7.lat_ref, bf16[768,128]{1,0:T(8,128)(2,1)S(1)} %get-tuple-element.8.rot_ref, bf16[256,2048]{1,0:T(8,128)(2,1)S(1)} %copy-done.1, bf16[256,2048]{1,0:T(8,128)(2,1)S(1)} %copy-done, ...), custom_call_target="tpu_custom_call" | custom-call | flops 3472883712 | bytes 9633792 | tf_op jit(solution)/shard_map/attend_0/pallas_call | solution.py:306
  88.2 0.0 collective-permute-done.5.refs_3_.refs_7_
  88.2 0.0 collective-permute-done.4.refs_2_.refs_6_
  88.2 0.0 collective-permute-done.3.refs_1_.refs_5_
  88.2 3.6 %attend_12.1 = bf16[256,2048]{1,0:T(8,128)(2,1)} custom-call(s32[2]{0:T(128)S(1)} %fusion.7.sel_ref, bf16[768,512]{1,0:T(8,128)(2,1)S(1)} %get-tuple-element.7.lat_ref, bf16[768,128]{1,0:T(8,128)(2,1)S(1)} %get-tuple-element.8.rot_ref, bf16[256,2048]{1,0:T(8,128)(2,1)S(1)} %copy-done.1, ...), custom_call_target="tpu_custom_call", output_to_operand_aliasing={{}: (13, {})} | custom-call | flops 1157627904 | bytes 3866624 | tf_op jit(solution)/shard_map/attend_12/pallas_call | solution.py:306
  (9 shorter events, 0.2 us)
Async XLA Ops:
  0.0 0.7 slice-start.3
  0.0 0.7 slice-start
  0.0 0.7 slice-start.1
  0.0 0.7 slice-start.2
  15.3 9.8 %copy-start.4 = (bf16[64,512]{1,0:T(8,128)(2,1)S(1)}, bf16[64,512]{1,0:T(8,128)(2,1)}, u32[]{:S(2)}) copy-start(bf16[64,512]{1,0:T(8,128)(2,1)} %param.9) | copy-start | bytes 196612
  15.3 9.8 %copy-start.5 = (bf16[64,64]{1,0:T(8,128)(2,1)S(1)}, bf16[64,64]{1,0:T(8,128)(2,1)}, u32[]{:S(2)}) copy-start(bf16[64,64]{1,0:T(8,128)(2,1)} %param.10) | copy-start | bytes 24580
  15.3 35.9 %all-to-all-start.1 = ((bf16[8,16,4096]{2,1,0:T(8,128)(2,1)}), bf16[8,16,4096]{2,1,0:T(8,128)(2,1)S(1)}, u32[]{:S(2)}, u32[]{:S(2)}) async-start(bf16[8,16,4096]{2,1,0:T(8,128)(2,1)} %broadcast_in_dim.47), calls=%async_computation.1 | async-start | bytes 2097152 | tf_op jit(solution)/shard_map/all_to_all | solution.py:42
  25.2 16.8 %collective-permute-start = (bf16[64,640]{1,0:T(8,128)(2,1)S(1)}, bf16[64,640]{1,0:T(8,128)(2,1)S(1)}, u32[]{:S(2)}, u32[]{:S(2)}) collective-permute-start(bf16[64,640]{1,0:T(8,128)(2,1)S(1)} %get-tuple-element.12), channel_id=1, source_target_pairs={{0,4},{4,8},{8,12},{12,16},{16,20},{20,24},{24,28},{28,32},{32,36}... | collective-permute-start | bytes 245768 | tf_op jit(solution)/shard_map/ppermute | solution.py:341
  27.3 14.7 %collective-permute-start.1 = (bf16[64,640]{1,0:T(8,128)(2,1)S(1)}, bf16[64,640]{1,0:T(8,128)(2,1)S(1)}, u32[]{:S(2)}, u32[]{:S(2)}) collective-permute-start(bf16[64,640]{1,0:T(8,128)(2,1)S(1)} %get-tuple-element.12), channel_id=1, source_target_pairs={{0,8},{4,12},{8,16},{12,20},{16,24},{20,28},{24,32},{28,36},{32,40... | collective-permute-start | bytes 245768 | tf_op jit(solution)/shard_map/ppermute | solution.py:341
  32.4 0.7 copy-start.6
  42.1 19.6 %collective-permute-start.2 = (bf16[3,64,640]{2,1,0:T(8,128)(2,1)S(1)}, bf16[3,64,640]{2,1,0:T(8,128)(2,1)S(1)}, u32[]{:S(2)}, u32[]{:S(2)}) collective-permute-start(bf16[3,64,640]{2,1,0:T(8,128)(2,1)S(1)} %pad_maximum_fusion.1), channel_id=1, source_target_pairs={{0,2},{2,0},{1,3},{3,1},{4,6},{6,4},{5,7},{7,5},{8,10},{10,8},{9,1... | collective-permute-start | bytes 737288 | tf_op jit(solution)/shard_map/ppermute | solution.py:360
  51.3 20.0 %collective-permute-start.8 = (bf16[128,3072]{1,0:T(8,128)(2,1)S(1)}, bf16[128,3072]{1,0:T(8,128)(2,1)S(1)}, u32[]{:S(2)}, u32[]{:S(2)}) collective-permute-start(bf16[128,3072]{1,0:T(8,128)(2,1)S(1)} %slice_add_fusion.refs_0_.refs_4_), channel_id=1, source_target_pairs={{64,0},{68,4},{72,8},{76,12},{80,16},{84,20},{88,24},{92,28},{96,3... | collective-permute-start | bytes 2359304 | tf_op jit(solution)/shard_map/ppermute | solution.py:78
  54.2 25.7 %collective-permute-start.7 = (bf16[128,3072]{1,0:T(8,128)(2,1)S(1)}, bf16[128,3072]{1,0:T(8,128)(2,1)S(1)}, u32[]{:S(2)}, u32[]{:S(2)}) collective-permute-start(bf16[128,3072]{1,0:T(8,128)(2,1)S(1)} %slice_add_fusion.refs_0_.refs_4_), channel_id=1, source_target_pairs={{48,0},{52,4},{56,8},{60,12},{0,16},{4,20},{8,24},{12,28},{16,32},... | collective-permute-start | bytes 2359304 | tf_op jit(solution)/shard_map/ppermute | solution.py:78
  57.8 22.1 %collective-permute-start.6 = (bf16[128,3072]{1,0:T(8,128)(2,1)S(1)}, bf16[128,3072]{1,0:T(8,128)(2,1)S(1)}, u32[]{:S(2)}, u32[]{:S(2)}) collective-permute-start(bf16[128,3072]{1,0:T(8,128)(2,1)S(1)} %slice_add_fusion.refs_0_.refs_4_), channel_id=1, source_target_pairs={{16,0},{20,4},{24,8},{28,12},{32,16},{36,20},{40,24},{44,28},{48,3... | collective-permute-start | bytes 2359304 | tf_op jit(solution)/shard_map/ppermute | solution.py:78
  61.9 2.7 %copy-start.2 = (f32[32,768]{1,0:T(8,128)S(1)}, f32[32,768]{1,0:T(8,128)}, u32[]{:S(2)}) copy-start(f32[32,768]{1,0:T(8,128)} %get-tuple-element.13.sin_ref) | copy-start | bytes 294916
  61.9 2.7 %copy-start.3 = (f32[32,768]{1,0:T(8,128)S(1)}, f32[32,768]{1,0:T(8,128)}, u32[]{:S(2)}) copy-start(f32[32,768]{1,0:T(8,128)} %get-tuple-element.14.cos_ref) | copy-start | bytes 294916
  61.9 18.0 %copy-start.1 = (bf16[256,2048]{1,0:T(8,128)(2,1)S(1)}, bf16[256,2048]{1,0:T(8,128)(2,1)}, u32[]{:S(2)}) copy-start(bf16[256,2048]{1,0:T(8,128)(2,1)} %qn_ref.3) | copy-start | bytes 3145732
  64.6 15.4 %copy-start = (bf16[256,2048]{1,0:T(8,128)(2,1)S(1)}, bf16[256,2048]{1,0:T(8,128)(2,1)}, u32[]{:S(2)}) copy-start(bf16[256,2048]{1,0:T(8,128)(2,1)} %rotate_queries.1.qr_ref) | copy-start | bytes 3145732
  65.3 23.0 %collective-permute-start.5 = (bf16[128,1024]{1,0:T(8,128)(2,1)S(1)}, bf16[128,1024]{1,0:T(8,128)(2,1)S(1)}, u32[]{:S(2)}, u32[]{:S(2)}) collective-permute-start(bf16[128,1024]{1,0:T(8,128)(2,1)S(1)} %slice_add_fusion.1.refs_0_.refs_4_), channel_id=1, source_target_pairs={{448,0},{452,4},{456,8},{460,12},{464,16},{468,20},{472,24},{476,2... | collective-permute-start | bytes 786440 | tf_op jit(solution)/shard_map/ppermute | solution.py:78
  69.2 19.1 %collective-permute-start.4 = (bf16[128,1024]{1,0:T(8,128)(2,1)S(1)}, bf16[128,1024]{1,0:T(8,128)(2,1)S(1)}, u32[]{:S(2)}, u32[]{:S(2)}) collective-permute-start(bf16[128,1024]{1,0:T(8,128)(2,1)S(1)} %slice_add_fusion.1.refs_0_.refs_4_), channel_id=1, source_target_pairs={{48,0},{52,4},{56,8},{60,12},{0,16},{4,20},{8,24},{12,28},{16,32},... | collective-permute-start | bytes 786440 | tf_op jit(solution)/shard_map/ppermute | solution.py:78
  71.4 16.9 %collective-permute-start.3 = (bf16[128,1024]{1,0:T(8,128)(2,1)S(1)}, bf16[128,1024]{1,0:T(8,128)(2,1)S(1)}, u32[]{:S(2)}, u32[]{:S(2)}) collective-permute-start(bf16[128,1024]{1,0:T(8,128)(2,1)S(1)} %slice_add_fusion.1.refs_0_.refs_4_), channel_id=1, source_target_pairs={{16,0},{20,4},{24,8},{28,12},{32,16},{36,20},{40,24},{44,28},{48,3... | collective-permute-start | bytes 786440 | tf_op jit(solution)/shard_map/ppermute | solution.py:78
